TPU v7x, 512 devices: a whole 4x4x16 slice. The times are simulated.
512 devices in a mesh: dp: 8 (over z_lo), chan: 4 (over z_hi, core), seq: 16 (over y, x).
Axes of the slice: x: 4, y: 4, z: 16 (z_hi: 2, z_lo: 8; z = z_hi * 8 + z_lo), core: 2. Of those that a mesh axis runs over, the one named last changes fastest.
Arguments:
- query_in: bfloat16 [8, 2048, 4096], P('dp', 'seq', 'chan'), may hold values from -6 to 6
- key_in: bfloat16 [8, 2048, 4096], P('dp', 'seq', 'chan'), may hold values from -6 to 6
- value_in: bfloat16 [8, 2048, 4096], P('dp', 'seq', 'chan'), may hold values from -6 to 6
- filter_taps: bfloat16 [2048, 4096], P('seq', 'chan'), may hold values from -1 to 1
- skip_gain: float32 [4096], P('chan'), may hold values from -4 to 4
- grad_out: bfloat16 [8, 2048, 4096], P('dp', 'seq', 'chan'), may hold values from -6 to 6
Outputs:
- mixed_out: bfloat16 [8, 2048, 4096], P('dp', 'seq', 'chan')
- grad_query: bfloat16 [8, 2048, 4096], P('dp', 'seq', 'chan')
- grad_key: bfloat16 [8, 2048, 4096], P('dp', 'seq', 'chan')
- grad_value: bfloat16 [8, 2048, 4096], P('dp', 'seq', 'chan')
- grad_filter: bfloat16 [2048, 4096], P('seq', 'chan')
All inputs are finite; a program needn't handle non-finite values.
Results may differ from a plain program's by a relative error of at most 0.017.
Values may be sent and summed in bfloat16 or wider, within the bound.
No kernel may reach another device: no remote copies, remote signals or barrier semaphores. Data moves between devices by JAX's collectives and lax.ppermute only.
A program may use at most 64 MiB of HBM per device.

v0:
```python
import math

import jax
import jax.numpy as jnp
from jax import lax
from jax.sharding import PartitionSpec as P

TRANSFORM_PRECISION = lax.Precision.HIGH


def rounded(values):
    return lax.optimization_barrier(values).astype(jnp.float32)


def dft_tables(block_rows, block_cols):
    outer_count = 2 * block_rows
    padded_len = outer_count * block_cols
    two_pi = 2.0 * math.pi
    row_pos = jnp.arange(block_rows, dtype=jnp.int32)
    row_freq = jnp.arange(outer_count, dtype=jnp.int32)
    col_idx = jnp.arange(block_cols, dtype=jnp.int32)
    outer_angle = (
        two_pi
        / outer_count
        * (row_pos[:, None] * row_freq[None, :] % outer_count).astype(jnp.float32)
    )
    inner_angle = (
        two_pi / block_cols * (col_idx[:, None] * col_idx[None, :] % block_cols).astype(jnp.float32)
    )
    twist_angle = (
        two_pi
        / padded_len
        * (row_freq[:, None] * col_idx[None, :] % padded_len).astype(jnp.float32)
    )
    return (
        jnp.cos(outer_angle),
        jnp.sin(outer_angle),
        jnp.cos(inner_angle),
        jnp.sin(inner_angle),
        jnp.cos(twist_angle),
        jnp.sin(twist_angle),
    )


def to_spectrum(signal, tables):
    outer_cos, outer_sin, inner_cos, inner_sin, twist_cos, twist_sin = tables
    blocked = signal.reshape(signal.shape[0], outer_cos.shape[0], inner_cos.shape[0])
    part_real = jnp.einsum("crs,rk->cks", blocked, outer_cos, precision=TRANSFORM_PRECISION)
    part_imag = -jnp.einsum("crs,rk->cks", blocked, outer_sin, precision=TRANSFORM_PRECISION)
    turned_real = part_real * twist_cos + part_imag * twist_sin
    turned_imag = part_imag * twist_cos - part_real * twist_sin
    spec_real = jnp.einsum(
        "cks,sm->ckm", turned_real, inner_cos, precision=TRANSFORM_PRECISION
    ) + jnp.einsum("cks,sm->ckm", turned_imag, inner_sin, precision=TRANSFORM_PRECISION)
    spec_imag = jnp.einsum(
        "cks,sm->ckm", turned_imag, inner_cos, precision=TRANSFORM_PRECISION
    ) - jnp.einsum("cks,sm->ckm", turned_real, inner_sin, precision=TRANSFORM_PRECISION)
    return (spec_real, spec_imag)


def to_signal(spec_real, spec_imag, tables):
    outer_cos, outer_sin, inner_cos, inner_sin, twist_cos, twist_sin = tables
    back_real = jnp.einsum(
        "ckm,sm->cks", spec_real, inner_cos, precision=TRANSFORM_PRECISION
    ) - jnp.einsum("ckm,sm->cks", spec_imag, inner_sin, precision=TRANSFORM_PRECISION)
    back_imag = jnp.einsum(
        "ckm,sm->cks", spec_imag, inner_cos, precision=TRANSFORM_PRECISION
    ) + jnp.einsum("ckm,sm->cks", spec_real, inner_sin, precision=TRANSFORM_PRECISION)
    turned_real = back_real * twist_cos - back_imag * twist_sin
    turned_imag = back_imag * twist_cos + back_real * twist_sin
    blocked = jnp.einsum(
        "cks,rk->crs", turned_real, outer_cos, precision=TRANSFORM_PRECISION
    ) - jnp.einsum("cks,rk->crs", turned_imag, outer_sin, precision=TRANSFORM_PRECISION)
    padded_len = twist_cos.shape[0] * twist_cos.shape[1]
    return blocked.reshape(blocked.shape[0], -1) / padded_len


def convolve(first_spec, second_spec):
    real_part = first_spec[0] * second_spec[0] - first_spec[1] * second_spec[1]
    imag_part = first_spec[0] * second_spec[1] + first_spec[1] * second_spec[0]
    return (real_part, imag_part)


def correlate(first_spec, second_spec):
    real_part = first_spec[0] * second_spec[0] + first_spec[1] * second_spec[1]
    imag_part = first_spec[0] * second_spec[1] - first_spec[1] * second_spec[0]
    return (real_part, imag_part)


def forward_channels(mixed_cols, taps_cols, skip_own, tables):
    mixed_float = mixed_cols.astype(jnp.float32)
    mixed_spec = to_spectrum(mixed_float, tables)
    taps_spec = to_spectrum(taps_cols.astype(jnp.float32), tables)
    product = convolve(taps_spec, mixed_spec)
    convolved = to_signal(product[0], product[1], tables)
    state_cols = lax.optimization_barrier((convolved + skip_own * mixed_float).astype(jnp.bfloat16))
    return (mixed_spec, taps_spec, state_cols)


def channel_grads(grad_cols, mixed_spec, taps_spec, skip_own, tables, factor):
    grad_float = grad_cols.astype(jnp.float32)
    grad_spec = to_spectrum(grad_float, tables)
    back_mixed = correlate(taps_spec, grad_spec)
    dmixed_cols = (to_signal(back_mixed[0], back_mixed[1], tables) + skip_own * grad_float).astype(
        jnp.bfloat16
    )
    back_taps = correlate(mixed_spec, grad_spec)
    dtaps_cols = (factor * to_signal(back_taps[0], back_taps[1], tables)).astype(jnp.bfloat16)
    return (dmixed_cols, dtaps_cols)


def on_device(query_in, key_in, value_in, filter_taps, skip_gain, grad_out):
    seq_count = lax.axis_size("seq")
    seq_rank = lax.axis_index("seq")
    rows_dev = query_in.shape[1]
    chan_dev = query_in.shape[2]
    owned_chans = chan_dev // seq_count
    seq_total = rows_dev * seq_count
    tables = dft_tables(seq_total // 128, 128)
    factor = 1.0 / math.sqrt(query_in.shape[0] * lax.axis_size("dp") * seq_total)
    skip_own = lax.dynamic_slice_in_dim(skip_gain, seq_rank * owned_chans, owned_chans)[:, None]
    query_rows = query_in[0]
    key_rows = key_in[0]
    value_rows = value_in[0]
    grad_rows = grad_out[0]
    key_float = key_rows.astype(jnp.float32)
    value_float = value_rows.astype(jnp.float32)
    mixed_rows = (key_float * value_float).astype(jnp.bfloat16)
    mixed_cols, taps_cols = (
        lax.all_to_all(mixed_rows.T, "seq", split_axis=0, concat_axis=1, tiled=True),
        lax.all_to_all(filter_taps.T, "seq", split_axis=0, concat_axis=1, tiled=True),
    )
    mixed_spec, taps_spec, state_cols = forward_channels(mixed_cols, taps_cols, skip_own, tables)
    state_rows = lax.all_to_all(
        state_cols, "seq", split_axis=1, concat_axis=0, tiled=True
    ).T.astype(jnp.float32)
    query_float = query_rows.astype(jnp.float32)
    grad_float = grad_rows.astype(jnp.float32)
    mixed_out = (query_float * state_rows).astype(jnp.bfloat16)
    grad_query = (grad_float * state_rows).astype(jnp.bfloat16)
    grad_state = (grad_float * query_float).astype(jnp.bfloat16)
    grad_cols = lax.all_to_all(grad_state.T, "seq", split_axis=0, concat_axis=1, tiled=True)
    dmixed_cols, dtaps_cols = channel_grads(
        grad_cols, mixed_spec, taps_spec, skip_own, tables, factor
    )
    dmixed_back, dtaps_back = (
        lax.all_to_all(dmixed_cols, "seq", split_axis=1, concat_axis=0, tiled=True),
        lax.all_to_all(dtaps_cols, "seq", split_axis=1, concat_axis=0, tiled=True),
    )
    grad_filter = lax.psum(rounded(dtaps_back).astype(jnp.bfloat16), "dp").T
    dmixed_float = dmixed_back.T.astype(jnp.float32)
    grad_key = (dmixed_float * value_float).astype(jnp.bfloat16)
    grad_value = (dmixed_float * key_float).astype(jnp.bfloat16)
    return (mixed_out[None], grad_query[None], grad_key[None], grad_value[None], grad_filter)


def solution(mesh):
    in_specs = (
        P("dp", "seq", "chan"),
        P("dp", "seq", "chan"),
        P("dp", "seq", "chan"),
        P("seq", "chan"),
        P("chan"),
        P("dp", "seq", "chan"),
    )
    out_specs = (
        P("dp", "seq", "chan"),
        P("dp", "seq", "chan"),
        P("dp", "seq", "chan"),
        P("dp", "seq", "chan"),
        P("seq", "chan"),
    )
    return jax.shard_map(
        on_device, mesh=mesh, in_specs=in_specs, out_specs=out_specs, check_vma=False
    )
```

profile of v0, /device:TPU:2, one launch (start us, length us, event | category | flops | bytes accessed | tf_op | source)
XLA Modules:
  0.0 228.3 jit_solution(16865464266880982269)
XLA Ops:
  7.2 1.2 copy.43
  9.8 9.4 %all-to-all-start.3 = ((bf16[16,64,128]{2,1,0:T(8,128)(2,1)}), bf16[16,64,128]{2,1,0:T(8,128)(2,1)S(1)}, u32[]{:S(2)}, u32[]{:S(2)}) async-start(bf16[16,64,128]{2,1,0:T(8,128)(2,1)} %bitcast.29), calls=%async_computation.3 | async-start | bytes 524288 | tf_op jit(solution)/shard_map/all_to_all | solution.py:142
  20.4 0.9 copy-done.22
  23.7 2.9 %all-to-all-done.3 = bf16[16,64,128]{2,1,0:T(8,128)(2,1)S(1)} async-done(((bf16[16,64,128]{2,1,0:T(8,128)(2,1)}), bf16[16,64,128]{2,1,0:T(8,128)(2,1)S(1)}, u32[]{:S(2)}, u32[]{:S(2)}) %all-to-all-start.3) | async-done | bytes 262176 | tf_op jit(solution)/shard_map/all_to_all | solution.py:142
  26.6 4.8 %all-to-all-start = ((bf16[16,64,128]{2,1,0:T(8,128)(2,1)}), bf16[16,64,128]{2,1,0:T(8,128)(2,1)S(1)}, u32[]{:S(2)}, u32[]{:S(2)}) async-start(bf16[16,64,128]{2,1,0:T(8,128)(2,1)} %bitcast.3), calls=%async_computation | async-start | bytes 524288 | tf_op jit(solution)/shard_map/all_to_all | solution.py:131
  32.5 1.8 fusion.12
  34.3 1.8 fusion.8
  36.2 2.7 %all-to-all-done = bf16[16,64,128]{2,1,0:T(8,128)(2,1)S(1)} async-done(((bf16[16,64,128]{2,1,0:T(8,128)(2,1)}), bf16[16,64,128]{2,1,0:T(8,128)(2,1)S(1)}, u32[]{:S(2)}, u32[]{:S(2)}) %all-to-all-start) | async-done | bytes 262176 | tf_op jit(solution)/shard_map/all_to_all | solution.py:131
  39.5 4.8 %all-to-all-start.1 = ((bf16[16,64,128]{2,1,0:T(8,128)(2,1)}), bf16[16,64,128]{2,1,0:T(8,128)(2,1)S(1)}, u32[]{:S(2)}, u32[]{:S(2)}) async-start(bf16[16,64,128]{2,1,0:T(8,128)(2,1)} %bitcast.13), calls=%async_computation.1 | async-start | bytes 524288 | tf_op jit(solution)/shard_map/all_to_all | solution.py:130
  44.3 1.6 convolution_negate_fusion.2
  46.4 1.9 fusion.24
  48.3 1.8 fusion.20
  50.1 1.6 all-to-all-done.1
  52.8 0.8 fusion.18
  54.9 0.9 convolution_add_fusion.2
  55.8 0.9 convolution_add_fusion.4
  57.0 0.9 convolution_subtract_fusion.2
  58.5 0.9 convolution_add_fusion.5
  59.8 0.9 convolution_subtract_fusion.5
  60.7 2.4 %multiply_add_fusion = (f32[64,32,128]{2,1,0:T(8,128)S(1)}, f32[64,32,128]{2,1,0:T(8,128)S(1)}, f32[64,32,128]{2,1,0:T(8,128)}, f32[64,32,128]{2,1,0:T(8,128)S(1...) fusion(f32[64,32,128]{2,1,0:T(8,128)S(1)} %convolution_subtract_fusion.2, ...), kind=kOutput, calls=%fused_computation.52 | convolution fusion | flops 207323136 | bytes 14712832 | tf_op jit(solution)/shard_map/cks,sm->ckm/dot_general | solution.py:57
  63.9 1.0 fusion.97
  68.4 5.7 %all-to-all-start.5 = ((bf16[64,16,128]{2,0,1:T(8,128)(2,1)}), bf16[64,16,128]{2,0,1:T(8,128)(2,1)}, u32[]{:S(2)}, u32[]{:S(2)}) async-start(bf16[64,16,128]{2,0,1:T(8,128)(2,1)} %copy.53), calls=%async_computation.5 | async-start | bytes 524288 | tf_op jit(solution)/shard_map/all_to_all | solution.py:148
  84.7 7.2 %all-to-all-start.4 = ((bf16[64,16,128]{2,0,1:T(8,128)(2,1)}), bf16[64,16,128]{2,0,1:T(8,128)(2,1)S(1)}, u32[]{:S(2)}, u32[]{:S(2)}) async-start(bf16[64,16,128]{2,0,1:T(8,128)(2,1)} %copy.52), calls=%async_computation.4 | async-start | bytes 524288 | tf_op jit(solution)/shard_map/all_to_all | solution.py:147
  93.2 6.1 %all-to-all-done.4 = bf16[64,16,128]{2,0,1:T(8,128)(2,1)S(1)} async-done(((bf16[64,16,128]{2,0,1:T(8,128)(2,1)}), bf16[64,16,128]{2,0,1:T(8,128)(2,1)S(1)}, u32[]{:S(2)}, u32[]{:S(2)}) %all-to-all-start.4) | async-done | bytes 262176 | tf_op jit(solution)/shard_map/all_to_all | solution.py:147
  99.2 4.8 %all-to-all-start.2 = ((bf16[64,16,128]{2,0,1:T(8,128)(2,1)}), bf16[64,16,128]{2,0,1:T(8,128)(2,1)S(1)}, u32[]{:S(2)}, u32[]{:S(2)}) async-start(bf16[64,16,128]{2,0,1:T(8,128)(2,1)} %copy_bitcast_fusion), calls=%async_computation.2 | async-start | bytes 524288 | tf_op jit(solution)/shard_map/all_to_all | solution.py:134
  104.2 0.9 copy.56
  105.0 0.8 copy.57
  105.9 5.6 %all-to-all-done.2 = bf16[64,16,128]{2,0,1:T(8,128)(2,1)S(1)} async-done(((bf16[64,16,128]{2,0,1:T(8,128)(2,1)}), bf16[64,16,128]{2,0,1:T(8,128)(2,1)S(1)}, u32[]{:S(2)}, u32[]{:S(2)}) %all-to-all-start.2) | async-done | bytes 262176 | tf_op jit(solution)/shard_map/all_to_all | solution.py:134
  111.6 0.9 copy.54
  112.4 0.8 copy.55
  113.3 106.4 %all-reduce.2.cloned.1.call-done = bf16[128,1024]{0,1:T(8,128)(2,1)} async-done(((bf16[128,1024]{0,1:T(8,128)(2,1)}), bf16[128,1024]{0,1:T(8,128)(2,1)}) %all-reduce.2.cloned.1.call-update) | async-done | bytes 262160 | tf_op jit(solution)/shard_map/psum | solution.py:150
  219.7 1.8 copy.58
  (86 shorter events, 27.2 us)
Async XLA Ops:
  7.2 1.2 copy-start.19
  8.4 0.7 copy-start.9
  9.1 0.8 copy-start.11
  9.8 9.5 %copy-start.20 = (bf16[1,128,1024]{2,1,0:T(8,128)(2,1)S(1)}, bf16[1,128,1024]{2,1,0:T(8,128)(2,1)}, u32[]{:S(2)}) copy-start(bf16[1,128,1024]{2,1,0:T(8,128)(2,1)} %param.7) | copy-start | bytes 786436
  9.8 16.8 %all-to-all-start.3 = ((bf16[16,64,128]{2,1,0:T(8,128)(2,1)}), bf16[16,64,128]{2,1,0:T(8,128)(2,1)S(1)}, u32[]{:S(2)}, u32[]{:S(2)}) async-start(bf16[16,64,128]{2,1,0:T(8,128)(2,1)} %bitcast.29), calls=%async_computation.3 | async-start | bytes 524288 | tf_op jit(solution)/shard_map/all_to_all | solution.py:142
  19.3 1.0 copy-start.21
  20.3 2.7 %copy-start.13 = (bf16[1,128,1024]{1,2,0:T(8,128)(2,1)}, bf16[1,128,1024]{1,2,0:T(8,128)(2,1)S(1)}, u32[]{:S(2)}) copy-start(bf16[1,128,1024]{1,2,0:T(8,128)(2,1)S(1)} %copy.46) | copy-start | bytes 786436
  20.3 1.0 copy-start.22
  21.3 1.6 copy-start.15
  26.6 5.3 %copy-start.7 = (bf16[16,64,128]{2,1,0:T(8,128)(2,1)}, bf16[16,64,128]{2,1,0:T(8,128)(2,1)S(1)}, u32[]{:S(2)}) copy-start(bf16[16,64,128]{2,1,0:T(8,128)(2,1)S(1)} %all-to-all-done.3) | copy-start | bytes 786436
  26.6 12.2 %all-to-all-start = ((bf16[16,64,128]{2,1,0:T(8,128)(2,1)}), bf16[16,64,128]{2,1,0:T(8,128)(2,1)S(1)}, u32[]{:S(2)}, u32[]{:S(2)}) async-start(bf16[16,64,128]{2,1,0:T(8,128)(2,1)} %bitcast.3), calls=%async_computation | async-start | bytes 524288 | tf_op jit(solution)/shard_map/all_to_all | solution.py:131
  38.8 0.7 copy-start.17
  39.5 12.2 %all-to-all-start.1 = ((bf16[16,64,128]{2,1,0:T(8,128)(2,1)}), bf16[16,64,128]{2,1,0:T(8,128)(2,1)S(1)}, u32[]{:S(2)}, u32[]{:S(2)}) async-start(bf16[16,64,128]{2,1,0:T(8,128)(2,1)} %bitcast.13), calls=%async_computation.1 | async-start | bytes 524288 | tf_op jit(solution)/shard_map/all_to_all | solution.py:130
  44.3 1.6 copy-start.18
  46.4 1.9 copy-start
  53.7 1.2 copy-start.4
  55.8 1.2 copy-start.3
  57.0 1.2 copy-start.1
  57.0 1.5 copy-start.6
  58.5 1.2 copy-start.5
  68.4 16.2 %all-to-all-start.5 = ((bf16[64,16,128]{2,0,1:T(8,128)(2,1)}), bf16[64,16,128]{2,0,1:T(8,128)(2,1)}, u32[]{:S(2)}, u32[]{:S(2)}) async-start(bf16[64,16,128]{2,0,1:T(8,128)(2,1)} %copy.53), calls=%async_computation.5 | async-start | bytes 524288 | tf_op jit(solution)/shard_map/all_to_all | solution.py:148
  74.1 1.2 copy-start.2
  81.7 1.0 copy-start.8
  84.7 14.6 %all-to-all-start.4 = ((bf16[64,16,128]{2,0,1:T(8,128)(2,1)}), bf16[64,16,128]{2,0,1:T(8,128)(2,1)S(1)}, u32[]{:S(2)}, u32[]{:S(2)}) async-start(bf16[64,16,128]{2,0,1:T(8,128)(2,1)} %copy.52), calls=%async_computation.4 | async-start | bytes 524288 | tf_op jit(solution)/shard_map/all_to_all | solution.py:147
  91.9 127.7 %all-reduce.2.cloned.1.call-start = ((), (), s32[]{:S(2)}) async-start(), calls=%async_computation.6 | async-start | bytes 524288 | tf_op jit(solution)/shard_map/psum | solution.py:150
  93.1 10.9 %copy-start.14 = (bf16[1,128,1024]{1,2,0:T(8,128)(2,1)S(1)}, bf16[1,128,1024]{1,2,0:T(8,128)(2,1)}, u32[]{:S(2)}) copy-start(bf16[1,128,1024]{1,2,0:T(8,128)(2,1)} %copy-done.13) | copy-start | bytes 786436
  93.2 10.9 %copy-start.16 = (bf16[1,128,1024]{1,2,0:T(8,128)(2,1)S(1)}, bf16[1,128,1024]{1,2,0:T(8,128)(2,1)}, u32[]{:S(2)}) copy-start(bf16[1,128,1024]{1,2,0:T(8,128)(2,1)} %copy-done.15) | copy-start | bytes 786436
  99.2 12.2 %all-to-all-start.2 = ((bf16[64,16,128]{2,0,1:T(8,128)(2,1)}), bf16[64,16,128]{2,0,1:T(8,128)(2,1)S(1)}, u32[]{:S(2)}, u32[]{:S(2)}) async-start(bf16[64,16,128]{2,0,1:T(8,128)(2,1)} %copy_bitcast_fusion), calls=%async_computation.2 | async-start | bytes 524288 | tf_op jit(solution)/shard_map/all_to_all | solution.py:134
  105.0 6.4 %copy-start.10 = (bf16[1,128,1024]{1,2,0:T(8,128)(2,1)S(1)}, bf16[1,128,1024]{1,2,0:T(8,128)(2,1)}, u32[]{:S(2)}) copy-start(bf16[1,128,1024]{1,2,0:T(8,128)(2,1)} %copy-done.9) | copy-start | bytes 786436
  105.0 6.4 %copy-start.12 = (bf16[1,128,1024]{1,2,0:T(8,128)(2,1)S(1)}, bf16[1,128,1024]{1,2,0:T(8,128)(2,1)}, u32[]{:S(2)}) copy-start(bf16[1,128,1024]{1,2,0:T(8,128)(2,1)} %copy-done.11) | copy-start | bytes 786436
Sparse Core Ops, SparseCore 0:
  95.7 123.9 all-reduce.1
where the time goes:
time: 229 us; the launch traced here: 228 us
  waiting for transfers between devices  125 us (55%)
  starting transfers between devices  36.7 us (16%)
  matrix products  33.3 us (15%)
  local copies, waits for them, and re-layouts  16.2 us (7%)
  between operations  14.5 us (6%)
  other arithmetic  2.43 us (1%)
    psum x1, waiting for transfers between devices, on_device(): grad_filter = lax.psum(rounded(dtaps_back).astype(jnp.bfloat16), 'dp').T  106 us
    unnamed x56, local copies, waits for them, and re-layouts  13.2 us
    all_to_all x1, starting transfers between devices, on_device(): lax.all_to_all(grad_state.T, 'seq', split_axis=0, concat_axis=1, tiled=True)  9.36 us
    all_to_all x1, starting transfers between devices, on_device(): lax.all_to_all(dmixed_cols, 'seq', split_axis=1, concat_axis=0, tiled=True)  7.24 us
    all_to_all x1, waiting for transfers between devices, on_device(): lax.all_to_all(dmixed_cols, 'seq', split_axis=1, concat_axis=0, tiled=True)  6.08 us
    all_to_all x1, starting transfers between devices, on_device(): lax.all_to_all(dtaps_cols, 'seq', split_axis=1, concat_axis=0, tiled=True)  5.69 us
    all_to_all x1, waiting for transfers between devices, on_device(): lax.all_to_all(state_cols, 'seq', split_axis=1, concat_axis=0, tiled=True)  5.57 us
    all_to_all x1, starting transfers between devices, on_device(): lax.all_to_all(state_cols, 'seq', split_axis=1, concat_axis=0, tiled=True)  4.78 us
  transfers between devices with their start and end apart: 7, of which 6 were waited for; matrix products, arithmetic and copies ran while one was open for 12% of the time, Pallas kernels for 0%

commit v1 on v0

v1 whole, which is shorter than its diff:
```python
import math

import jax
import jax.numpy as jnp
import numpy as np
from jax import lax
from jax.experimental import pallas as pl
from jax.experimental.pallas import tpu as pltpu
from jax.sharding import Mesh
from jax.sharding import PartitionSpec as P

F32 = jnp.float32
BF16 = jnp.bfloat16
LANES = 128
ROWS = 16
FREQS = 2 * ROWS
HALF = ROWS + 1
CHUNK = 16
VMEM_LIMIT = 48 * 1024 * 1024


def unit(numer, denom):
    angle = 2.0 * math.pi * numer / denom
    return (math.cos(angle), math.sin(angle))


def times_unit(value, numer, denom):
    re, im = value
    numer = numer % denom
    if 4 * numer % denom == 0:
        return ((re, im), (-im, re), (-re, -im), (im, -re))[4 * numer // denom]
    if 8 * numer % denom == 0:
        root = math.sqrt(0.5)
        summed, apart = (re + im) * root, (re - im) * root
        return {1: (apart, summed), 3: (-summed, apart), 5: (-apart, -summed), 7: (summed, -apart)}[
            8 * numer // denom
        ]
    cos, sin = unit(numer, denom)
    return (re * cos - im * sin, re * sin + im * cos)


def add(a, b):
    return (a[0] + b[0], a[1] + b[1])


def sub(a, b):
    return (a[0] - b[0], a[1] - b[1])


def conj(a):
    return (a[0], -a[1])


def complex_dft(values, sign):
    count = len(values)
    if count == 1:
        return list(values)
    even = complex_dft(values[0::2], sign)
    odd = complex_dft(values[1::2], sign)
    turned = [times_unit(v, sign * j, count) for j, v in enumerate(odd)]
    return [add(e, t) for e, t in zip(even, turned)] + [sub(e, t) for e, t in zip(even, turned)]


def odd_freqs(first, second, count):
    turned = [
        times_unit((a, -b), -r, count) for r, (a, b) in enumerate(zip(first, second))
    ]
    return {4 * j + 1: v for j, v in enumerate(complex_dft(turned, -1))}


def real_dft(values, count):
    half, quarter = count // 2, count // 4
    if count == 2:
        return [(values[0] + values[1], None), (values[0] - values[1], None)]
    if len(values) == half:
        folded, apart = values, values
    else:
        folded = [values[r] + values[r + half] for r in range(half)]
        apart = [values[r] - values[r + half] for r in range(half)]
    out = [None] * (half + 1)
    out[0::2] = real_dft(folded, half)
    for freq, value in odd_freqs(apart[:quarter], apart[quarter:], count).items():
        if freq <= half:
            out[freq] = value
        else:
            out[count - freq] = conj(value)
    return out


def real_inverse(freqs, count, keep_half):
    half, quarter = count // 2, count // 4
    if count == 2:
        first, last = freqs[0][0], freqs[1][0]
        return [first + last, first - last]
    even = real_inverse(freqs[0::2], half, False)
    picked = [
        freqs[4 * j + 1] if 4 * j + 1 <= half else conj(freqs[count - 4 * j - 1])
        for j in range(quarter)
    ]
    turned = [times_unit(v, r, count) for r, v in enumerate(complex_dft(picked, 1))]
    odd = [re for re, _ in turned] + [-im for _, im in turned]
    low = [e + o for e, o in zip(even, odd)]
    if keep_half:
        return low
    return low + [e - o for e, o in zip(even, odd)]


def split_table(table):
    high = table.astype(np.float32).astype(BF16)
    low = (table - high.astype(np.float64)).astype(BF16)
    return np.stack([high, low])


def lane_tables():
    idx = np.arange(LANES)
    angle = 2.0 * np.pi / LANES * (idx[:, None] * idx[None, :] % LANES)
    cos, sin = np.cos(angle), np.sin(angle)
    forward = np.block([[cos, -sin], [sin, cos]])
    inverse = np.block([[cos, sin], [-sin, cos]])
    return split_table(forward), split_table(inverse)


def twist_tables(factor):
    padded = FREQS * LANES
    angle = 2.0 * np.pi / padded * (np.arange(HALF)[:, None] * np.arange(LANES)[None, :])
    weight = np.full((HALF, 1), 2.0)
    weight[0] = weight[-1] = 1.0
    weight = weight / padded * factor
    cos, sin = np.cos(angle), np.sin(angle)
    return np.stack([cos, sin, cos * weight, sin * weight], axis=1).astype(np.float32)


def split_value(value):
    high = value.astype(BF16)
    return high, (value - high.astype(F32)).astype(BF16)


def store_parts(high_ref, low_ref, k, chans, first, base, re, im):
    for col, value in ((0, re), (LANES, im)):
        high, low = split_value(value)
        rows = pl.ds(pl.multiple_of(base + k * chans + first, CHUNK), CHUNK)
        high_ref[rows, pl.ds(col, LANES)] = high
        low_ref[rows, pl.ds(col, LANES)] = low


def rows_to_parts(get_row, twist_ref, high_ref, low_ref, chans, first, base):
    freqs = real_dft([get_row(r) for r in range(ROWS)], FREQS)
    for k, (re, im) in enumerate(freqs):
        cos, sin = twist_ref[k, 0:1, :], twist_ref[k, 1:2, :]
        if im is None:
            store_parts(high_ref, low_ref, k, chans, first, base, re * cos, -re * sin)
        else:
            store_parts(
                high_ref, low_ref, k, chans, first, base, re * cos + im * sin, im * cos - re * sin
            )


def lane_transform(high_ref, low_ref, table_ref, out_ref, total, step):
    def body(i, carry):
        rows = pl.ds(pl.multiple_of(i * step, CHUNK), step)
        high, low = high_ref[rows, :], low_ref[rows, :]
        out = jnp.dot(high, table_ref[0], preferred_element_type=F32)
        out += jnp.dot(low, table_ref[0], preferred_element_type=F32)
        out += jnp.dot(high, table_ref[1], preferred_element_type=F32)
        out_ref[rows, :] = out
        return carry

    lax.fori_loop(0, total // step, body, 0)


def correlate_parts(first_ref, second_ref, high_ref, low_ref, first_base, second_base, base, total, sign):
    def body(i, carry):
        start = i * CHUNK
        one = pl.ds(pl.multiple_of(first_base + start, CHUNK), CHUNK)
        two = pl.ds(pl.multiple_of(second_base + start, CHUNK), CHUNK)
        out = pl.ds(pl.multiple_of(base + start, CHUNK), CHUNK)
        are, aim = first_ref[one, 0:LANES], first_ref[one, LANES : 2 * LANES]
        bre, bim = second_ref[two, 0:LANES], second_ref[two, LANES : 2 * LANES]
        if sign > 0:
            re, im = are * bre + aim * bim, are * bim - aim * bre
        else:
            re, im = are * bre - aim * bim, are * bim + aim * bre
        for col, value in ((0, re), (LANES, im)):
            high, low = split_value(value)
            high_ref[out, pl.ds(col, LANES)] = high
            low_ref[out, pl.ds(col, LANES)] = low
        return carry

    lax.fori_loop(0, total // CHUNK, body, 0, unroll=4)


def parts_to_rows(back_ref, twist_ref, chans, first, base):
    freqs = []
    for k in range(HALF):
        rows = pl.ds(pl.multiple_of(base + k * chans + first, CHUNK), CHUNK)
        re, im = back_ref[rows, 0:LANES], back_ref[rows, LANES : 2 * LANES]
        cos, sin = twist_ref[k, 2:3, :], twist_ref[k, 3:4, :]
        if k in (0, ROWS):
            freqs.append((re * cos - im * sin, None))
        else:
            freqs.append((re * cos - im * sin, im * cos + re * sin))
    return real_inverse(freqs, FREQS, True)


def gate_kernel(query, key, value, grad, taps, out):
    own = out.shape[1] // 3
    for pair in range(out.shape[0] // 2):
        cols = pl.ds(pair * LANES, LANES)
        mixed = (key[:, cols].astype(F32) * value[:, cols].astype(F32)).astype(BF16)
        state = (grad[:, cols].astype(F32) * query[:, cols].astype(F32)).astype(BF16)
        for place, block in enumerate((mixed, state, taps[:, cols])):
            turned = block.T
            rows = pl.ds(place * own, own)
            out[2 * pair, rows, :] = turned[:own]
            out[2 * pair + 1, rows, :] = turned[own:]


def taps_grad_kernel(signals, lane_ref, back_lane_ref, twist_ref, spec_ref, out, high, low, back):
    chans = signals.shape[1] // 3
    total = HALF * chans

    def forward(i, carry):
        first = i * CHUNK
        for which in range(2):
            rows = pl.ds(pl.multiple_of(which * chans + first, CHUNK), CHUNK)
            rows_to_parts(
                lambda r: signals[r, rows, :].astype(F32),
                twist_ref, high, low, chans, first, which * total,
            )
        return carry

    lax.fori_loop(0, chans // CHUNK, forward, 0)
    lane_transform(high, low, lane_ref, spec_ref, 2 * total, total // 4)
    correlate_parts(spec_ref, spec_ref, high, low, 0, total, 0, total, 1)
    lane_transform(high, low, back_lane_ref, back, total, total // 4)

    def inverse(i, carry):
        rows = parts_to_rows(back, twist_ref, chans, i * CHUNK, 0)
        for r in range(ROWS):
            out[i, r] = rows[r].astype(BF16)
        return carry

    lax.fori_loop(0, chans // CHUNK, inverse, 0)


def state_kernel(signals, spec_ref, skip_ref, lane_ref, back_lane_ref, twist_ref, out, high, low, taps_spec, back):
    chans = signals.shape[1] // 3
    total = HALF * chans

    def forward(i, carry):
        first = i * CHUNK
        rows = pl.ds(pl.multiple_of(2 * chans + first, CHUNK), CHUNK)
        rows_to_parts(
            lambda r: signals[r, rows, :].astype(F32), twist_ref, high, low, chans, first, 0
        )
        return carry

    lax.fori_loop(0, chans // CHUNK, forward, 0)
    lane_transform(high, low, lane_ref, taps_spec, total, total // 4)
    correlate_parts(taps_spec, spec_ref, high, low, 0, 0, 0, total, -1)
    correlate_parts(taps_spec, spec_ref, high, low, 0, total, total, total, 1)
    lane_transform(high, low, back_lane_ref, back, 2 * total, total // 4)

    def inverse(i, carry):
        first = i * CHUNK
        skip = skip_ref[pl.ds(pl.multiple_of(first, CHUNK), CHUNK), :]
        for which in range(2):
            place = pl.ds(pl.multiple_of(which * chans + first, CHUNK), CHUNK)
            rows = parts_to_rows(back, twist_ref, chans, first, which * total)
            for r in range(ROWS):
                own = signals[r, place, :].astype(F32)
                out[r, place, :] = (rows[r] + skip * own).astype(BF16)
        return carry

    lax.fori_loop(0, chans // CHUNK, inverse, 0)


def output_kernel(back, query, key, value, grad, mixed_out, grad_query, grad_key, grad_value):
    own = back.shape[1] // 2
    for pair in range(back.shape[0] // 2):
        cols = pl.ds(pair * LANES, LANES)
        state, dmixed = (
            jnp.concatenate(
                [back[2 * pair + i, pl.ds(which * own, own), :] for i in range(2)], axis=0
            ).T.astype(F32)
            for which in range(2)
        )
        mixed_out[:, cols] = (query[:, cols].astype(F32) * state).astype(BF16)
        grad_query[:, cols] = (grad[:, cols].astype(F32) * state).astype(BF16)
        grad_key[:, cols] = (dmixed * value[:, cols].astype(F32)).astype(BF16)
        grad_value[:, cols] = (dmixed * key[:, cols].astype(F32)).astype(BF16)


def filter_kernel(blocks, out):
    shares = blocks.shape[0]
    for pair in range(blocks.shape[1] // 2):
        rows = [blocks[i, 2 * pair + s] for s in range(2) for i in range(shares)]
        out[:, pl.ds(pair * LANES, LANES)] = jnp.concatenate(rows, axis=0).T


def call(kernel, shapes, args, scratch=(), flops=0, moved=2 << 20):
    return pl.pallas_call(
        kernel,
        out_shape=shapes,
        in_specs=[pl.BlockSpec(memory_space=pltpu.VMEM)] * len(args),
        out_specs=jax.tree.map(lambda _: pl.BlockSpec(memory_space=pltpu.VMEM), shapes),
        scratch_shapes=list(scratch),
        compiler_params=pltpu.CompilerParams(vmem_limit_bytes=VMEM_LIMIT),
        cost_estimate=pl.CostEstimate(flops=flops, bytes_accessed=moved, transcendentals=0),
    )(*args)


def on_device(query_in, key_in, value_in, filter_taps, skip_gain, grad_out):
    seq_count = lax.axis_size("seq")
    shares = lax.axis_size("dl")
    rows_dev, chan_dev = query_in.shape[1:]
    own = chan_dev // seq_count
    total = HALF * own
    batch = query_in.shape[0] * lax.axis_size("dh") * shares
    factor = 1.0 / math.sqrt(batch * seq_count * rows_dev)
    shape = jax.ShapeDtypeStruct
    forward_lane, inverse_lane = lane_tables()
    query, key, value, grad = query_in[0], key_in[0], value_in[0], grad_out[0]
    skip_own = lax.dynamic_slice_in_dim(skip_gain, lax.axis_index("seq") * own, own)
    skip_own = jnp.broadcast_to(skip_own[:, None], (own, LANES))

    gated = call(
        gate_kernel,
        shape((seq_count, 3 * own, rows_dev), BF16),
        (query, key, value, grad, filter_taps),
    )
    signals = lax.all_to_all(gated, "seq", split_axis=0, concat_axis=0, tiled=True)

    parts = pltpu.VMEM((2 * total, 2 * LANES), BF16)
    spectra, taps_term = call(
        taps_grad_kernel,
        (
            shape((2 * total, 2 * LANES), F32),
            shape((own // CHUNK, seq_count, CHUNK, LANES), BF16),
        ),
        (signals, forward_lane, inverse_lane, twist_tables(factor)),
        (parts, parts, pltpu.VMEM((total, 2 * LANES), F32)),
        flops=10**9,
    )

    terms = taps_term.reshape(shares * seq_count, own // shares, LANES)
    terms = lax.all_to_all(terms, ("dl", "seq"), split_axis=0, concat_axis=0, tiled=True)
    part = terms.reshape(shares, seq_count, own // shares, LANES).astype(F32).sum(0).astype(BF16)
    other = lax.ppermute(part, "dh", [(0, 1), (1, 0)])
    summed = (part.astype(F32) + other.astype(F32)).astype(BF16)
    copies = jnp.broadcast_to(summed[None], (shares,) + summed.shape)
    gathered = lax.all_to_all(copies, "dl", split_axis=0, concat_axis=0, tiled=True)
    grad_filter = call(filter_kernel, shape((rows_dev, chan_dev), BF16), (gathered,))

    results = call(
        state_kernel,
        shape((seq_count, 2 * own, LANES), BF16),
        (signals, spectra, skip_own, forward_lane, inverse_lane, twist_tables(1.0)),
        (
            parts,
            parts,
            pltpu.VMEM((total, 2 * LANES), F32),
            pltpu.VMEM((2 * total, 2 * LANES), F32),
        ),
        flops=10**9,
    )
    back = lax.all_to_all(results, "seq", split_axis=0, concat_axis=0, tiled=True)
    block = shape((rows_dev, chan_dev), BF16)
    outs = call(output_kernel, (block,) * 4, (back, query, key, value, grad))
    return tuple(out[None] for out in outs) + (grad_filter,)


def solution(mesh):
    dp, chan, seq = (mesh.shape[name] for name in ("dp", "chan", "seq"))
    shares = 4
    split_mesh = Mesh(
        mesh.devices.reshape(dp // shares, shares, chan, seq), ("dh", "dl", "chan", "seq")
    )
    rows = P(("dh", "dl"), "seq", "chan")
    taps = P("seq", "chan")
    return jax.shard_map(
        on_device,
        mesh=split_mesh,
        in_specs=(rows, rows, rows, taps, P("chan"), rows),
        out_specs=(rows, rows, rows, rows, taps),
        check_vma=False,
    )
```

time: 229 us -> 85.1 us (0.37)
  the two profiles are of different devices: /device:TPU:2 before, /device:TPU:128 now
where the time goes in v1:
time: 85.1 us; the launch traced here: 84.4 us
  blocking collectives  21.2 us (25%)
  starting transfers between devices  20.1 us (24%)
  waiting for transfers between devices  19.3 us (23%)
  Pallas kernels  14.2 us (17%)
  local copies, waits for them, and re-layouts  7.81 us (9%)
  other arithmetic  1.01 us (1%)
    all_to_all x1, blocking collectives, on_device(): lax.all_to_all(gated, 'seq', split_axis=0, concat_axis=0, tiled=True)  21.2 us
    pallas_call x5, Pallas kernels, call(): pl.pallas_call(kernel, out_shape=shapes, in_specs=[pl.BlockSpec(memory_sp...  14.2 us
    ppermute x1, waiting for transfers between devices, on_device(): other = lax.ppermute(part, 'dh', [(0, 1), (1, 0)])  8.34 us
    all_to_all x1, starting transfers between devices, on_device(): lax.all_to_all(terms, ('dl', 'seq'), split_axis=0, concat_axis=0, tiled=T...  8.33 us
    all_to_all x1, waiting for transfers between devices, on_device(): lax.all_to_all(copies, 'dl', split_axis=0, concat_axis=0, tiled=True)  7.23 us
    all_to_all x1, starting transfers between devices, on_device(): lax.all_to_all(copies, 'dl', split_axis=0, concat_axis=0, tiled=True)  6.27 us
    unnamed x28, local copies, waits for them, and re-layouts  6.23 us
    all_to_all x1, waiting for transfers between devices, on_device(): lax.all_to_all(terms, ('dl', 'seq'), split_axis=0, concat_axis=0, tiled=T...  3.75 us
  transfers between devices with their start and end apart: 4, of which 3 were waited for; matrix products, arithmetic and copies ran while one was open for 2% of the time, Pallas kernels for 9%

profile of v1, /device:TPU:128, one launch (start us, length us, event | category | flops | bytes accessed | tf_op | source)
XLA Modules:
  0.0 84.4 jit_solution(214055212062067899)
XLA Ops:
  0.6 0.0 copy-start
  0.6 0.9 %copy-done = bf16[1,128,1024]{2,1,0:T(8,128)(2,1)S(1)} copy-done((bf16[1,128,1024]{2,1,0:T(8,128)(2,1)S(1)}, bf16[1,128,1024]{2,1,0:T(8,128)(2,1)}, u32[]{:S(2)}) %copy-start) | copy-done | bytes 262168
  1.6 0.9 %copy-done.2 = bf16[1,128,1024]{2,1,0:T(8,128)(2,1)S(1)} copy-done((bf16[1,128,1024]{2,1,0:T(8,128)(2,1)S(1)}, bf16[1,128,1024]{2,1,0:T(8,128)(2,1)}, u32[]{:S(2)}) %copy-start.2) | copy-done | bytes 262168
  2.5 0.9 %copy-done.4 = bf16[1,128,1024]{2,1,0:T(8,128)(2,1)S(1)} copy-done((bf16[1,128,1024]{2,1,0:T(8,128)(2,1)S(1)}, bf16[1,128,1024]{2,1,0:T(8,128)(2,1)}, u32[]{:S(2)}) %copy-start.4) | copy-done | bytes 262168
  3.5 0.9 %copy-done.6 = bf16[1,128,1024]{2,1,0:T(8,128)(2,1)S(1)} copy-done((bf16[1,128,1024]{2,1,0:T(8,128)(2,1)S(1)}, bf16[1,128,1024]{2,1,0:T(8,128)(2,1)}, u32[]{:S(2)}) %copy-start.6) | copy-done | bytes 262168
  4.4 0.9 %copy-done.11 = bf16[128,1024]{1,0:T(8,128)(2,1)S(1)} copy-done((bf16[128,1024]{1,0:T(8,128)(2,1)S(1)}, bf16[128,1024]{1,0:T(8,128)(2,1)}, u32[]{:S(2)}) %copy-start.11) | copy-done | bytes 262168
  5.4 0.3 shard_map.137
  5.7 21.2 %all_to_all.20.signals = bf16[16,192,128]{2,1,0:T(8,128)(2,1)S(1)} all-to-all(bf16[16,192,128]{2,1,0:T(8,128)(2,1)S(1)} %shard_map.137), channel_id=1, replica_groups=mesh['dh'=2,'dl'=4,'chan'=4,'seq'=16] {'seq'}, dimensions={0} | all-to-all | bytes 1572864 | tf_op jit(solution)/shard_map/all_to_all | solution.py:332
  26.9 0.0 copy-done.8
  26.9 0.0 copy-done.9
  26.9 0.0 copy-done.13
  26.9 5.3 %shard_map.138 = (f32[2176,256]{1,0:T(8,128)S(1)}, bf16[4,16,16,128]{3,2,1,0:T(8,128)(2,1)S(1)}) custom-call(bf16[16,192,128]{2,1,0:T(8,128)(2,1)S(1)} %all_to_all.20.signals, bf16[2,256,256]{2,1,0:T(8,128)(2,1)S(1)} %copy-done.9, bf16[2,256,256]{2,1,0:T(8,128)(2,1)S(1)} %copy-done.8, f32[17,4,128]{2,1,0:T(4,128)S(1)} %copy-done.13), custom_call_target="tpu_custom_call" | custom-call | flops 1000000000 | bytes 2097152 | tf_op jit(solution)/shard_map/pallas_call | solution.py:302
  32.2 0.0 copy-start.10
  32.2 0.7 copy-done.10
  32.9 8.3 %all-to-all-start.2 = ((bf16[64,16,128]{2,1,0:T(8,128)(2,1)}), bf16[64,16,128]{2,1,0:T(8,128)(2,1)}, u32[]{:S(2)}, u32[]{:S(2)}) async-start(bf16[64,16,128]{2,1,0:T(8,128)(2,1)} %bitcast.18), calls=%async_computation.2 | async-start | bytes 524288 | tf_op jit(solution)/shard_map/all_to_all | solution.py:347
  41.3 0.8 dynamic_slice.3
  42.0 0.1 broadcast_in_dim.24.skip_ref
  42.1 0.8 copy-done.12
  42.9 6.5 %shard_map.139 = bf16[16,128,128]{2,1,0:T(8,128)(2,1)} custom-call(bf16[16,192,128]{2,1,0:T(8,128)(2,1)S(1)} %all_to_all.20.signals, f32[2176,256]{1,0:T(8,128)S(1)} %get-tuple-element.11.spec_ref, f32[64,128]{1,0:T(8,128)S(1)} %broadcast_in_dim.24.skip_ref, bf16[2,256,256]{2,1,0:T(8,128)(2,1)S(1)} %copy-done.9, bf16[2,256,256]{2,1,0:T(8,128)(2,1)S(1)} %copy-done.8, ...), custom_call_target="tpu_custom_call" | custom-call | flops 1000000000 | bytes 2097152 | tf_op jit(solution)/shard_map/pallas_call | solution.py:302
  49.4 3.8 %all-to-all-done.2 = bf16[64,16,128]{2,1,0:T(8,128)(2,1)} async-done(((bf16[64,16,128]{2,1,0:T(8,128)(2,1)}), bf16[64,16,128]{2,1,0:T(8,128)(2,1)}, u32[]{:S(2)}, u32[]{:S(2)}) %all-to-all-start.2) | async-done | bytes 262176 | tf_op jit(solution)/shard_map/all_to_all | solution.py:347
  53.1 3.6 %all-to-all-start.1 = ((bf16[16,128,128]{2,1,0:T(8,128)(2,1)}), bf16[16,128,128]{2,1,0:T(8,128)(2,1)S(1)}, u32[]{:S(2)}, u32[]{:S(2)}) async-start(bf16[16,128,128]{2,1,0:T(8,128)(2,1)} %shard_map.139), calls=%async_computation.1 | async-start | bytes 1048576 | tf_op jit(solution)/shard_map/all_to_all | solution.py:367
  56.7 1.0 %reduce_sum.12 = bf16[16,16,128]{2,1,0:T(8,128)(2,1)S(1)} reduce(bf16[4,16,16,128]{3,2,1,0:T(8,128)(2,1)} %bitcast.9, bf16[]{:T(256)} %constant.20.clone.1), dimensions={0}, to_apply=%region_0.0 | reduce | flops 98304 | bytes 327682 | tf_op jit(solution)/shard_map/reduce_sum | solution.py:348
  57.7 1.9 %collective-permute-start = (bf16[16,16,128]{2,1,0:T(8,128)(2,1)S(1)}, bf16[16,16,128]{2,1,0:T(8,128)(2,1)S(1)}, u32[]{:S(2)}, u32[]{:S(2)}) collective-permute-start(bf16[16,16,128]{2,1,0:T(8,128)(2,1)S(1)} %reduce_sum.12), channel_id=1, source_target_pairs={{0,256},{256,0},{1,257},{257,1},{2,258},{258,2},{3,259},{259,3},{4... | collective-permute-start | bytes 196616 | tf_op jit(solution)/shard_map/ppermute | solution.py:349
  59.6 8.3 %collective-permute-done = bf16[16,16,128]{2,1,0:T(8,128)(2,1)S(1)} collective-permute-done((bf16[16,16,128]{2,1,0:T(8,128)(2,1)S(1)}, bf16[16,16,128]{2,1,0:T(8,128)(2,1)S(1)}, u32[]{:S(2)}, u32[]{:S(2)}) %collective-permute-start) | collective-permute-done | bytes 65568 | tf_op jit(solution)/shard_map/ppermute | solution.py:349
  68.0 0.0 all-to-all-done.1.back
  68.0 0.7 broadcast_in_dim.29
  68.7 6.3 %all-to-all-start.3 = ((bf16[4,16,16,128]{3,2,1,0:T(8,128)(2,1)}), bf16[4,16,16,128]{3,2,1,0:T(8,128)(2,1)S(1)}, u32[]{:S(2)}, u32[]{:S(2)}) async-start(bf16[4,16,16,128]{3,2,1,0:T(8,128)(2,1)} %broadcast_in_dim.29), calls=%async_computation.3 | async-start | bytes 524288 | tf_op jit(solution)/shard_map/all_to_all | solution.py:352
  75.0 0.0 copy-done.1
  75.0 0.0 copy-done.3
  75.0 1.3 %shard_map.140 = (bf16[128,1024]{1,0:T(8,128)(2,1)}, bf16[128,1024]{1,0:T(8,128)(2,1)}, bf16[128,1024]{1,0:T(8,128)(2,1)}, bf16[128,1024]{1,0:T(8,128)(2,1)}) custom-call(bf16[16,128,128]{2,1,0:T(8,128)(2,1)S(1)} %all-to-all-done.1.back, bf16[128,1024]{1,0:T(8,128)(2,1)S(1)} %bitcast.11, bf16[128,1024]{1,0:T(8,128)(2,1)S(1)} %bitcast.13, ...), custom_call_target="tpu_custom_call" | custom-call | bytes 2097152 | tf_op jit(solution)/shard_map/pallas_call | solution.py:302
  76.3 7.2 %all-to-all-done.3.blocks = bf16[4,16,16,128]{3,2,1,0:T(8,128)(2,1)S(1)} async-done(((bf16[4,16,16,128]{3,2,1,0:T(8,128)(2,1)}), bf16[4,16,16,128]{3,2,1,0:T(8,128)(2,1)S(1)}, u32[]{:S(2)}, u32[]{:S(2)}) %all-to-all-start.3) | async-done | bytes 262176 | tf_op jit(solution)/shard_map/all_to_all | solution.py:352
  83.5 0.8 shard_map.141
  (15 shorter events, 0.0 us)
Async XLA Ops:
  0.6 1.0 %copy-start = (bf16[1,128,1024]{2,1,0:T(8,128)(2,1)S(1)}, bf16[1,128,1024]{2,1,0:T(8,128)(2,1)}, u32[]{:S(2)}) copy-start(bf16[1,128,1024]{2,1,0:T(8,128)(2,1)} %param.10) | copy-start | bytes 786436
  1.6 0.9 %copy-start.2 = (bf16[1,128,1024]{2,1,0:T(8,128)(2,1)S(1)}, bf16[1,128,1024]{2,1,0:T(8,128)(2,1)}, u32[]{:S(2)}) copy-start(bf16[1,128,1024]{2,1,0:T(8,128)(2,1)} %param.11) | copy-start | bytes 786436
  2.5 0.9 %copy-start.4 = (bf16[1,128,1024]{2,1,0:T(8,128)(2,1)S(1)}, bf16[1,128,1024]{2,1,0:T(8,128)(2,1)}, u32[]{:S(2)}) copy-start(bf16[1,128,1024]{2,1,0:T(8,128)(2,1)} %param.12) | copy-start | bytes 786436
  3.5 0.9 %copy-start.6 = (bf16[1,128,1024]{2,1,0:T(8,128)(2,1)S(1)}, bf16[1,128,1024]{2,1,0:T(8,128)(2,1)}, u32[]{:S(2)}) copy-start(bf16[1,128,1024]{2,1,0:T(8,128)(2,1)} %param.15) | copy-start | bytes 786436
  4.4 0.9 %copy-start.11 = (bf16[128,1024]{1,0:T(8,128)(2,1)S(1)}, bf16[128,1024]{1,0:T(8,128)(2,1)}, u32[]{:S(2)}) copy-start(bf16[128,1024]{1,0:T(8,128)(2,1)} %taps.1) | copy-start | bytes 786436
  5.4 21.5 %copy-start.8 = (bf16[2,256,256]{2,1,0:T(8,128)(2,1)S(1)}, bf16[2,256,256]{2,1,0:T(8,128)(2,1)}, u32[]{:S(2)}) copy-start(bf16[2,256,256]{2,1,0:T(8,128)(2,1)} %constant.22.clone.back_lane_ref) | copy-start | bytes 786436
  5.4 21.5 %copy-start.9 = (bf16[2,256,256]{2,1,0:T(8,128)(2,1)S(1)}, bf16[2,256,256]{2,1,0:T(8,128)(2,1)}, u32[]{:S(2)}) copy-start(bf16[2,256,256]{2,1,0:T(8,128)(2,1)} %constant.21.clone.lane_ref) | copy-start | bytes 786436
  5.4 21.5 %copy-start.13 = (f32[17,4,128]{2,1,0:T(4,128)S(1)}, f32[17,4,128]{2,1,0:T(4,128)}, u32[]{:S(2)}) copy-start(f32[17,4,128]{2,1,0:T(4,128)} %constant.23.clone.twist_ref) | copy-start | bytes 104452
  32.2 0.7 copy-start.10
  32.9 20.2 %all-to-all-start.2 = ((bf16[64,16,128]{2,1,0:T(8,128)(2,1)}), bf16[64,16,128]{2,1,0:T(8,128)(2,1)}, u32[]{:S(2)}, u32[]{:S(2)}) async-start(bf16[64,16,128]{2,1,0:T(8,128)(2,1)} %bitcast.18), calls=%async_computation.2 | async-start | bytes 524288 | tf_op jit(solution)/shard_map/all_to_all | solution.py:347
  42.1 0.8 copy-start.12
  49.3 25.7 %copy-start.1 = (bf16[1,128,1024]{2,1,0:T(8,128)(2,1)S(1)}, bf16[1,128,1024]{2,1,0:T(8,128)(2,1)}, u32[]{:S(2)}) copy-start(bf16[1,128,1024]{2,1,0:T(8,128)(2,1)} %param.10) | copy-start | bytes 786436
  49.3 25.7 %copy-start.3 = (bf16[1,128,1024]{2,1,0:T(8,128)(2,1)S(1)}, bf16[1,128,1024]{2,1,0:T(8,128)(2,1)}, u32[]{:S(2)}) copy-start(bf16[1,128,1024]{2,1,0:T(8,128)(2,1)} %param.11) | copy-start | bytes 786436
  49.3 25.7 %copy-start.5 = (bf16[1,128,1024]{2,1,0:T(8,128)(2,1)S(1)}, bf16[1,128,1024]{2,1,0:T(8,128)(2,1)}, u32[]{:S(2)}) copy-start(bf16[1,128,1024]{2,1,0:T(8,128)(2,1)} %param.12) | copy-start | bytes 786436
  49.3 25.7 %copy-start.7 = (bf16[1,128,1024]{2,1,0:T(8,128)(2,1)S(1)}, bf16[1,128,1024]{2,1,0:T(8,128)(2,1)}, u32[]{:S(2)}) copy-start(bf16[1,128,1024]{2,1,0:T(8,128)(2,1)} %param.15) | copy-start | bytes 786436
  53.1 14.9 %all-to-all-start.1 = ((bf16[16,128,128]{2,1,0:T(8,128)(2,1)}), bf16[16,128,128]{2,1,0:T(8,128)(2,1)S(1)}, u32[]{:S(2)}, u32[]{:S(2)}) async-start(bf16[16,128,128]{2,1,0:T(8,128)(2,1)} %shard_map.139), calls=%async_computation.1 | async-start | bytes 1048576 | tf_op jit(solution)/shard_map/all_to_all | solution.py:367
  57.7 10.3 %collective-permute-start = (bf16[16,16,128]{2,1,0:T(8,128)(2,1)S(1)}, bf16[16,16,128]{2,1,0:T(8,128)(2,1)S(1)}, u32[]{:S(2)}, u32[]{:S(2)}) collective-permute-start(bf16[16,16,128]{2,1,0:T(8,128)(2,1)S(1)} %reduce_sum.12), channel_id=1, source_target_pairs={{0,256},{256,0},{1,257},{257,1},{2,258},{258,2},{3,259},{259,3},{4... | collective-permute-start | bytes 196616 | tf_op jit(solution)/shard_map/ppermute | solution.py:349
  68.7 14.8 %all-to-all-start.3 = ((bf16[4,16,16,128]{3,2,1,0:T(8,128)(2,1)}), bf16[4,16,16,128]{3,2,1,0:T(8,128)(2,1)S(1)}, u32[]{:S(2)}, u32[]{:S(2)}) async-start(bf16[4,16,16,128]{3,2,1,0:T(8,128)(2,1)} %broadcast_in_dim.29), calls=%async_computation.3 | async-start | bytes 524288 | tf_op jit(solution)/shard_map/all_to_all | solution.py:352

commit v2 on v1

--- a/solution.py
+++ b/solution.py
@@ -16,7 +16,6 @@
 FREQS = 2 * ROWS
 HALF = ROWS + 1
 CHUNK = 16
-VMEM_LIMIT = 48 * 1024 * 1024
 
 
 def unit(numer, denom):
@@ -168,25 +167,30 @@
     lax.fori_loop(0, total // step, body, 0)
 
 
-def correlate_parts(first_ref, second_ref, high_ref, low_ref, first_base, second_base, base, total, sign):
+def multiply_parts(first_ref, second_ref, high_ref, low_ref, first_bases, second_bases, base, total, sign):
     def body(i, carry):
         start = i * CHUNK
-        one = pl.ds(pl.multiple_of(first_base + start, CHUNK), CHUNK)
-        two = pl.ds(pl.multiple_of(second_base + start, CHUNK), CHUNK)
         out = pl.ds(pl.multiple_of(base + start, CHUNK), CHUNK)
-        are, aim = first_ref[one, 0:LANES], first_ref[one, LANES : 2 * LANES]
-        bre, bim = second_ref[two, 0:LANES], second_ref[two, LANES : 2 * LANES]
-        if sign > 0:
-            re, im = are * bre + aim * bim, are * bim - aim * bre
-        else:
-            re, im = are * bre - aim * bim, are * bim + aim * bre
+        terms = []
+        for first_base, second_base in zip(first_bases, second_bases):
+            one = pl.ds(pl.multiple_of(first_base + start, CHUNK), CHUNK)
+            two = pl.ds(pl.multiple_of(second_base + start, CHUNK), CHUNK)
+            are, aim = first_ref[one, 0:LANES], first_ref[one, LANES : 2 * LANES]
+            bre, bim = second_ref[two, 0:LANES], second_ref[two, LANES : 2 * LANES]
+            if sign > 0:
+                terms.append((are * bre + aim * bim, are * bim - aim * bre))
+            else:
+                terms.append((are * bre - aim * bim, are * bim + aim * bre))
+        re, im = terms[0]
+        for more in terms[1:]:
+            re, im = re + more[0], im + more[1]
         for col, value in ((0, re), (LANES, im)):
             high, low = split_value(value)
             high_ref[out, pl.ds(col, LANES)] = high
             low_ref[out, pl.ds(col, LANES)] = low
         return carry
 
-    lax.fori_loop(0, total // CHUNK, body, 0, unroll=4)
+    lax.fori_loop(0, total // CHUNK, body, 0, unroll=2)
 
 
 def parts_to_rows(back_ref, twist_ref, chans, first, base):
@@ -202,37 +206,68 @@
     return real_inverse(freqs, FREQS, True)
 
 
-def gate_kernel(query, key, value, grad, taps, out):
-    own = out.shape[1] // 3
-    for pair in range(out.shape[0] // 2):
-        cols = pl.ds(pair * LANES, LANES)
-        mixed = (key[:, cols].astype(F32) * value[:, cols].astype(F32)).astype(BF16)
-        state = (grad[:, cols].astype(F32) * query[:, cols].astype(F32)).astype(BF16)
-        for place, block in enumerate((mixed, state, taps[:, cols])):
+def start_copies(pairs, sems):
+    copies = [pltpu.make_async_copy(a, b, sems.at[i]) for i, (a, b) in enumerate(pairs)]
+    for copy in copies:
+        copy.start()
+    return copies
+
+
+def gate_kernel(query, key, value, grad, taps, out, query_v, key_v, value_v, grad_v, taps_v, out_v, sems, out_sem):
+    peers = out.shape[0]
+    own = taps.shape[1] // peers
+    share = out.shape[1] - 2 * own
+    pieces = LANES // own
+    begin = lax.axis_index("pl") * share
+    held = ((key, key_v), (value, value_v), (grad, grad_v), (query, query_v), (taps, taps_v))
+    copies = start_copies(held, sems)
+    for copy in copies:
+        copy.wait()
+    sent = []
+    for tile in range(peers // pieces):
+        cols = pl.ds(tile * LANES, LANES)
+        mixed = (key_v[:, cols].astype(F32) * value_v[:, cols].astype(F32)).astype(BF16)
+        state = (grad_v[:, cols].astype(F32) * query_v[:, cols].astype(F32)).astype(BF16)
+        for place, block in enumerate((mixed, state)):
             turned = block.T
-            rows = pl.ds(place * own, own)
-            out[2 * pair, rows, :] = turned[:own]
-            out[2 * pair + 1, rows, :] = turned[own:]
+            for i in range(pieces):
+                out_v[tile * pieces + i, pl.ds(place * own, own), :] = turned[i * own : (i + 1) * own]
+        turned = taps_v[:, cols].T
+        for i in range(pieces):
+            low = turned[i * own : i * own + share]
+            high = turned[i * own + share : (i + 1) * own]
+            out_v[tile * pieces + i, pl.ds(2 * own, share), :] = jnp.where(begin == 0, low, high)
+        rows = pl.ds(tile * pieces, pieces)
+        copy = pltpu.make_async_copy(out_v.at[rows], out.at[rows], out_sem.at[tile])
+        copy.start()
+        sent.append(copy)
+    for copy in sent:
+        copy.wait()
 
 
 def taps_grad_kernel(signals, lane_ref, back_lane_ref, twist_ref, spec_ref, out, high, low, back):
-    chans = signals.shape[1] // 3
+    batch = signals.shape[0] // ROWS
+    chans = out.shape[0] * CHUNK
     total = HALF * chans
 
     def forward(i, carry):
         first = i * CHUNK
         for which in range(2):
             rows = pl.ds(pl.multiple_of(which * chans + first, CHUNK), CHUNK)
-            rows_to_parts(
-                lambda r: signals[r, rows, :].astype(F32),
-                twist_ref, high, low, chans, first, which * total,
-            )
+            for b in range(batch):
+                rows_to_parts(
+                    lambda r: signals[b * ROWS + r, rows, :].astype(F32),
+                    twist_ref, high, low, chans, first, (which * batch + b) * total,
+                )
         return carry
 
     lax.fori_loop(0, chans // CHUNK, forward, 0)
-    lane_transform(high, low, lane_ref, spec_ref, 2 * total, total // 4)
-    correlate_parts(spec_ref, spec_ref, high, low, 0, total, 0, total, 1)
-    lane_transform(high, low, back_lane_ref, back, total, total // 4)
+    lane_transform(high, low, lane_ref, spec_ref, 2 * batch * total, total // 2)
+    multiply_parts(
+        spec_ref, spec_ref, high, low,
+        [b * total for b in range(batch)], [(batch + b) * total for b in range(batch)], 0, total, 1,
+    )
+    lane_transform(high, low, back_lane_ref, back, total, total // 2)
 
     def inverse(i, carry):
         rows = parts_to_rows(back, twist_ref, chans, i * CHUNK, 0)
@@ -244,32 +279,37 @@
 
 
 def state_kernel(signals, spec_ref, skip_ref, lane_ref, back_lane_ref, twist_ref, out, high, low, taps_spec, back):
-    chans = signals.shape[1] // 3
+    batch = signals.shape[0] // ROWS
+    chans = out.shape[1] // 2
+    share = signals.shape[1] - 2 * chans
     total = HALF * chans
 
-    def forward(i, carry):
-        first = i * CHUNK
-        rows = pl.ds(pl.multiple_of(2 * chans + first, CHUNK), CHUNK)
-        rows_to_parts(
-            lambda r: signals[r, rows, :].astype(F32), twist_ref, high, low, chans, first, 0
-        )
-        return carry
-
-    lax.fori_loop(0, chans // CHUNK, forward, 0)
-    lane_transform(high, low, lane_ref, taps_spec, total, total // 4)
-    correlate_parts(taps_spec, spec_ref, high, low, 0, 0, 0, total, -1)
-    correlate_parts(taps_spec, spec_ref, high, low, 0, total, total, total, 1)
-    lane_transform(high, low, back_lane_ref, back, 2 * total, total // 4)
+    for b in range(batch):
+        for first in range(0, share, CHUNK):
+            rows = pl.ds(2 * chans + first, CHUNK)
+            rows_to_parts(
+                lambda r: signals[b * ROWS + r, rows, :].astype(F32),
+                twist_ref, high, low, chans, b * share + first, 0,
+            )
+    lane_transform(high, low, lane_ref, taps_spec, total, total // 2)
+    for which in range(2):
+        for b in range(batch):
+            base = (which * batch + b) * total
+            multiply_parts(
+                taps_spec, spec_ref, high, low, [0], [base], base, total, 1 if which else -1
+            )
+    lane_transform(high, low, back_lane_ref, back, 2 * batch * total, total // 2)
 
     def inverse(i, carry):
         first = i * CHUNK
         skip = skip_ref[pl.ds(pl.multiple_of(first, CHUNK), CHUNK), :]
         for which in range(2):
             place = pl.ds(pl.multiple_of(which * chans + first, CHUNK), CHUNK)
-            rows = parts_to_rows(back, twist_ref, chans, first, which * total)
-            for r in range(ROWS):
-                own = signals[r, place, :].astype(F32)
-                out[r, place, :] = (rows[r] + skip * own).astype(BF16)
+            for b in range(batch):
+                rows = parts_to_rows(back, twist_ref, chans, first, (which * batch + b) * total)
+                for r in range(ROWS):
+                    own = signals[b * ROWS + r, place, :].astype(F32)
+                    out[b * ROWS + r, place, :] = (rows[r] + skip * own).astype(BF16)
         return carry
 
     lax.fori_loop(0, chans // CHUNK, inverse, 0)
@@ -277,11 +317,12 @@
 
 def output_kernel(back, query, key, value, grad, mixed_out, grad_query, grad_key, grad_value):
     own = back.shape[1] // 2
-    for pair in range(back.shape[0] // 2):
-        cols = pl.ds(pair * LANES, LANES)
+    pieces = LANES // own
+    for tile in range(back.shape[0] // pieces):
+        cols = pl.ds(tile * LANES, LANES)
         state, dmixed = (
             jnp.concatenate(
-                [back[2 * pair + i, pl.ds(which * own, own), :] for i in range(2)], axis=0
+                [back[tile * pieces + i, pl.ds(which * own, own), :] for i in range(pieces)], axis=0
             ).T.astype(F32)
             for which in range(2)
         )
@@ -292,91 +333,127 @@
 
 
 def filter_kernel(blocks, out):
-    shares = blocks.shape[0]
-    for pair in range(blocks.shape[1] // 2):
-        rows = [blocks[i, 2 * pair + s] for s in range(2) for i in range(shares)]
-        out[:, pl.ds(pair * LANES, LANES)] = jnp.concatenate(rows, axis=0).T
-
-
-def call(kernel, shapes, args, scratch=(), flops=0, moved=2 << 20):
+    shares, owners, depth = blocks.shape[:3]
+    pieces = LANES // (shares * depth)
+    for tile in range(owners // pieces):
+        rows = [blocks[i, tile * pieces + s] for s in range(pieces) for i in range(shares)]
+        out[:, pl.ds(tile * LANES, LANES)] = jnp.concatenate(rows, axis=0).T
+
+
+def call(kernel, shapes, args, scratch=(), in_hbm=False, out_hbm=False, flops=0, moved=2 << 20, limit=24):
+    place = lambda hbm: pl.BlockSpec(memory_space=pltpu.HBM if hbm else pltpu.VMEM)
     return pl.pallas_call(
         kernel,
         out_shape=shapes,
-        in_specs=[pl.BlockSpec(memory_space=pltpu.VMEM)] * len(args),
-        out_specs=jax.tree.map(lambda _: pl.BlockSpec(memory_space=pltpu.VMEM), shapes),
+        in_specs=[place(in_hbm)] * len(args),
+        out_specs=jax.tree.map(lambda _: place(out_hbm), shapes),
         scratch_shapes=list(scratch),
-        compiler_params=pltpu.CompilerParams(vmem_limit_bytes=VMEM_LIMIT),
+        compiler_params=pltpu.CompilerParams(vmem_limit_bytes=limit << 20),
         cost_estimate=pl.CostEstimate(flops=flops, bytes_accessed=moved, transcendentals=0),
     )(*args)
 
 
-def on_device(query_in, key_in, value_in, filter_taps, skip_gain, grad_out):
-    seq_count = lax.axis_size("seq")
-    shares = lax.axis_size("dl")
-    rows_dev, chan_dev = query_in.shape[1:]
-    own = chan_dev // seq_count
+def gate(query, key, value, grad, taps, peers):
+    rows_dev, chan_dev = query.shape
+    own = chan_dev // peers
+    out_shape = (peers, 2 * own + own // 2, rows_dev)
+    return call(
+        gate_kernel,
+        jax.ShapeDtypeStruct(out_shape, BF16),
+        (query, key, value, grad, taps),
+        [pltpu.VMEM((rows_dev, chan_dev), BF16)] * 5
+        + [
+            pltpu.VMEM(out_shape, BF16),
+            pltpu.SemaphoreType.DMA((5,)),
+            pltpu.SemaphoreType.DMA((chan_dev // LANES,)),
+        ],
+        in_hbm=True,
+        out_hbm=True,
+    )
+
+
+def taps_grad(signals, own, factor):
     total = HALF * own
-    batch = query_in.shape[0] * lax.axis_size("dh") * shares
-    factor = 1.0 / math.sqrt(batch * seq_count * rows_dev)
+    batch = signals.shape[0] // ROWS
+    forward_lane, inverse_lane = lane_tables()
     shape = jax.ShapeDtypeStruct
-    forward_lane, inverse_lane = lane_tables()
-    query, key, value, grad = query_in[0], key_in[0], value_in[0], grad_out[0]
-    skip_own = lax.dynamic_slice_in_dim(skip_gain, lax.axis_index("seq") * own, own)
-    skip_own = jnp.broadcast_to(skip_own[:, None], (own, LANES))
-
-    gated = call(
-        gate_kernel,
-        shape((seq_count, 3 * own, rows_dev), BF16),
-        (query, key, value, grad, filter_taps),
-    )
-    signals = lax.all_to_all(gated, "seq", split_axis=0, concat_axis=0, tiled=True)
-
-    parts = pltpu.VMEM((2 * total, 2 * LANES), BF16)
-    spectra, taps_term = call(
+    parts = pltpu.VMEM((2 * batch * total, 2 * LANES), BF16)
+    return call(
         taps_grad_kernel,
         (
-            shape((2 * total, 2 * LANES), F32),
-            shape((own // CHUNK, seq_count, CHUNK, LANES), BF16),
+            shape((2 * batch * total, 2 * LANES), F32),
+            shape((own // CHUNK, ROWS, CHUNK, LANES), BF16),
         ),
         (signals, forward_lane, inverse_lane, twist_tables(factor)),
         (parts, parts, pltpu.VMEM((total, 2 * LANES), F32)),
         flops=10**9,
     )
 
-    terms = taps_term.reshape(shares * seq_count, own // shares, LANES)
-    terms = lax.all_to_all(terms, ("dl", "seq"), split_axis=0, concat_axis=0, tiled=True)
-    part = terms.reshape(shares, seq_count, own // shares, LANES).astype(F32).sum(0).astype(BF16)
-    other = lax.ppermute(part, "dh", [(0, 1), (1, 0)])
-    summed = (part.astype(F32) + other.astype(F32)).astype(BF16)
-    copies = jnp.broadcast_to(summed[None], (shares,) + summed.shape)
-    gathered = lax.all_to_all(copies, "dl", split_axis=0, concat_axis=0, tiled=True)
-    grad_filter = call(filter_kernel, shape((rows_dev, chan_dev), BF16), (gathered,))
-
-    results = call(
+
+def states(signals, spectra, skip_own, own):
+    total = HALF * own
+    batch = signals.shape[0] // ROWS
+    forward_lane, inverse_lane = lane_tables()
+    parts = pltpu.VMEM((2 * batch * total, 2 * LANES), BF16)
+    return call(
         state_kernel,
-        shape((seq_count, 2 * own, LANES), BF16),
+        jax.ShapeDtypeStruct((batch * ROWS, 2 * own, LANES), BF16),
         (signals, spectra, skip_own, forward_lane, inverse_lane, twist_tables(1.0)),
         (
             parts,
             parts,
             pltpu.VMEM((total, 2 * LANES), F32),
-            pltpu.VMEM((2 * total, 2 * LANES), F32),
+            pltpu.VMEM((2 * batch * total, 2 * LANES), F32),
         ),
         flops=10**9,
     )
-    back = lax.all_to_all(results, "seq", split_axis=0, concat_axis=0, tiled=True)
-    block = shape((rows_dev, chan_dev), BF16)
-    outs = call(output_kernel, (block,) * 4, (back, query, key, value, grad))
+
+
+def outputs(back, query, key, value, grad):
+    block = jax.ShapeDtypeStruct(query.shape, BF16)
+    return call(output_kernel, (block,) * 4, (back, query, key, value, grad))
+
+
+def on_device(query_in, key_in, value_in, filter_taps, skip_gain, grad_out):
+    seq_count, pair = lax.axis_size("seq"), lax.axis_size("pl")
+    peers = seq_count * pair
+    rows_dev, chan_dev = query_in.shape[1:]
+    own = chan_dev // peers
+    batch = query_in.shape[0] * lax.axis_size("dh") * lax.axis_size("dm") * pair
+    factor = 1.0 / math.sqrt(batch * seq_count * rows_dev)
+    query, key, value, grad = query_in[0], key_in[0], value_in[0], grad_out[0]
+    place = lax.axis_index("pl") * seq_count + lax.axis_index("seq")
+    skip_own = lax.dynamic_slice_in_dim(skip_gain, place * own, own)
+    skip_own = jnp.broadcast_to(skip_own[:, None], (own, LANES))
+
+    def swap(values, axes):
+        return lax.all_to_all(values, axes, split_axis=0, concat_axis=0, tiled=True)
+
+    signals = swap(gate(query, key, value, grad, filter_taps, peers), ("pl", "seq"))
+    spectra, taps_term = taps_grad(signals, own, factor)
+
+    groups = own // CHUNK
+    terms = swap(taps_term.reshape(groups * seq_count, CHUNK, LANES), ("dm", "seq"))
+    part = terms.reshape(groups, seq_count, CHUNK, LANES).astype(F32).sum(0).astype(BF16)
+    other = lax.ppermute(part, "dh", [(0, 1), (1, 0)])
+    summed = (part.astype(F32) + other.astype(F32)).astype(BF16)
+    copies = jnp.broadcast_to(summed[None], (groups * pair,) + summed.shape)
+    gathered = swap(copies, ("dm", "pl")).reshape(groups, peers, CHUNK, LANES)
+    grad_filter = call(
+        filter_kernel, jax.ShapeDtypeStruct((rows_dev, chan_dev), BF16), (gathered,)
+    )
+
+    back = swap(states(signals, spectra, skip_own, own), ("pl", "seq"))
+    outs = outputs(back, query, key, value, grad)
     return tuple(out[None] for out in outs) + (grad_filter,)
 
 
 def solution(mesh):
     dp, chan, seq = (mesh.shape[name] for name in ("dp", "chan", "seq"))
-    shares = 4
     split_mesh = Mesh(
-        mesh.devices.reshape(dp // shares, shares, chan, seq), ("dh", "dl", "chan", "seq")
-    )
-    rows = P(("dh", "dl"), "seq", "chan")
+        mesh.devices.reshape(dp // 4, 2, 2, chan, seq), ("dh", "dm", "pl", "chan", "seq")
+    )
+    rows = P(("dh", "dm", "pl"), "seq", "chan")
     taps = P("seq", "chan")
     return jax.shard_map(
         on_device,

time: 85.1 us -> 94.2 us (1.11)
  the two profiles are of different devices: /device:TPU:128 before, /device:TPU:64 now
where the time goes in v2:
time: 94.2 us; the launch traced here: 93.5 us
  blocking collectives  34.7 us (37%)
  starting transfers between devices  21.2 us (23%)
  Pallas kernels  15.2 us (16%)
  waiting for transfers between devices  11.5 us (12%)
  local copies, waits for them, and re-layouts  10.1 us (11%)
    all_to_all x2, blocking collectives, swap(): return lax.all_to_all(values, axes, split_axis=0, concat_axis=0, tiled=True)  34.7 us
    pallas_call x5, Pallas kernels, call(): pl.pallas_call(kernel, out_shape=shapes, in_specs=[place(in_hbm)] * len(a...  15.2 us
    all_to_all x2, starting transfers between devices, swap(): return lax.all_to_all(values, axes, split_axis=0, concat_axis=0, tiled=True)  12.1 us
    ppermute x1, starting transfers between devices, on_device(): other = lax.ppermute(part, 'dh', [(0, 1), (1, 0)])  9.1 us
    unnamed x30, local copies, waits for them, and re-layouts  8.57 us
    all_to_all x2, waiting for transfers between devices, swap(): return lax.all_to_all(values, axes, split_axis=0, concat_axis=0, tiled=True)  8.4 us
    ppermute x1, waiting for transfers between devices, on_device(): other = lax.ppermute(part, 'dh', [(0, 1), (1, 0)])  3.13 us
  transfers between devices with their start and end apart: 3, of which 2 were waited for; matrix products, arithmetic and copies ran while one was open for 1% of the time, Pallas kernels for 8%

profile of v2, /device:TPU:64, one launch (start us, length us, event | category | flops | bytes accessed | tf_op | source)
XLA Modules:
  0.0 93.5 jit_solution(15508179655510754245)
XLA Ops:
  0.6 0.0 copy-start
  0.6 0.9 %copy-done = bf16[1,128,1024]{2,1,0:T(8,128)(2,1)S(1)} copy-done((bf16[1,128,1024]{2,1,0:T(8,128)(2,1)S(1)}, bf16[1,128,1024]{2,1,0:T(8,128)(2,1)}, u32[]{:S(2)}) %copy-start) | copy-done | bytes 262168
  1.6 0.9 %copy-done.2 = bf16[1,128,1024]{2,1,0:T(8,128)(2,1)S(1)} copy-done((bf16[1,128,1024]{2,1,0:T(8,128)(2,1)S(1)}, bf16[1,128,1024]{2,1,0:T(8,128)(2,1)}, u32[]{:S(2)}) %copy-start.2) | copy-done | bytes 262168
  2.5 0.9 %copy-done.4 = bf16[1,128,1024]{2,1,0:T(8,128)(2,1)S(1)} copy-done((bf16[1,128,1024]{2,1,0:T(8,128)(2,1)S(1)}, bf16[1,128,1024]{2,1,0:T(8,128)(2,1)}, u32[]{:S(2)}) %copy-start.4) | copy-done | bytes 262168
  3.5 0.9 %copy-done.6 = bf16[1,128,1024]{2,1,0:T(8,128)(2,1)S(1)} copy-done((bf16[1,128,1024]{2,1,0:T(8,128)(2,1)S(1)}, bf16[1,128,1024]{2,1,0:T(8,128)(2,1)}, u32[]{:S(2)}) %copy-start.6) | copy-done | bytes 262168
  4.4 0.9 %copy-done.8 = bf16[128,1024]{1,0:T(8,128)(2,1)S(1)} copy-done((bf16[128,1024]{1,0:T(8,128)(2,1)S(1)}, bf16[128,1024]{1,0:T(8,128)(2,1)}, u32[]{:S(2)}) %copy-start.8) | copy-done | bytes 262168
  5.4 1.8 %shard_map.155 = bf16[32,80,128]{2,1,0:T(8,128)(2,1)S(1)} custom-call(bf16[128,1024]{1,0:T(8,128)(2,1)S(1)} %bitcast.11, bf16[128,1024]{1,0:T(8,128)(2,1)S(1)} %bitcast.13, bf16[128,1024]{1,0:T(8,128)(2,1)S(1)} %bitcast.15, bf16[128,1024]{1,0:T(8,128)(2,1)S(1)} %bitcast.17, bf16[128,1024]{1,0:T(8,128)(2,1)S(1)} %copy-done.8), custom_call_target="tpu_custom_call" | custom-call | bytes 2097152 | tf_op jit(solution)/shard_map/pallas_call | solution.py:345
  7.2 21.3 %all_to_all.20.signals = bf16[32,80,128]{2,1,0:T(8,128)(2,1)S(1)} all-to-all(bf16[32,80,128]{2,1,0:T(8,128)(2,1)S(1)} %shard_map.155), channel_id=1, replica_groups=mesh['dh'=2,'dm'=2,'pl'=2,'chan'=4,'seq'=16] {'pl','seq'}, dimensions={0} | all-to-all | bytes 1310720 | tf_op jit(solution)/shard_map/all_to_all | solution.py:430
  28.5 0.0 copy-done.9
  28.5 0.0 copy-done.11
  28.5 0.0 copy-done.14
  28.5 0.0 copy-start.13
  28.5 4.5 %shard_map.156 = (f32[2176,256]{1,0:T(8,128)S(1)}, bf16[2,16,16,128]{3,2,1,0:T(8,128)(2,1)S(1)}) custom-call(bf16[32,80,128]{2,1,0:T(8,128)(2,1)S(1)} %all_to_all.20.signals, bf16[2,256,256]{2,1,0:T(8,128)(2,1)S(1)} %copy-done.11, bf16[2,256,256]{2,1,0:T(8,128)(2,1)S(1)} %copy-done.9, f32[17,4,128]{2,1,0:T(4,128)S(1)} %copy-done.14), custom_call_target="tpu_custom_call" | custom-call | flops 1000000000 | bytes 2097152 | tf_op jit(solution)/shard_map/pallas_call | solution.py:345
  33.1 13.4 %all_to_all.21 = bf16[32,16,128]{2,1,0:T(8,128)(2,1)S(1)} all-to-all(bf16[32,16,128]{2,1,0:T(8,128)(2,1)S(1)} %bitcast.19), channel_id=1, replica_groups=mesh['dh'=2,'dm'=2,'pl'=2,'chan'=4,'seq'=16] {'dm','seq'}, dimensions={0} | all-to-all | bytes 262144 | tf_op jit(solution)/shard_map/all_to_all | solution.py:430
  46.5 9.1 %collective-permute-start = (bf16[16,16,128]{2,1,0:T(8,128)(2,1)S(1)}, bf16[16,16,128]{2,1,0:T(8,128)(2,1)S(1)}, u32[]{:S(2)}, u32[]{:S(2)}) collective-permute-start(bf16[16,16,128]{2,1,0:T(8,128)(2,1)S(1)} %reduce_sum.12), channel_id=1, source_target_pairs={{0,256},{256,0},{1,257},{257,1},{2,258},{258,2},{3,259},{259,3},{4... | collective-permute-start | bytes 196616 | tf_op jit(solution)/shard_map/ppermute | solution.py:438
  55.6 3.1 %collective-permute-done = bf16[16,16,128]{2,1,0:T(8,128)(2,1)S(1)} collective-permute-done((bf16[16,16,128]{2,1,0:T(8,128)(2,1)S(1)}, bf16[16,16,128]{2,1,0:T(8,128)(2,1)S(1)}, u32[]{:S(2)}, u32[]{:S(2)}) %collective-permute-start) | collective-permute-done | bytes 65568 | tf_op jit(solution)/shard_map/ppermute | solution.py:438
  58.7 0.7 broadcast_in_dim.29
  59.5 7.6 %all-to-all-start.3 = ((bf16[4,16,16,128]{3,2,1,0:T(8,128)(2,1)}), bf16[4,16,16,128]{3,2,1,0:T(8,128)(2,1)}, u32[]{:S(2)}, u32[]{:S(2)}) async-start(bf16[4,16,16,128]{3,2,1,0:T(8,128)(2,1)} %broadcast_in_dim.29), calls=%async_computation.3 | async-start | bytes 524288 | tf_op jit(solution)/shard_map/all_to_all | solution.py:430
  67.0 0.8 dynamic_slice.3
  67.8 0.1 broadcast_in_dim.24.skip_ref
  67.9 0.0 copy-done.13
  67.9 0.9 %copy-done.10 = bf16[2,256,256]{2,1,0:T(8,128)(2,1)S(1)} copy-done((bf16[2,256,256]{2,1,0:T(8,128)(2,1)S(1)}, bf16[2,256,256]{2,1,0:T(8,128)(2,1)}, u32[]{:S(2)}) %copy-start.10) | copy-done | bytes 262168
  68.8 0.9 %copy-done.12 = bf16[2,256,256]{2,1,0:T(8,128)(2,1)S(1)} copy-done((bf16[2,256,256]{2,1,0:T(8,128)(2,1)S(1)}, bf16[2,256,256]{2,1,0:T(8,128)(2,1)}, u32[]{:S(2)}) %copy-start.12) | copy-done | bytes 262168
  69.8 5.8 %shard_map.157 = bf16[32,64,128]{2,1,0:T(8,128)(2,1)} custom-call(bf16[32,80,128]{2,1,0:T(8,128)(2,1)S(1)} %all_to_all.20.signals, f32[2176,256]{1,0:T(8,128)S(1)} %get-tuple-element.11.spec_ref, f32[32,128]{1,0:T(8,128)S(1)} %broadcast_in_dim.24.skip_ref, bf16[2,256,256]{2,1,0:T(8,128)(2,1)S(1)} %copy-done.12, bf16[2,256,256]{2,1,0:T(8,128)(2,1)S(1)} %copy-done.10, ...), custom_call_target="tpu_custom_call" | custom-call | flops 1000000000 | bytes 2097152 | tf_op jit(solution)/shard_map/pallas_call | solution.py:345
  75.6 0.0 all-to-all-done.3
  75.6 4.6 %all-to-all-start.1 = ((bf16[32,64,128]{2,1,0:T(8,128)(2,1)}), bf16[32,64,128]{2,1,0:T(8,128)(2,1)S(1)}, u32[]{:S(2)}, u32[]{:S(2)}) async-start(bf16[32,64,128]{2,1,0:T(8,128)(2,1)} %shard_map.157), calls=%async_computation.1 | async-start | bytes 1048576 | tf_op jit(solution)/shard_map/all_to_all | solution.py:430
  80.1 1.8 %shard_map.159 = bf16[128,1024]{1,0:T(8,128)(2,1)} custom-call(bf16[2,32,16,128]{3,2,1,0:T(8,128)(2,1)} %bitcast.10.blocks), custom_call_target="tpu_custom_call" | custom-call | bytes 2097152 | tf_op jit(solution)/shard_map/pallas_call | solution.py:345
  81.9 8.4 %all-to-all-done.1.back = bf16[32,64,128]{2,1,0:T(8,128)(2,1)S(1)} async-done(((bf16[32,64,128]{2,1,0:T(8,128)(2,1)}), bf16[32,64,128]{2,1,0:T(8,128)(2,1)S(1)}, u32[]{:S(2)}, u32[]{:S(2)}) %all-to-all-start.1) | async-done | bytes 524320 | tf_op jit(solution)/shard_map/all_to_all | solution.py:430
  90.3 0.0 copy-done.1
  90.3 0.9 %copy-done.5 = bf16[1,128,1024]{2,1,0:T(8,128)(2,1)S(1)} copy-done((bf16[1,128,1024]{2,1,0:T(8,128)(2,1)S(1)}, bf16[1,128,1024]{2,1,0:T(8,128)(2,1)}, u32[]{:S(2)}) %copy-start.5) | copy-done | bytes 262168
  91.2 0.9 %copy-done.7 = bf16[1,128,1024]{2,1,0:T(8,128)(2,1)S(1)} copy-done((bf16[1,128,1024]{2,1,0:T(8,128)(2,1)S(1)}, bf16[1,128,1024]{2,1,0:T(8,128)(2,1)}, u32[]{:S(2)}) %copy-start.7) | copy-done | bytes 262168
  92.2 1.3 %shard_map.158 = (bf16[128,1024]{1,0:T(8,128)(2,1)}, bf16[128,1024]{1,0:T(8,128)(2,1)}, bf16[128,1024]{1,0:T(8,128)(2,1)}, bf16[128,1024]{1,0:T(8,128)(2,1)}) custom-call(bf16[32,64,128]{2,1,0:T(8,128)(2,1)S(1)} %all-to-all-done.1.back, bf16[128,1024]{1,0:T(8,128)(2,1)S(1)} %bitcast.12, bf16[128,1024]{1,0:T(8,128)(2,1)S(1)} %bitcast.14, ...), custom_call_target="tpu_custom_call" | custom-call | bytes 2097152 | tf_op jit(solution)/shard_map/pallas_call | solution.py:345
  (16 shorter events, 0.1 us)
Async XLA Ops:
  0.6 1.0 %copy-start = (bf16[1,128,1024]{2,1,0:T(8,128)(2,1)S(1)}, bf16[1,128,1024]{2,1,0:T(8,128)(2,1)}, u32[]{:S(2)}) copy-start(bf16[1,128,1024]{2,1,0:T(8,128)(2,1)} %param.12) | copy-start | bytes 786436
  1.6 0.9 %copy-start.2 = (bf16[1,128,1024]{2,1,0:T(8,128)(2,1)S(1)}, bf16[1,128,1024]{2,1,0:T(8,128)(2,1)}, u32[]{:S(2)}) copy-start(bf16[1,128,1024]{2,1,0:T(8,128)(2,1)} %param.13) | copy-start | bytes 786436
  2.5 0.9 %copy-start.4 = (bf16[1,128,1024]{2,1,0:T(8,128)(2,1)S(1)}, bf16[1,128,1024]{2,1,0:T(8,128)(2,1)}, u32[]{:S(2)}) copy-start(bf16[1,128,1024]{2,1,0:T(8,128)(2,1)} %param.14) | copy-start | bytes 786436
  3.5 0.9 %copy-start.6 = (bf16[1,128,1024]{2,1,0:T(8,128)(2,1)S(1)}, bf16[1,128,1024]{2,1,0:T(8,128)(2,1)}, u32[]{:S(2)}) copy-start(bf16[1,128,1024]{2,1,0:T(8,128)(2,1)} %param.17) | copy-start | bytes 786436
  4.4 0.9 %copy-start.8 = (bf16[128,1024]{1,0:T(8,128)(2,1)S(1)}, bf16[128,1024]{1,0:T(8,128)(2,1)}, u32[]{:S(2)}) copy-start(bf16[128,1024]{1,0:T(8,128)(2,1)} %taps.1) | copy-start | bytes 786436
  5.4 23.1 %copy-start.9 = (bf16[2,256,256]{2,1,0:T(8,128)(2,1)S(1)}, bf16[2,256,256]{2,1,0:T(8,128)(2,1)}, u32[]{:S(2)}) copy-start(bf16[2,256,256]{2,1,0:T(8,128)(2,1)} %constant.30.clone.back_lane_ref) | copy-start | bytes 786436
  5.4 23.1 %copy-start.11 = (bf16[2,256,256]{2,1,0:T(8,128)(2,1)S(1)}, bf16[2,256,256]{2,1,0:T(8,128)(2,1)}, u32[]{:S(2)}) copy-start(bf16[2,256,256]{2,1,0:T(8,128)(2,1)} %constant.29.clone.lane_ref) | copy-start | bytes 786436
  5.4 23.1 %copy-start.14 = (f32[17,4,128]{2,1,0:T(4,128)S(1)}, f32[17,4,128]{2,1,0:T(4,128)}, u32[]{:S(2)}) copy-start(f32[17,4,128]{2,1,0:T(4,128)} %constant.31.clone.twist_ref) | copy-start | bytes 104452
  28.5 39.3 %copy-start.13 = (f32[17,4,128]{2,1,0:T(4,128)S(1)}, f32[17,4,128]{2,1,0:T(4,128)}, u32[]{:S(2)}) copy-start(f32[17,4,128]{2,1,0:T(4,128)} %constant.32.clone.twist_ref) | copy-start | bytes 104452
  46.5 12.2 %collective-permute-start = (bf16[16,16,128]{2,1,0:T(8,128)(2,1)S(1)}, bf16[16,16,128]{2,1,0:T(8,128)(2,1)S(1)}, u32[]{:S(2)}, u32[]{:S(2)}) collective-permute-start(bf16[16,16,128]{2,1,0:T(8,128)(2,1)S(1)} %reduce_sum.12), channel_id=1, source_target_pairs={{0,256},{256,0},{1,257},{257,1},{2,258},{258,2},{3,259},{259,3},{4... | collective-permute-start | bytes 196616 | tf_op jit(solution)/shard_map/ppermute | solution.py:438
  59.5 16.1 %all-to-all-start.3 = ((bf16[4,16,16,128]{3,2,1,0:T(8,128)(2,1)}), bf16[4,16,16,128]{3,2,1,0:T(8,128)(2,1)}, u32[]{:S(2)}, u32[]{:S(2)}) async-start(bf16[4,16,16,128]{3,2,1,0:T(8,128)(2,1)} %broadcast_in_dim.29), calls=%async_computation.3 | async-start | bytes 524288 | tf_op jit(solution)/shard_map/all_to_all | solution.py:430
  67.9 1.0 %copy-start.10 = (bf16[2,256,256]{2,1,0:T(8,128)(2,1)S(1)}, bf16[2,256,256]{2,1,0:T(8,128)(2,1)}, u32[]{:S(2)}) copy-start(bf16[2,256,256]{2,1,0:T(8,128)(2,1)} %constant.30.clone.back_lane_ref) | copy-start | bytes 786436
  68.8 0.9 %copy-start.12 = (bf16[2,256,256]{2,1,0:T(8,128)(2,1)S(1)}, bf16[2,256,256]{2,1,0:T(8,128)(2,1)}, u32[]{:S(2)}) copy-start(bf16[2,256,256]{2,1,0:T(8,128)(2,1)} %constant.29.clone.lane_ref) | copy-start | bytes 786436
  69.8 20.5 %copy-start.1 = (bf16[1,128,1024]{2,1,0:T(8,128)(2,1)S(1)}, bf16[1,128,1024]{2,1,0:T(8,128)(2,1)}, u32[]{:S(2)}) copy-start(bf16[1,128,1024]{2,1,0:T(8,128)(2,1)} %param.12) | copy-start | bytes 786436
  69.8 20.5 %copy-start.3 = (bf16[1,128,1024]{2,1,0:T(8,128)(2,1)S(1)}, bf16[1,128,1024]{2,1,0:T(8,128)(2,1)}, u32[]{:S(2)}) copy-start(bf16[1,128,1024]{2,1,0:T(8,128)(2,1)} %param.13) | copy-start | bytes 786436
  75.6 14.7 %all-to-all-start.1 = ((bf16[32,64,128]{2,1,0:T(8,128)(2,1)}), bf16[32,64,128]{2,1,0:T(8,128)(2,1)S(1)}, u32[]{:S(2)}, u32[]{:S(2)}) async-start(bf16[32,64,128]{2,1,0:T(8,128)(2,1)} %shard_map.157), calls=%async_computation.1 | async-start | bytes 1048576 | tf_op jit(solution)/shard_map/all_to_all | solution.py:430
  90.3 1.0 %copy-start.5 = (bf16[1,128,1024]{2,1,0:T(8,128)(2,1)S(1)}, bf16[1,128,1024]{2,1,0:T(8,128)(2,1)}, u32[]{:S(2)}) copy-start(bf16[1,128,1024]{2,1,0:T(8,128)(2,1)} %param.14) | copy-start | bytes 786436
  91.2 0.9 %copy-start.7 = (bf16[1,128,1024]{2,1,0:T(8,128)(2,1)S(1)}, bf16[1,128,1024]{2,1,0:T(8,128)(2,1)}, u32[]{:S(2)}) copy-start(bf16[1,128,1024]{2,1,0:T(8,128)(2,1)} %param.17) | copy-start | bytes 786436

commit v3 on v2

--- a/solution.py
+++ b/solution.py
@@ -247,7 +247,7 @@
 
 def taps_grad_kernel(signals, lane_ref, back_lane_ref, twist_ref, spec_ref, out, high, low, back):
     batch = signals.shape[0] // ROWS
-    chans = out.shape[0] * CHUNK
+    chans = out.shape[1]
     total = HALF * chans
 
     def forward(i, carry):
@@ -269,13 +269,10 @@
     )
     lane_transform(high, low, back_lane_ref, back, total, total // 2)
 
-    def inverse(i, carry):
-        rows = parts_to_rows(back, twist_ref, chans, i * CHUNK, 0)
+    for first in range(0, chans, CHUNK):
+        rows = parts_to_rows(back, twist_ref, chans, first, 0)
         for r in range(ROWS):
-            out[i, r] = rows[r].astype(BF16)
-        return carry
-
-    lax.fori_loop(0, chans // CHUNK, inverse, 0)
+            out[r, pl.ds(first, CHUNK), :] = rows[r].astype(BF16)
 
 
 def state_kernel(signals, spec_ref, skip_ref, lane_ref, back_lane_ref, twist_ref, out, high, low, taps_spec, back):
@@ -315,29 +312,23 @@
     lax.fori_loop(0, chans // CHUNK, inverse, 0)
 
 
-def output_kernel(back, query, key, value, grad, mixed_out, grad_query, grad_key, grad_value):
-    own = back.shape[1] // 2
+def output_kernel(back, query, key, value, grad, mixed_out, grad_query, grad_key, grad_value, grad_filter):
+    own = back.shape[1] // 3
     pieces = LANES // own
     for tile in range(back.shape[0] // pieces):
         cols = pl.ds(tile * LANES, LANES)
-        state, dmixed = (
+        state, dmixed, term = (
             jnp.concatenate(
                 [back[tile * pieces + i, pl.ds(which * own, own), :] for i in range(pieces)], axis=0
-            ).T.astype(F32)
-            for which in range(2)
+            ).T
+            for which in range(3)
         )
+        state, dmixed = state.astype(F32), dmixed.astype(F32)
         mixed_out[:, cols] = (query[:, cols].astype(F32) * state).astype(BF16)
         grad_query[:, cols] = (grad[:, cols].astype(F32) * state).astype(BF16)
         grad_key[:, cols] = (dmixed * value[:, cols].astype(F32)).astype(BF16)
         grad_value[:, cols] = (dmixed * key[:, cols].astype(F32)).astype(BF16)
-
-
-def filter_kernel(blocks, out):
-    shares, owners, depth = blocks.shape[:3]
-    pieces = LANES // (shares * depth)
-    for tile in range(owners // pieces):
-        rows = [blocks[i, tile * pieces + s] for s in range(pieces) for i in range(shares)]
-        out[:, pl.ds(tile * LANES, LANES)] = jnp.concatenate(rows, axis=0).T
+        grad_filter[:, cols] = term
 
 
 def call(kernel, shapes, args, scratch=(), in_hbm=False, out_hbm=False, flops=0, moved=2 << 20, limit=24):
@@ -350,7 +341,7 @@
         scratch_shapes=list(scratch),
         compiler_params=pltpu.CompilerParams(vmem_limit_bytes=limit << 20),
         cost_estimate=pl.CostEstimate(flops=flops, bytes_accessed=moved, transcendentals=0),
-    )(*args)
+    )(*[pltpu.with_memory_space_constraint(a, pltpu.HBM) for a in args] if in_hbm else args)
 
 
 def gate(query, key, value, grad, taps, peers):
@@ -382,11 +373,11 @@
         taps_grad_kernel,
         (
             shape((2 * batch * total, 2 * LANES), F32),
-            shape((own // CHUNK, ROWS, CHUNK, LANES), BF16),
+            shape((ROWS, own, LANES), BF16),
         ),
         (signals, forward_lane, inverse_lane, twist_tables(factor)),
         (parts, parts, pltpu.VMEM((total, 2 * LANES), F32)),
-        flops=10**9,
+        flops=5 * 10**9,
     )
 
 
@@ -405,13 +396,13 @@
             pltpu.VMEM((total, 2 * LANES), F32),
             pltpu.VMEM((2 * batch * total, 2 * LANES), F32),
         ),
-        flops=10**9,
+        flops=5 * 10**9,
     )
 
 
 def outputs(back, query, key, value, grad):
     block = jax.ShapeDtypeStruct(query.shape, BF16)
-    return call(output_kernel, (block,) * 4, (back, query, key, value, grad))
+    return call(output_kernel, (block,) * 5, (back, query, key, value, grad))
 
 
 def on_device(query_in, key_in, value_in, filter_taps, skip_gain, grad_out):
@@ -430,22 +421,23 @@
         return lax.all_to_all(values, axes, split_axis=0, concat_axis=0, tiled=True)
 
     signals = swap(gate(query, key, value, grad, filter_taps, peers), ("pl", "seq"))
-    spectra, taps_term = taps_grad(signals, own, factor)
-
-    groups = own // CHUNK
-    terms = swap(taps_term.reshape(groups * seq_count, CHUNK, LANES), ("dm", "seq"))
-    part = terms.reshape(groups, seq_count, CHUNK, LANES).astype(F32).sum(0).astype(BF16)
-    other = lax.ppermute(part, "dh", [(0, 1), (1, 0)])
-    summed = (part.astype(F32) + other.astype(F32)).astype(BF16)
-    copies = jnp.broadcast_to(summed[None], (groups * pair,) + summed.shape)
-    gathered = swap(copies, ("dm", "pl")).reshape(groups, peers, CHUNK, LANES)
-    grad_filter = call(
-        filter_kernel, jax.ShapeDtypeStruct((rows_dev, chan_dev), BF16), (gathered,)
-    )
-
-    back = swap(states(signals, spectra, skip_own, own), ("pl", "seq"))
+    spectra, term = taps_grad(signals, own, factor)
+
+    def exchange(values, axis):
+        return lax.ppermute(values, axis, [(0, 1), (1, 0)])
+
+    def plus(a, b):
+        return (a.astype(F32) + b.astype(F32)).astype(BF16)
+
+    taken = exchange(term, "dm")
+    results = states(signals, spectra, skip_own, own)
+    taken, results = lax.optimization_barrier((taken, results))
+    term = plus(term, taken)
+    term = plus(term, exchange(term, "dh"))
+    copies = jnp.broadcast_to(term[None], (pair,) + term.shape).reshape((peers,) + term.shape[1:])
+    back = swap(jnp.concatenate([results, copies], axis=1), ("pl", "seq"))
     outs = outputs(back, query, key, value, grad)
-    return tuple(out[None] for out in outs) + (grad_filter,)
+    return tuple(out[None] for out in outs[:4]) + (outs[4],)
 
 
 def solution(mesh):

time: 94.2 us -> 77.7 us (0.82)
  the two profiles are of different devices: /device:TPU:64 before, /device:TPU:2 now
where the time goes in v3:
time: 77.7 us; the launch traced here: 77.4 us
  starting transfers between devices  23.7 us (31%)
  waiting for transfers between devices  20.5 us (26%)
  blocking collectives  17.9 us (23%)
  Pallas kernels  13.4 us (17%)
  local copies, waits for them, and re-layouts  0.92 us (1%)
  between operations  0.79 us (1%)
    all_to_all x1, blocking collectives, swap(): return lax.all_to_all(values, axes, split_axis=0, concat_axis=0, tiled=True)  17.9 us
    ppermute x2, starting transfers between devices, exchange(): return lax.ppermute(values, axis, [(0, 1), (1, 0)])  14.3 us
    pallas_call x4, Pallas kernels, call(): pl.pallas_call(kernel, out_shape=shapes, in_specs=[place(in_hbm)] * len(a...  13.4 us
    all_to_all x1, waiting for transfers between devices, swap(): return lax.all_to_all(values, axes, split_axis=0, concat_axis=0, tiled=True)  10.3 us
    ppermute x2, waiting for transfers between devices, exchange(): return lax.ppermute(values, axis, [(0, 1), (1, 0)])  10.2 us
    all_to_all x1, starting transfers between devices, swap(): return lax.all_to_all(values, axes, split_axis=0, concat_axis=0, tiled=True)  9.47 us
  transfers between devices with their start and end apart: 3, of which 2 were waited for; matrix products, arithmetic and copies ran while one was open for 1% of the time, Pallas kernels for 6%

profile of v3, /device:TPU:2, one launch (start us, length us, event | category | flops | bytes accessed | tf_op | source)
XLA Modules:
  0.0 77.4 jit_solution(5400817851461924988)
XLA Ops:
  0.6 0.0 copy-start.4
  0.6 0.0 copy-start.5
  0.7 0.0 copy-start.7
  0.7 2.4 %shard_map.155 = bf16[32,80,128]{2,1,0:T(8,128)(2,1)} custom-call(bf16[128,1024]{1,0:T(8,128)(2,1)} %bitcast.9, bf16[128,1024]{1,0:T(8,128)(2,1)} %bitcast.11, bf16[128,1024]{1,0:T(8,128)(2,1)} %bitcast.13, bf16[128,1024]{1,0:T(8,128)(2,1)} %bitcast.15, bf16[128,1024]{1,0:T(8,128)(2,1)} %taps.1), custom_call_target="tpu_custom_call" | custom-call | bytes 2097152 | tf_op jit(solution)/shard_map/pallas_call | solution.py:336
  3.1 9.5 %all-to-all-start = ((bf16[32,80,128]{2,1,0:T(8,128)(2,1)}), bf16[32,80,128]{2,1,0:T(8,128)(2,1)S(1)}, u32[]{:S(2)}, u32[]{:S(2)}) async-start(bf16[32,80,128]{2,1,0:T(8,128)(2,1)} %shard_map.155), calls=%async_computation | async-start | bytes 1310720 | tf_op jit(solution)/shard_map/all_to_all | solution.py:421
  12.6 0.8 dynamic_slice.3
  13.3 0.0 copy-start.6
  13.3 10.3 %all-to-all-done.signals = bf16[32,80,128]{2,1,0:T(8,128)(2,1)S(1)} async-done(((bf16[32,80,128]{2,1,0:T(8,128)(2,1)}), bf16[32,80,128]{2,1,0:T(8,128)(2,1)S(1)}, u32[]{:S(2)}, u32[]{:S(2)}) %all-to-all-start) | async-done | bytes 655392 | tf_op jit(solution)/shard_map/all_to_all | solution.py:421
  23.6 0.0 copy-done.4
  23.6 0.0 copy-done.5
  23.6 0.0 copy-done.7
  23.7 4.5 %shard_map.156 = (f32[2176,256]{1,0:T(8,128)S(1)}, bf16[16,32,128]{2,1,0:T(8,128)(2,1)S(1)}) custom-call(bf16[32,80,128]{2,1,0:T(8,128)(2,1)S(1)} %all-to-all-done.signals, bf16[2,256,256]{2,1,0:T(8,128)(2,1)S(1)} %copy-done.5, bf16[2,256,256]{2,1,0:T(8,128)(2,1)S(1)} %copy-done.4, f32[17,4,128]{2,1,0:T(4,128)S(1)} %copy-done.7), custom_call_target="tpu_custom_call" | custom-call | flops 5000000000 | bytes 2097152 | tf_op jit(solution)/shard_map/pallas_call | solution.py:336
  28.2 5.2 %collective-permute-start = (bf16[16,32,128]{2,1,0:T(8,128)(2,1)S(1)}, bf16[16,32,128]{2,1,0:T(8,128)(2,1)S(1)}, u32[]{:S(2)}, u32[]{:S(2)}) collective-permute-start(bf16[16,32,128]{2,1,0:T(8,128)(2,1)S(1)} %get-tuple-element.14), channel_id=1, source_target_pairs={{0,128},{128,0},{1,129},{129,1},{2,130},{130,2},{3,131},{131,3},{4... | collective-permute-start | bytes 393224 | tf_op jit(solution)/shard_map/ppermute | solution.py:427
  33.4 0.1 broadcast_in_dim.24.skip_ref
  33.4 0.0 copy-done.6
  33.4 5.0 %shard_map.157 = bf16[32,64,128]{2,1,0:T(8,128)(2,1)S(1)} custom-call(bf16[32,80,128]{2,1,0:T(8,128)(2,1)S(1)} %all-to-all-done.signals, f32[2176,256]{1,0:T(8,128)S(1)} %get-tuple-element.15.spec_ref, f32[32,128]{1,0:T(8,128)S(1)} %broadcast_in_dim.24.skip_ref, bf16[2,256,256]{2,1,0:T(8,128)(2,1)S(1)} %copy-done.5, bf16[2,256,256]{2,1,0:T(8,128)(2,1)S(1)} %copy-done.4, ...), custom_call_target="tpu_custom_call" | custom-call | flops 5000000000 | bytes 2097152 | tf_op jit(solution)/shard_map/pallas_call | solution.py:336
  38.4 0.0 collective-permute-done
  38.5 9.1 %collective-permute-start.1 = (bf16[16,32,128]{2,1,0:T(8,128)(2,1)S(1)}, bf16[16,32,128]{2,1,0:T(8,128)(2,1)S(1)}, u32[]{:S(2)}, u32[]{:S(2)}) collective-permute-start(bf16[16,32,128]{2,1,0:T(8,128)(2,1)S(1)} %add_convert_fusion.1), channel_id=1, source_target_pairs={{0,256},{256,0},{1,257},{257,1},{2,258},{258,2},{3,259},{259,3},{4... | collective-permute-start | bytes 393224 | tf_op jit(solution)/shard_map/ppermute | solution.py:427
  47.6 10.2 %collective-permute-done.1 = bf16[16,32,128]{2,1,0:T(8,128)(2,1)S(1)} collective-permute-done((bf16[16,32,128]{2,1,0:T(8,128)(2,1)S(1)}, bf16[16,32,128]{2,1,0:T(8,128)(2,1)S(1)}, u32[]{:S(2)}, u32[]{:S(2)}) %collective-permute-start.1) | collective-permute-done | bytes 131104 | tf_op jit(solution)/shard_map/ppermute | solution.py:427
  57.8 0.0 copy-start
  57.9 0.0 copy-start.1
  57.9 0.0 copy-start.2
  57.9 0.0 copy-start.3
  57.9 0.1 pad_maximum_fusion
  58.0 17.9 %all_to_all.10.back = bf16[32,96,128]{2,1,0:T(8,128)(2,1)S(1)} all-to-all(bf16[32,96,128]{2,1,0:T(8,128)(2,1)S(1)} %pad_maximum_fusion), channel_id=1, replica_groups=mesh['dh'=2,'dm'=2,'pl'=2,'chan'=4,'seq'=16] {'pl','seq'}, dimensions={0} | all-to-all | bytes 1572864 | tf_op jit(solution)/shard_map/all_to_all | solution.py:421
  75.9 0.0 copy-done
  75.9 0.0 copy-done.1
  75.9 0.0 copy-done.2
  75.9 0.0 copy-done.3
  75.9 1.5 %shard_map.158 = (bf16[128,1024]{1,0:T(8,128)(2,1)}, bf16[128,1024]{1,0:T(8,128)(2,1)}, bf16[128,1024]{1,0:T(8,128)(2,1)}, bf16[128,1024]{1,0:T(8,128)(2,1)}, bf16[128,1024]{1,0:T(8,128)(2,1)}) custom-call(bf16[32,96,128]{2,1,0:T(8,128)(2,1)S(1)} %all_to_all.10.back, bf16[128,1024]{1,0:T(8,128)(2,1)S(1)} %bitcast.10, bf16[128,1024]{1,0:T(8,128)(2,1)S(1)} %bitcast.12, ...), custom_call_target="tpu_custom_call" | custom-call | bytes 2097152 | tf_op jit(solution)/shard_map/pallas_call | solution.py:336
  (3 shorter events, 0.1 us)
Async XLA Ops:
  0.6 23.0 %copy-start.4 = (bf16[2,256,256]{2,1,0:T(8,128)(2,1)S(1)}, bf16[2,256,256]{2,1,0:T(8,128)(2,1)}, u32[]{:S(2)}) copy-start(bf16[2,256,256]{2,1,0:T(8,128)(2,1)} %constant.27.clone.back_lane_ref) | copy-start | bytes 786436
  0.6 23.0 %copy-start.5 = (bf16[2,256,256]{2,1,0:T(8,128)(2,1)S(1)}, bf16[2,256,256]{2,1,0:T(8,128)(2,1)}, u32[]{:S(2)}) copy-start(bf16[2,256,256]{2,1,0:T(8,128)(2,1)} %constant.26.clone.lane_ref) | copy-start | bytes 786436
  0.7 23.0 %copy-start.7 = (f32[17,4,128]{2,1,0:T(4,128)S(1)}, f32[17,4,128]{2,1,0:T(4,128)}, u32[]{:S(2)}) copy-start(f32[17,4,128]{2,1,0:T(4,128)} %constant.28.clone.twist_ref) | copy-start | bytes 104452
  3.1 20.6 %all-to-all-start = ((bf16[32,80,128]{2,1,0:T(8,128)(2,1)}), bf16[32,80,128]{2,1,0:T(8,128)(2,1)S(1)}, u32[]{:S(2)}, u32[]{:S(2)}) async-start(bf16[32,80,128]{2,1,0:T(8,128)(2,1)} %shard_map.155), calls=%async_computation | async-start | bytes 1310720 | tf_op jit(solution)/shard_map/all_to_all | solution.py:421
  13.3 20.1 %copy-start.6 = (f32[17,4,128]{2,1,0:T(4,128)S(1)}, f32[17,4,128]{2,1,0:T(4,128)}, u32[]{:S(2)}) copy-start(f32[17,4,128]{2,1,0:T(4,128)} %constant.29.clone.twist_ref) | copy-start | bytes 104452
  28.2 10.3 %collective-permute-start = (bf16[16,32,128]{2,1,0:T(8,128)(2,1)S(1)}, bf16[16,32,128]{2,1,0:T(8,128)(2,1)S(1)}, u32[]{:S(2)}, u32[]{:S(2)}) collective-permute-start(bf16[16,32,128]{2,1,0:T(8,128)(2,1)S(1)} %get-tuple-element.14), channel_id=1, source_target_pairs={{0,128},{128,0},{1,129},{129,1},{2,130},{130,2},{3,131},{131,3},{4... | collective-permute-start | bytes 393224 | tf_op jit(solution)/shard_map/ppermute | solution.py:427
  38.5 19.3 %collective-permute-start.1 = (bf16[16,32,128]{2,1,0:T(8,128)(2,1)S(1)}, bf16[16,32,128]{2,1,0:T(8,128)(2,1)S(1)}, u32[]{:S(2)}, u32[]{:S(2)}) collective-permute-start(bf16[16,32,128]{2,1,0:T(8,128)(2,1)S(1)} %add_convert_fusion.1), channel_id=1, source_target_pairs={{0,256},{256,0},{1,257},{257,1},{2,258},{258,2},{3,259},{259,3},{4... | collective-permute-start | bytes 393224 | tf_op jit(solution)/shard_map/ppermute | solution.py:427
  57.8 18.0 %copy-start = (bf16[1,128,1024]{2,1,0:T(8,128)(2,1)S(1)}, bf16[1,128,1024]{2,1,0:T(8,128)(2,1)}, u32[]{:S(2)}) copy-start(bf16[1,128,1024]{2,1,0:T(8,128)(2,1)} %param.12) | copy-start | bytes 786436
  57.9 18.0 %copy-start.1 = (bf16[1,128,1024]{2,1,0:T(8,128)(2,1)S(1)}, bf16[1,128,1024]{2,1,0:T(8,128)(2,1)}, u32[]{:S(2)}) copy-start(bf16[1,128,1024]{2,1,0:T(8,128)(2,1)} %param.13) | copy-start | bytes 786436
  57.9 18.0 %copy-start.2 = (bf16[1,128,1024]{2,1,0:T(8,128)(2,1)S(1)}, bf16[1,128,1024]{2,1,0:T(8,128)(2,1)}, u32[]{:S(2)}) copy-start(bf16[1,128,1024]{2,1,0:T(8,128)(2,1)} %param.14) | copy-start | bytes 786436
  57.9 18.0 %copy-start.3 = (bf16[1,128,1024]{2,1,0:T(8,128)(2,1)S(1)}, bf16[1,128,1024]{2,1,0:T(8,128)(2,1)}, u32[]{:S(2)}) copy-start(bf16[1,128,1024]{2,1,0:T(8,128)(2,1)} %param.17) | copy-start | bytes 786436

commit v4 on v3

v4 whole, which is shorter than its diff:
```python
import math

import jax
import jax.numpy as jnp
import numpy as np
from jax import lax
from jax.experimental import pallas as pl
from jax.experimental.pallas import tpu as pltpu
from jax.sharding import Mesh
from jax.sharding import PartitionSpec as P

F32 = jnp.float32
BF16 = jnp.bfloat16
LANES = 128
ROWS = 16
FREQS = 2 * ROWS
HALF = ROWS + 1
CHUNK = 16
GROUPS = 2


def unit(numer, denom):
    angle = 2.0 * math.pi * numer / denom
    return (math.cos(angle), math.sin(angle))


def times_unit(value, numer, denom):
    re, im = value
    numer = numer % denom
    if 4 * numer % denom == 0:
        return ((re, im), (-im, re), (-re, -im), (im, -re))[4 * numer // denom]
    if 8 * numer % denom == 0:
        root = math.sqrt(0.5)
        summed, apart = (re + im) * root, (re - im) * root
        return {1: (apart, summed), 3: (-summed, apart), 5: (-apart, -summed), 7: (summed, -apart)}[
            8 * numer // denom
        ]
    cos, sin = unit(numer, denom)
    return (re * cos - im * sin, re * sin + im * cos)


def add(a, b):
    return (a[0] + b[0], a[1] + b[1])


def sub(a, b):
    return (a[0] - b[0], a[1] - b[1])


def conj(a):
    return (a[0], -a[1])


def complex_dft(values, sign):
    count = len(values)
    if count == 1:
        return list(values)
    even = complex_dft(values[0::2], sign)
    odd = complex_dft(values[1::2], sign)
    turned = [times_unit(v, sign * j, count) for j, v in enumerate(odd)]
    return [add(e, t) for e, t in zip(even, turned)] + [sub(e, t) for e, t in zip(even, turned)]


def odd_freqs(first, second, count):
    turned = [
        times_unit((a, -b), -r, count) for r, (a, b) in enumerate(zip(first, second))
    ]
    return {4 * j + 1: v for j, v in enumerate(complex_dft(turned, -1))}


def real_dft(values, count):
    half, quarter = count // 2, count // 4
    if count == 2:
        return [(values[0] + values[1], None), (values[0] - values[1], None)]
    if len(values) == half:
        folded, apart = values, values
    else:
        folded = [values[r] + values[r + half] for r in range(half)]
        apart = [values[r] - values[r + half] for r in range(half)]
    out = [None] * (half + 1)
    out[0::2] = real_dft(folded, half)
    for freq, value in odd_freqs(apart[:quarter], apart[quarter:], count).items():
        if freq <= half:
            out[freq] = value
        else:
            out[count - freq] = conj(value)
    return out


def real_inverse(freqs, count, keep_half):
    half, quarter = count // 2, count // 4
    if count == 2:
        first, last = freqs[0][0], freqs[1][0]
        return [first + last, first - last]
    even = real_inverse(freqs[0::2], half, False)
    picked = [
        freqs[4 * j + 1] if 4 * j + 1 <= half else conj(freqs[count - 4 * j - 1])
        for j in range(quarter)
    ]
    turned = [times_unit(v, r, count) for r, v in enumerate(complex_dft(picked, 1))]
    odd = [re for re, _ in turned] + [-im for _, im in turned]
    low = [e + o for e, o in zip(even, odd)]
    if keep_half:
        return low
    return low + [e - o for e, o in zip(even, odd)]


def split_table(table):
    high = table.astype(np.float32).astype(BF16)
    low = (table - high.astype(np.float64)).astype(BF16)
    return np.stack([high, low])


def lane_tables():
    idx = np.arange(LANES)
    angle = 2.0 * np.pi / LANES * (idx[:, None] * idx[None, :] % LANES)
    cos, sin = np.cos(angle), np.sin(angle)
    forward = np.block([[cos, -sin], [sin, cos]])
    inverse = np.block([[cos, sin], [-sin, cos]])
    return split_table(forward), split_table(inverse)


def twist_tables(factor):
    padded = FREQS * LANES
    angle = 2.0 * np.pi / padded * (np.arange(HALF)[:, None] * np.arange(LANES)[None, :])
    weight = np.full((HALF, 1), 2.0)
    weight[0] = weight[-1] = 1.0
    weight = weight / padded * factor
    cos, sin = np.cos(angle), np.sin(angle)
    return np.stack([cos, sin, cos * weight, sin * weight], axis=1).astype(np.float32)


def split_value(value):
    high = value.astype(BF16)
    return high, (value - high.astype(F32)).astype(BF16)


def start_copies(pairs, sems):
    copies = [pltpu.make_async_copy(a, b, sems.at[i]) for i, (a, b) in enumerate(pairs)]
    for copy in copies:
        copy.start()
    return copies


def gate_kernel(query, key, value, grad, taps, out, *scratch):
    held, sems = scratch[:5], scratch[5]
    key_v, value_v, grad_v, query_v, taps_v = held
    peers = out.shape[0]
    own = taps.shape[1] // peers
    share = out.shape[1] - 2 * own
    pieces = LANES // own
    width = taps.shape[1] // GROUPS
    begin = lax.axis_index("pl") * share
    arrivals = []
    for group in range(GROUPS):
        cols = pl.ds(group * width, width)
        pairs = [(a.at[:, cols], b.at[:, cols]) for a, b in zip((key, value, grad, query, taps), held)]
        arrivals.append(start_copies(pairs, sems.at[group]))
    for group, copies in enumerate(arrivals):
        for copy in copies:
            copy.wait()
        tiles = width // LANES
        for tile in range(group * tiles, (group + 1) * tiles):
            cols = pl.ds(tile * LANES, LANES)
            mixed = (key_v[:, cols].astype(F32) * value_v[:, cols].astype(F32)).astype(BF16)
            state = (grad_v[:, cols].astype(F32) * query_v[:, cols].astype(F32)).astype(BF16)
            for place, block in enumerate((mixed, state)):
                turned = block.T
                for i in range(pieces):
                    rows = pl.ds(place * own, own)
                    out[tile * pieces + i, rows, :] = turned[i * own : (i + 1) * own]
            turned = taps_v[:, cols].T
            for i in range(pieces):
                low = turned[i * own : i * own + share]
                high = turned[i * own + share : (i + 1) * own]
                rows = pl.ds(2 * own, share)
                out[tile * pieces + i, rows, :] = jnp.where(begin == 0, low, high)


def spectrum(get_row, twist_ref, lane_ref):
    freqs = real_dft([get_row(r) for r in range(ROWS)], FREQS)
    rows = []
    for k, (re, im) in enumerate(freqs):
        cos, sin = twist_ref[k, 0:1, :], twist_ref[k, 1:2, :]
        if im is None:
            rows.append(jnp.concatenate([re * cos, -re * sin], axis=1))
        else:
            rows.append(jnp.concatenate([re * cos + im * sin, im * cos - re * sin], axis=1))
    return lane_product(jnp.concatenate(rows, axis=0), lane_ref)


def lane_product(value, table_ref):
    high, low = split_value(value)
    out = jnp.dot(high, table_ref[0], preferred_element_type=F32)
    out += jnp.dot(low, table_ref[0], preferred_element_type=F32)
    return out + jnp.dot(high, table_ref[1], preferred_element_type=F32)


def conj_product(first, second):
    are, aim = first[:, :LANES], first[:, LANES:]
    bre, bim = second[:, :LANES], second[:, LANES:]
    return jnp.concatenate([are * bre + aim * bim, are * bim - aim * bre], axis=1)


def plain_product(first, second):
    are, aim = first[:, :LANES], first[:, LANES:]
    bre, bim = second[:, :LANES], second[:, LANES:]
    return jnp.concatenate([are * bre - aim * bim, are * bim + aim * bre], axis=1)


def signal_rows(spec, twist_ref, back_lane_ref):
    back = lane_product(spec, back_lane_ref)
    freqs = []
    for k in range(HALF):
        re = back[k * CHUNK : (k + 1) * CHUNK, :LANES]
        im = back[k * CHUNK : (k + 1) * CHUNK, LANES:]
        cos, sin = twist_ref[k, 2:3, :], twist_ref[k, 3:4, :]
        if k in (0, ROWS):
            freqs.append((re * cos - im * sin, None))
        else:
            freqs.append((re * cos - im * sin, im * cos + re * sin))
    return real_inverse(freqs, FREQS, True)


def taps_grad_kernel(signals, lane_ref, back_lane_ref, twist_ref, spec_ref, out):
    batch = signals.shape[0] // ROWS
    chans = out.shape[1]
    total = HALF * chans

    def chunk(first):
        rows = {}
        for which in range(2):
            place = pl.ds(which * chans + first, CHUNK)
            for b in range(batch):
                rows[which, b] = spectrum(
                    lambda r: signals[b * ROWS + r, place, :].astype(F32), twist_ref, lane_ref
                )
                base = (which * batch + b) * total
                for k in range(HALF):
                    spec_ref[pl.ds(base + k * chans + first, CHUNK), :] = rows[which, b][
                        k * CHUNK : (k + 1) * CHUNK
                    ]
        product = conj_product(rows[0, 0], rows[1, 0])
        for b in range(1, batch):
            product = product + conj_product(rows[0, b], rows[1, b])
        for r, row in enumerate(signal_rows(product, twist_ref, back_lane_ref)):
            out[r, pl.ds(first, CHUNK), :] = row.astype(BF16)

    for first in range(0, chans, CHUNK):
        chunk(first)


def state_kernel(signals, spec_ref, gain_ref, lane_ref, back_lane_ref, twist_ref, out, skip_ref):
    batch = signals.shape[0] // ROWS
    chans = out.shape[1] // 2
    share = signals.shape[1] - 2 * chans
    total = HALF * chans
    place = lax.axis_index("pl") * lax.axis_size("seq") + lax.axis_index("seq")
    pieces = LANES // chans
    gains = jnp.broadcast_to(gain_ref[pl.ds(place // pieces, 1), :], (LANES, LANES))
    skip_ref[...] = gains.T
    begin = pl.multiple_of(place % pieces * chans, chans)
    for first in range(0, chans, CHUNK):
        source, place = divmod(first, share)
        taps = spectrum(
            lambda r: signals[source * ROWS + r, pl.ds(2 * chans + place, CHUNK), :].astype(F32),
            twist_ref,
            lane_ref,
        )
        skip = skip_ref[pl.ds(begin + first, CHUNK), :]
        for which, product in enumerate((plain_product, conj_product)):
            place = pl.ds(which * chans + first, CHUNK)
            for b in range(batch):
                base = (which * batch + b) * total + first
                other = [spec_ref[pl.ds(base + k * chans, CHUNK), :] for k in range(HALF)]
                spec = product(taps, jnp.concatenate(other, axis=0))
                for r, row in enumerate(signal_rows(spec, twist_ref, back_lane_ref)):
                    own = signals[b * ROWS + r, place, :].astype(F32)
                    out[b * ROWS + r, place, :] = (row + skip * own).astype(BF16)


def output_kernel(back, query, key, value, grad, *refs):
    outs, held, sems = refs[:5], refs[5:10], refs[10]
    own = back.shape[1] // 3
    pieces = LANES // own
    width = query.shape[1] // GROUPS
    sent = []
    for group in range(GROUPS):
        for tile in range(group * width // LANES, (group + 1) * width // LANES):
            cols = pl.ds(tile * LANES, LANES)
            state, dmixed, term = (
                jnp.concatenate(
                    [back[tile * pieces + i, pl.ds(which * own, own), :] for i in range(pieces)],
                    axis=0,
                ).T
                for which in range(3)
            )
            state, dmixed = state.astype(F32), dmixed.astype(F32)
            held[0][:, cols] = (query[:, cols].astype(F32) * state).astype(BF16)
            held[1][:, cols] = (grad[:, cols].astype(F32) * state).astype(BF16)
            held[2][:, cols] = (dmixed * value[:, cols].astype(F32)).astype(BF16)
            held[3][:, cols] = (dmixed * key[:, cols].astype(F32)).astype(BF16)
            held[4][:, cols] = term
        cols = pl.ds(group * width, width)
        pairs = [(a.at[:, cols], b.at[:, cols]) for a, b in zip(held, outs)]
        sent += start_copies(pairs, sems.at[group])
    for copy in sent:
        copy.wait()


def call(kernel, shapes, args, scratch=(), in_hbm=False, out_hbm=False, flops=0, moved=2 << 20, limit=24):
    place = lambda hbm: pl.BlockSpec(memory_space=pltpu.HBM if hbm else pltpu.VMEM)
    return pl.pallas_call(
        kernel,
        out_shape=shapes,
        in_specs=[place(in_hbm)] * len(args),
        out_specs=jax.tree.map(lambda _: place(out_hbm), shapes),
        scratch_shapes=list(scratch),
        compiler_params=pltpu.CompilerParams(vmem_limit_bytes=limit << 20),
        cost_estimate=pl.CostEstimate(flops=flops, bytes_accessed=moved, transcendentals=0),
    )(*[pltpu.with_memory_space_constraint(a, pltpu.HBM) for a in args] if in_hbm else args)


def gate(query, key, value, grad, taps, peers):
    rows_dev, chan_dev = query.shape
    own = chan_dev // peers
    out_shape = (peers, 2 * own + own // 2, rows_dev)
    return call(
        gate_kernel,
        jax.ShapeDtypeStruct(out_shape, BF16),
        (query, key, value, grad, taps),
        [pltpu.VMEM((rows_dev, chan_dev), BF16)] * 5
        + [
            pltpu.SemaphoreType.DMA((GROUPS, 5)),
        ],
        in_hbm=True,
    )


def taps_grad(signals, own, factor):
    total = HALF * own
    batch = signals.shape[0] // ROWS
    forward_lane, inverse_lane = lane_tables()
    shape = jax.ShapeDtypeStruct
    return call(
        taps_grad_kernel,
        (
            shape((2 * batch * total, 2 * LANES), F32),
            shape((ROWS, own, LANES), BF16),
        ),
        (signals, forward_lane, inverse_lane, twist_tables(factor)),
        flops=5 * 10**9,
    )


def states(signals, spectra, skip_gain, own):
    total = HALF * own
    batch = signals.shape[0] // ROWS
    forward_lane, inverse_lane = lane_tables()
    return call(
        state_kernel,
        jax.ShapeDtypeStruct((batch * ROWS, 2 * own, LANES), BF16),
        (signals, spectra, skip_gain.reshape(-1, LANES), forward_lane, inverse_lane, twist_tables(1.0)),
        (pltpu.VMEM((LANES, LANES), F32),),
        flops=5 * 10**9,
    )


def outputs(back, query, key, value, grad):
    block = jax.ShapeDtypeStruct(query.shape, BF16)
    return call(
        output_kernel,
        (block,) * 5,
        (back, query, key, value, grad),
        [pltpu.VMEM(query.shape, BF16)] * 5 + [pltpu.SemaphoreType.DMA((GROUPS, 5))],
        out_hbm=True,
    )


def on_device(query_in, key_in, value_in, filter_taps, skip_gain, grad_out):
    seq_count, pair = lax.axis_size("seq"), lax.axis_size("pl")
    peers = seq_count * pair
    rows_dev, chan_dev = query_in.shape[1:]
    own = chan_dev // peers
    batch = query_in.shape[0] * lax.axis_size("dh") * lax.axis_size("dm") * pair
    factor = 1.0 / math.sqrt(batch * seq_count * rows_dev)
    query, key, value, grad = query_in[0], key_in[0], value_in[0], grad_out[0]

    def swap(values, axes):
        return lax.all_to_all(values, axes, split_axis=0, concat_axis=0, tiled=True)

    signals = swap(gate(query, key, value, grad, filter_taps, peers), ("pl", "seq"))
    spectra, term = taps_grad(signals, own, factor)

    def exchange(values, axis):
        return lax.ppermute(values, axis, [(0, 1), (1, 0)])

    def plus(a, b):
        return (a.astype(F32) + b.astype(F32)).astype(BF16)

    taken = exchange(term, "dm")
    results = states(signals, spectra, skip_gain, own)
    taken, results = lax.optimization_barrier((taken, results))
    term = plus(term, taken)
    term = plus(term, exchange(term, "dh"))
    copies = jnp.broadcast_to(term[None], (pair,) + term.shape).reshape((peers,) + term.shape[1:])
    back = swap(jnp.concatenate([results, copies], axis=1), ("pl", "seq"))
    outs = outputs(back, query, key, value, grad)
    return tuple(out[None] for out in outs[:4]) + (outs[4],)


def solution(mesh):
    dp, chan, seq = (mesh.shape[name] for name in ("dp", "chan", "seq"))
    split_mesh = Mesh(
        mesh.devices.reshape(dp // 4, 2, 2, chan, seq), ("dh", "dm", "pl", "chan", "seq")
    )
    rows = P(("dh", "dm", "pl"), "seq", "chan")
    taps = P("seq", "chan")
    return jax.shard_map(
        on_device,
        mesh=split_mesh,
        in_specs=(rows, rows, rows, taps, P("chan"), rows),
        out_specs=(rows, rows, rows, rows, taps),
        check_vma=False,
    )
```

time: 77.7 us -> 73.2 us (0.942)
  blocking collectives: 17.9 us -> 38.8 us
  starting transfers between devices: 23.7 us -> 14.3 us
  waiting for transfers between devices: 20.5 us -> 11.7 us
  Pallas kernels: 13.4 us -> 7.2 us
  local copies, waits for them, and re-layouts: 0.92 us -> 0.09 us
    all_to_all x1 -> x2, blocking collectives: 17.9 us -> 38.8 us  [swap(): return lax.all_to_all(values, axes, split_axis=0, concat_axis=0, tiled=True)]
    all_to_all x1 -> x0, waiting for transfers between devices: 10.3 us -> none  [swap(): return lax.all_to_all(values, axes, split_axis=0, concat_axis=0, tiled=True)]
    all_to_all x1 -> x0, starting transfers between devices: 9.47 us -> none  [swap(): return lax.all_to_all(values, axes, split_axis=0, concat_axis=0, tiled=True)]
    pallas_call x4, Pallas kernels: 13.4 us -> 7.2 us  [call(): pl.pallas_call(kernel, out_shape=shapes, in_specs=[place(in_hbm)] * len(a...]
    ppermute x2, waiting for transfers between devices: 10.2 us -> 11.7 us  [exchange(): return lax.ppermute(values, axis, [(0, 1), (1, 0)])]
  transfers between devices with their start and end apart: 3 -> 2, of which waited for: 2 -> 2; matrix products, arithmetic and copies ran while one was open for 1% -> 0% of each run, Pallas kernels for 6% -> 3%
where the time goes in v4:
time: 73.2 us; the launch traced here: 73 us
  blocking collectives  38.8 us (53%)
  starting transfers between devices  14.3 us (20%)
  waiting for transfers between devices  11.7 us (16%)
  Pallas kernels  7.2 us (10%)
  between operations  0.8 us (1%)
    all_to_all x2, blocking collectives, swap(): return lax.all_to_all(values, axes, split_axis=0, concat_axis=0, tiled=True)  38.8 us
    ppermute x2, starting transfers between devices, exchange(): return lax.ppermute(values, axis, [(0, 1), (1, 0)])  14.3 us
    ppermute x2, waiting for transfers between devices, exchange(): return lax.ppermute(values, axis, [(0, 1), (1, 0)])  11.7 us
    pallas_call x4, Pallas kernels, call(): pl.pallas_call(kernel, out_shape=shapes, in_specs=[place(in_hbm)] * len(a...  7.2 us
  transfers between devices with their start and end apart: 2, of which 2 were waited for; matrix products, arithmetic and copies ran while one was open for 0% of the time, Pallas kernels for 3%

profile of v4, /device:TPU:2, one launch (start us, length us, event | category | flops | bytes accessed | tf_op | source)
XLA Modules:
  0.0 73.0 jit_solution(9703334800055012016)
XLA Ops:
  0.6 0.0 copy-start.5
  0.6 0.0 copy-start.6
  0.7 0.0 copy-start.8
  0.7 1.7 %shard_map.155 = bf16[32,80,128]{2,1,0:T(8,128)(2,1)S(1)} custom-call(bf16[128,1024]{1,0:T(8,128)(2,1)} %bitcast.10, bf16[128,1024]{1,0:T(8,128)(2,1)} %bitcast.12, bf16[128,1024]{1,0:T(8,128)(2,1)} %bitcast.14, bf16[128,1024]{1,0:T(8,128)(2,1)} %bitcast.16, bf16[128,1024]{1,0:T(8,128)(2,1)} %taps.1), custom_call_target="tpu_custom_call" | custom-call | bytes 2097152 | tf_op jit(solution)/shard_map/pallas_call | solution.py:313
  2.3 20.4 %all_to_all.10.signals = bf16[32,80,128]{2,1,0:T(8,128)(2,1)S(1)} all-to-all(bf16[32,80,128]{2,1,0:T(8,128)(2,1)S(1)} %shard_map.155), channel_id=1, replica_groups=mesh['dh'=2,'dm'=2,'pl'=2,'chan'=4,'seq'=16] {'pl','seq'}, dimensions={0} | all-to-all | bytes 1310720 | tf_op jit(solution)/shard_map/all_to_all | solution.py:390
  22.7 0.0 copy-done.5
  22.7 0.0 copy-done.6
  22.7 0.0 copy-done.8
  22.7 0.0 copy-start.4
  22.7 0.0 copy-start.7
  22.7 2.0 %shard_map.156 = (f32[2176,256]{1,0:T(8,128)S(1)}, bf16[16,32,128]{2,1,0:T(8,128)(2,1)S(1)}) custom-call(bf16[32,80,128]{2,1,0:T(8,128)(2,1)S(1)} %all_to_all.10.signals, bf16[2,256,256]{2,1,0:T(8,128)(2,1)S(1)} %copy-done.6, bf16[2,256,256]{2,1,0:T(8,128)(2,1)S(1)} %copy-done.5, f32[17,4,128]{2,1,0:T(4,128)S(1)} %copy-done.8), custom_call_target="tpu_custom_call" | custom-call | flops 5000000000 | bytes 2097152 | tf_op jit(solution)/shard_map/pallas_call | solution.py:313
  24.7 5.2 %collective-permute-start = (bf16[16,32,128]{2,1,0:T(8,128)(2,1)S(1)}, bf16[16,32,128]{2,1,0:T(8,128)(2,1)S(1)}, u32[]{:S(2)}, u32[]{:S(2)}) collective-permute-start(bf16[16,32,128]{2,1,0:T(8,128)(2,1)S(1)} %get-tuple-element.14), channel_id=1, source_target_pairs={{0,128},{128,0},{1,129},{129,1},{2,130},{130,2},{3,131},{131,3},{4... | collective-permute-start | bytes 393224 | tf_op jit(solution)/shard_map/ppermute | solution.py:396
  29.9 0.0 copy-done.4
  29.9 0.0 copy-done.7
  30.0 2.2 %shard_map.157 = bf16[32,64,128]{2,1,0:T(8,128)(2,1)S(1)} custom-call(bf16[32,80,128]{2,1,0:T(8,128)(2,1)S(1)} %all_to_all.10.signals, f32[2176,256]{1,0:T(8,128)S(1)} %get-tuple-element.15.spec_ref, f32[8,128]{1,0:T(8,128)S(1)} %bitcast.18, bf16[2,256,256]{2,1,0:T(8,128)(2,1)S(1)} %copy-done.6, bf16[2,256,256]{2,1,0:T(8,128)(2,1)S(1)} %copy-done.5, ...), custom_call_target="tpu_custom_call" | custom-call | flops 5000000000 | bytes 2097152 | tf_op jit(solution)/shard_map/pallas_call | solution.py:313
  32.1 2.7 %collective-permute-done = bf16[16,32,128]{2,1,0:T(8,128)(2,1)S(1)} collective-permute-done((bf16[16,32,128]{2,1,0:T(8,128)(2,1)S(1)}, bf16[16,32,128]{2,1,0:T(8,128)(2,1)S(1)}, u32[]{:S(2)}, u32[]{:S(2)}) %collective-permute-start) | collective-permute-done | bytes 131104 | tf_op jit(solution)/shard_map/ppermute | solution.py:396
  34.9 9.1 %collective-permute-start.1 = (bf16[16,32,128]{2,1,0:T(8,128)(2,1)S(1)}, bf16[16,32,128]{2,1,0:T(8,128)(2,1)S(1)}, u32[]{:S(2)}, u32[]{:S(2)}) collective-permute-start(bf16[16,32,128]{2,1,0:T(8,128)(2,1)S(1)} %add_convert_fusion.1), channel_id=1, source_target_pairs={{0,256},{256,0},{1,257},{257,1},{2,258},{258,2},{3,259},{259,3},{4... | collective-permute-start | bytes 393224 | tf_op jit(solution)/shard_map/ppermute | solution.py:396
  44.0 8.9 %collective-permute-done.1 = bf16[16,32,128]{2,1,0:T(8,128)(2,1)S(1)} collective-permute-done((bf16[16,32,128]{2,1,0:T(8,128)(2,1)S(1)}, bf16[16,32,128]{2,1,0:T(8,128)(2,1)S(1)}, u32[]{:S(2)}, u32[]{:S(2)}) %collective-permute-start.1) | collective-permute-done | bytes 131104 | tf_op jit(solution)/shard_map/ppermute | solution.py:396
  53.0 0.0 copy-start
  53.0 0.0 copy-start.1
  53.0 0.0 copy-start.2
  53.1 0.0 copy-start.3
  53.1 0.1 pad_maximum_fusion
  53.1 18.5 %all_to_all.11.back = bf16[32,96,128]{2,1,0:T(8,128)(2,1)S(1)} all-to-all(bf16[32,96,128]{2,1,0:T(8,128)(2,1)S(1)} %pad_maximum_fusion), channel_id=1, replica_groups=mesh['dh'=2,'dm'=2,'pl'=2,'chan'=4,'seq'=16] {'pl','seq'}, dimensions={0} | all-to-all | bytes 1572864 | tf_op jit(solution)/shard_map/all_to_all | solution.py:390
  71.6 0.0 copy-done
  71.6 0.0 copy-done.1
  71.6 0.0 copy-done.2
  71.6 0.0 copy-done.3
  71.6 1.4 %shard_map.158 = (bf16[128,1024]{1,0:T(8,128)(2,1)}, bf16[128,1024]{1,0:T(8,128)(2,1)}, bf16[128,1024]{1,0:T(8,128)(2,1)}, bf16[128,1024]{1,0:T(8,128)(2,1)}, bf16[128,1024]{1,0:T(8,128)(2,1)}) custom-call(bf16[32,96,128]{2,1,0:T(8,128)(2,1)S(1)} %all_to_all.11.back, bf16[128,1024]{1,0:T(8,128)(2,1)S(1)} %bitcast.11, bf16[128,1024]{1,0:T(8,128)(2,1)S(1)} %bitcast.13, ...), custom_call_target="tpu_custom_call" | custom-call | bytes 2097152 | tf_op jit(solution)/shard_map/pallas_call | solution.py:313
  (3 shorter events, 0.1 us)
Async XLA Ops:
  0.6 22.1 %copy-start.5 = (bf16[2,256,256]{2,1,0:T(8,128)(2,1)S(1)}, bf16[2,256,256]{2,1,0:T(8,128)(2,1)}, u32[]{:S(2)}) copy-start(bf16[2,256,256]{2,1,0:T(8,128)(2,1)} %constant.9.clone.back_lane_ref) | copy-start | bytes 786436
  0.6 22.1 %copy-start.6 = (bf16[2,256,256]{2,1,0:T(8,128)(2,1)S(1)}, bf16[2,256,256]{2,1,0:T(8,128)(2,1)}, u32[]{:S(2)}) copy-start(bf16[2,256,256]{2,1,0:T(8,128)(2,1)} %constant.8.clone.lane_ref) | copy-start | bytes 786436
  0.7 22.1 %copy-start.8 = (f32[17,4,128]{2,1,0:T(4,128)S(1)}, f32[17,4,128]{2,1,0:T(4,128)}, u32[]{:S(2)}) copy-start(f32[17,4,128]{2,1,0:T(4,128)} %constant.10.clone.twist_ref) | copy-start | bytes 104452
  22.7 7.2 %copy-start.4 = (f32[1024]{0:T(1024)S(1)}, f32[1024]{0:T(1024)}, u32[]{:S(2)}) copy-start(f32[1024]{0:T(1024)} %param.16) | copy-start | bytes 12292
  22.7 7.2 %copy-start.7 = (f32[17,4,128]{2,1,0:T(4,128)S(1)}, f32[17,4,128]{2,1,0:T(4,128)}, u32[]{:S(2)}) copy-start(f32[17,4,128]{2,1,0:T(4,128)} %constant.11.clone.twist_ref) | copy-start | bytes 104452
  24.7 10.1 %collective-permute-start = (bf16[16,32,128]{2,1,0:T(8,128)(2,1)S(1)}, bf16[16,32,128]{2,1,0:T(8,128)(2,1)S(1)}, u32[]{:S(2)}, u32[]{:S(2)}) collective-permute-start(bf16[16,32,128]{2,1,0:T(8,128)(2,1)S(1)} %get-tuple-element.14), channel_id=1, source_target_pairs={{0,128},{128,0},{1,129},{129,1},{2,130},{130,2},{3,131},{131,3},{4... | collective-permute-start | bytes 393224 | tf_op jit(solution)/shard_map/ppermute | solution.py:396
  34.9 18.0 %collective-permute-start.1 = (bf16[16,32,128]{2,1,0:T(8,128)(2,1)S(1)}, bf16[16,32,128]{2,1,0:T(8,128)(2,1)S(1)}, u32[]{:S(2)}, u32[]{:S(2)}) collective-permute-start(bf16[16,32,128]{2,1,0:T(8,128)(2,1)S(1)} %add_convert_fusion.1), channel_id=1, source_target_pairs={{0,256},{256,0},{1,257},{257,1},{2,258},{258,2},{3,259},{259,3},{4... | collective-permute-start | bytes 393224 | tf_op jit(solution)/shard_map/ppermute | solution.py:396
  53.0 18.6 %copy-start = (bf16[1,128,1024]{2,1,0:T(8,128)(2,1)S(1)}, bf16[1,128,1024]{2,1,0:T(8,128)(2,1)}, u32[]{:S(2)}) copy-start(bf16[1,128,1024]{2,1,0:T(8,128)(2,1)} %param.12) | copy-start | bytes 786436
  53.0 18.6 %copy-start.1 = (bf16[1,128,1024]{2,1,0:T(8,128)(2,1)S(1)}, bf16[1,128,1024]{2,1,0:T(8,128)(2,1)}, u32[]{:S(2)}) copy-start(bf16[1,128,1024]{2,1,0:T(8,128)(2,1)} %param.13) | copy-start | bytes 786436
  53.0 18.6 %copy-start.2 = (bf16[1,128,1024]{2,1,0:T(8,128)(2,1)S(1)}, bf16[1,128,1024]{2,1,0:T(8,128)(2,1)}, u32[]{:S(2)}) copy-start(bf16[1,128,1024]{2,1,0:T(8,128)(2,1)} %param.14) | copy-start | bytes 786436
  53.1 18.6 %copy-start.3 = (bf16[1,128,1024]{2,1,0:T(8,128)(2,1)S(1)}, bf16[1,128,1024]{2,1,0:T(8,128)(2,1)}, u32[]{:S(2)}) copy-start(bf16[1,128,1024]{2,1,0:T(8,128)(2,1)} %param.17) | copy-start | bytes 786436

commit v5 on v4

--- a/solution.py
+++ b/solution.py
@@ -1,3 +1,4 @@
+import functools
 import math
 
 import jax
@@ -222,39 +223,29 @@
     return real_inverse(freqs, FREQS, True)
 
 
-def taps_grad_kernel(signals, lane_ref, back_lane_ref, twist_ref, spec_ref, out):
+def taps_grad_kernel(first, signals, lane_ref, back_lane_ref, twist_ref, spec_ref, out):
     batch = signals.shape[0] // ROWS
-    chans = out.shape[1]
-    total = HALF * chans
-
-    def chunk(first):
-        rows = {}
-        for which in range(2):
-            place = pl.ds(which * chans + first, CHUNK)
-            for b in range(batch):
-                rows[which, b] = spectrum(
-                    lambda r: signals[b * ROWS + r, place, :].astype(F32), twist_ref, lane_ref
-                )
-                base = (which * batch + b) * total
-                for k in range(HALF):
-                    spec_ref[pl.ds(base + k * chans + first, CHUNK), :] = rows[which, b][
-                        k * CHUNK : (k + 1) * CHUNK
-                    ]
-        product = conj_product(rows[0, 0], rows[1, 0])
-        for b in range(1, batch):
-            product = product + conj_product(rows[0, b], rows[1, b])
-        for r, row in enumerate(signal_rows(product, twist_ref, back_lane_ref)):
-            out[r, pl.ds(first, CHUNK), :] = row.astype(BF16)
-
-    for first in range(0, chans, CHUNK):
-        chunk(first)
-
-
-def state_kernel(signals, spec_ref, gain_ref, lane_ref, back_lane_ref, twist_ref, out, skip_ref):
+    chans = 2 * (signals.shape[1] // 5)
+    rows = {}
+    for which in range(2):
+        place = pl.ds(which * chans + first, CHUNK)
+        for b in range(batch):
+            rows[which, b] = spectrum(
+                lambda r: signals[b * ROWS + r, place, :].astype(F32), twist_ref, lane_ref
+            )
+            spec_ref[which * batch + b] = rows[which, b]
+    product = conj_product(rows[0, 0], rows[1, 0])
+    for b in range(1, batch):
+        product = product + conj_product(rows[0, b], rows[1, b])
+    for r, row in enumerate(signal_rows(product, twist_ref, back_lane_ref)):
+        out[r] = row.astype(BF16)
+
+
+def state_kernel(signals, gain_ref, lane_ref, back_lane_ref, twist_ref, *refs):
+    *specs, out, skip_ref = refs
     batch = signals.shape[0] // ROWS
     chans = out.shape[1] // 2
     share = signals.shape[1] - 2 * chans
-    total = HALF * chans
     place = lax.axis_index("pl") * lax.axis_size("seq") + lax.axis_index("seq")
     pieces = LANES // chans
     gains = jnp.broadcast_to(gain_ref[pl.ds(place // pieces, 1), :], (LANES, LANES))
@@ -271,9 +262,7 @@
         for which, product in enumerate((plain_product, conj_product)):
             place = pl.ds(which * chans + first, CHUNK)
             for b in range(batch):
-                base = (which * batch + b) * total + first
-                other = [spec_ref[pl.ds(base + k * chans, CHUNK), :] for k in range(HALF)]
-                spec = product(taps, jnp.concatenate(other, axis=0))
+                spec = product(taps, specs[first // CHUNK][which * batch + b])
                 for r, row in enumerate(signal_rows(spec, twist_ref, back_lane_ref)):
                     own = signals[b * ROWS + r, place, :].astype(F32)
                     out[b * ROWS + r, place, :] = (row + skip * own).astype(BF16)
@@ -337,32 +326,30 @@
     )
 
 
-def taps_grad(signals, own, factor):
-    total = HALF * own
+def taps_grad(signals, first, factor):
     batch = signals.shape[0] // ROWS
     forward_lane, inverse_lane = lane_tables()
     shape = jax.ShapeDtypeStruct
     return call(
-        taps_grad_kernel,
+        functools.partial(taps_grad_kernel, first),
         (
-            shape((2 * batch * total, 2 * LANES), F32),
-            shape((ROWS, own, LANES), BF16),
+            shape((2 * batch, HALF * CHUNK, 2 * LANES), F32),
+            shape((ROWS, CHUNK, LANES), BF16),
         ),
         (signals, forward_lane, inverse_lane, twist_tables(factor)),
-        flops=5 * 10**9,
+        flops=2 * 10**9,
     )
 
 
 def states(signals, spectra, skip_gain, own):
-    total = HALF * own
     batch = signals.shape[0] // ROWS
     forward_lane, inverse_lane = lane_tables()
     return call(
         state_kernel,
         jax.ShapeDtypeStruct((batch * ROWS, 2 * own, LANES), BF16),
-        (signals, spectra, skip_gain.reshape(-1, LANES), forward_lane, inverse_lane, twist_tables(1.0)),
+        (signals, skip_gain.reshape(-1, LANES), forward_lane, inverse_lane, twist_tables(1.0), *spectra),
         (pltpu.VMEM((LANES, LANES), F32),),
-        flops=5 * 10**9,
+        flops=3 * 10**9,
     )
 
 
@@ -390,7 +377,6 @@
         return lax.all_to_all(values, axes, split_axis=0, concat_axis=0, tiled=True)
 
     signals = swap(gate(query, key, value, grad, filter_taps, peers), ("pl", "seq"))
-    spectra, term = taps_grad(signals, own, factor)
 
     def exchange(values, axis):
         return lax.ppermute(values, axis, [(0, 1), (1, 0)])
@@ -398,13 +384,16 @@
     def plus(a, b):
         return (a.astype(F32) + b.astype(F32)).astype(BF16)
 
-    taken = exchange(term, "dm")
+    spectra, terms = zip(*(taps_grad(signals, first, factor) for first in range(0, own, CHUNK)))
+    orders = [("dm", "dh"), ("dh", "dm")]
+    terms = [plus(term, exchange(term, order[0])) for term, order in zip(terms, orders)]
+    others = [exchange(term, order[1]) for term, order in zip(terms, orders)]
+    spectra, _ = lax.optimization_barrier((spectra, terms[0]))
     results = states(signals, spectra, skip_gain, own)
-    taken, results = lax.optimization_barrier((taken, results))
-    term = plus(term, taken)
-    term = plus(term, exchange(term, "dh"))
-    copies = jnp.broadcast_to(term[None], (pair,) + term.shape).reshape((peers,) + term.shape[1:])
-    back = swap(jnp.concatenate([results, copies], axis=1), ("pl", "seq"))
+    others, results = lax.optimization_barrier((others, results))
+    terms = [plus(term, other) for term, other in zip(terms, others)]
+    copies = [jnp.broadcast_to(t[None], (pair,) + t.shape).reshape((peers,) + t.shape[1:]) for t in terms]
+    back = swap(jnp.concatenate([results, *copies], axis=1), ("pl", "seq"))
     outs = outputs(back, query, key, value, grad)
     return tuple(out[None] for out in outs[:4]) + (outs[4],)
 

time: 73.2 us -> 72 us (0.984)
  the two profiles are of different devices: /device:TPU:2 before, /device:TPU:8 now
where the time goes in v5:
time: 72 us; the launch traced here: 71.6 us
  blocking collectives  38.6 us (54%)
  starting transfers between devices  21.2 us (29%)
  Pallas kernels  7.6 us (11%)
  waiting for transfers between devices  3.15 us (4%)
  between operations  0.85 us (1%)
    all_to_all x2, blocking collectives, swap(): return lax.all_to_all(values, axes, split_axis=0, concat_axis=0, tiled=True)  38.6 us
    ppermute x4, starting transfers between devices, exchange(): return lax.ppermute(values, axis, [(0, 1), (1, 0)])  21.2 us
    pallas_call x5, Pallas kernels, call(): pl.pallas_call(kernel, out_shape=shapes, in_specs=[place(in_hbm)] * len(a...  7.6 us
    ppermute x4, waiting for transfers between devices, exchange(): return lax.ppermute(values, axis, [(0, 1), (1, 0)])  3.15 us
  transfers between devices with their start and end apart: 4, of which 3 were waited for; matrix products, arithmetic and copies ran while one was open for 0% of the time, Pallas kernels for 5%

profile of v5, /device:TPU:8, one launch (start us, length us, event | category | flops | bytes accessed | tf_op | source)
XLA Modules:
  0.0 71.6 jit_solution(15059046503054835555)
XLA Ops:
  0.6 1.6 %shard_map.182 = bf16[32,80,128]{2,1,0:T(8,128)(2,1)S(1)} custom-call(bf16[128,1024]{1,0:T(8,128)(2,1)} %bitcast.11, bf16[128,1024]{1,0:T(8,128)(2,1)} %bitcast.13, bf16[128,1024]{1,0:T(8,128)(2,1)} %bitcast.15, bf16[128,1024]{1,0:T(8,128)(2,1)} %bitcast.17, bf16[128,1024]{1,0:T(8,128)(2,1)} %taps.1), custom_call_target="tpu_custom_call" | custom-call | bytes 2097152 | tf_op jit(solution)/shard_map/pallas_call | solution.py:302
  2.3 0.0 copy-start.5
  2.3 0.0 copy-start.6
  2.3 0.0 copy-start.8
  2.3 20.5 %all_to_all.10.signals = bf16[32,80,128]{2,1,0:T(8,128)(2,1)S(1)} all-to-all(bf16[32,80,128]{2,1,0:T(8,128)(2,1)S(1)} %shard_map.182), channel_id=1, replica_groups=mesh['dh'=2,'dm'=2,'pl'=2,'chan'=4,'seq'=16] {'pl','seq'}, dimensions={0} | all-to-all | bytes 1310720 | tf_op jit(solution)/shard_map/all_to_all | solution.py:377
  22.8 0.0 copy-done.5
  22.8 0.0 copy-done.6
  22.8 0.0 copy-done.8
  22.8 1.2 %shard_map.183 = (f32[4,272,256]{2,1,0:T(8,128)S(1)}, bf16[16,16,128]{2,1,0:T(8,128)(2,1)S(1)}) custom-call(bf16[32,80,128]{2,1,0:T(8,128)(2,1)S(1)} %all_to_all.10.signals, bf16[2,256,256]{2,1,0:T(8,128)(2,1)S(1)} %copy-done.5, bf16[2,256,256]{2,1,0:T(8,128)(2,1)S(1)} %copy-done.6, f32[17,4,128]{2,1,0:T(4,128)S(1)} %copy-done.8), custom_call_target="tpu_custom_call" | custom-call | flops 2000000000 | bytes 2097152 | tf_op jit(solution)/shard_map/pallas_call | solution.py:302
  24.1 0.0 copy-start.4
  24.1 0.0 copy-start.7
  24.1 5.2 %collective-permute-start = (bf16[16,16,128]{2,1,0:T(8,128)(2,1)S(1)}, bf16[16,16,128]{2,1,0:T(8,128)(2,1)S(1)}, u32[]{:S(2)}, u32[]{:S(2)}) collective-permute-start(bf16[16,16,128]{2,1,0:T(8,128)(2,1)S(1)} %get-tuple-element.19), channel_id=1, source_target_pairs={{0,128},{128,0},{1,129},{129,1},{2,130},{130,2},{3,131},{131,3},{4... | collective-permute-start | bytes 196616 | tf_op jit(solution)/shard_map/ppermute | solution.py:382
  29.3 1.2 %shard_map.184 = (f32[4,272,256]{2,1,0:T(8,128)S(1)}, bf16[16,16,128]{2,1,0:T(8,128)(2,1)S(1)}) custom-call(bf16[32,80,128]{2,1,0:T(8,128)(2,1)S(1)} %all_to_all.10.signals, bf16[2,256,256]{2,1,0:T(8,128)(2,1)S(1)} %copy-done.5, bf16[2,256,256]{2,1,0:T(8,128)(2,1)S(1)} %copy-done.6, f32[17,4,128]{2,1,0:T(4,128)S(1)} %copy-done.8), custom_call_target="tpu_custom_call" | custom-call | flops 2000000000 | bytes 2097152 | tf_op jit(solution)/shard_map/pallas_call | solution.py:302
  30.5 9.1 %collective-permute-start.2 = (bf16[16,16,128]{2,1,0:T(8,128)(2,1)S(1)}, bf16[16,16,128]{2,1,0:T(8,128)(2,1)S(1)}, u32[]{:S(2)}, u32[]{:S(2)}) collective-permute-start(bf16[16,16,128]{2,1,0:T(8,128)(2,1)S(1)} %get-tuple-element.20), channel_id=1, source_target_pairs={{0,256},{256,0},{1,257},{257,1},{2,258},{258,2},{3,259},{259,3},{4... | collective-permute-start | bytes 196616 | tf_op jit(solution)/shard_map/ppermute | solution.py:382
  39.6 0.0 collective-permute-done
  39.6 2.8 %collective-permute-start.1 = (bf16[16,16,128]{2,1,0:T(8,128)(2,1)S(1)}, bf16[16,16,128]{2,1,0:T(8,128)(2,1)S(1)}, u32[]{:S(2)}, u32[]{:S(2)}) collective-permute-start(bf16[16,16,128]{2,1,0:T(8,128)(2,1)S(1)} %add_convert_fusion.3), channel_id=1, source_target_pairs={{0,256},{256,0},{1,257},{257,1},{2,258},{258,2},{3,259},{259,3},{4... | collective-permute-start | bytes 196616 | tf_op jit(solution)/shard_map/ppermute | solution.py:382
  42.5 1.3 %collective-permute-done.2 = bf16[16,16,128]{2,1,0:T(8,128)(2,1)S(1)} collective-permute-done((bf16[16,16,128]{2,1,0:T(8,128)(2,1)S(1)}, bf16[16,16,128]{2,1,0:T(8,128)(2,1)S(1)}, u32[]{:S(2)}, u32[]{:S(2)}) %collective-permute-start.2) | collective-permute-done | bytes 65568 | tf_op jit(solution)/shard_map/ppermute | solution.py:382
  43.8 4.1 %collective-permute-start.3 = (bf16[16,16,128]{2,1,0:T(8,128)(2,1)S(1)}, bf16[16,16,128]{2,1,0:T(8,128)(2,1)S(1)}, u32[]{:S(2)}, u32[]{:S(2)}) collective-permute-start(bf16[16,16,128]{2,1,0:T(8,128)(2,1)S(1)} %add_convert_fusion.2), channel_id=1, source_target_pairs={{0,128},{128,0},{1,129},{129,1},{2,130},{130,2},{3,131},{131,3},{4... | collective-permute-start | bytes 196616 | tf_op jit(solution)/shard_map/ppermute | solution.py:382
  47.9 0.0 copy-done.4
  47.9 0.0 copy-done.7
  47.9 2.2 %shard_map.185 = bf16[32,64,128]{2,1,0:T(8,128)(2,1)S(1)} custom-call(bf16[32,80,128]{2,1,0:T(8,128)(2,1)S(1)} %all_to_all.10.signals, f32[8,128]{1,0:T(8,128)S(1)} %bitcast.19, bf16[2,256,256]{2,1,0:T(8,128)(2,1)S(1)} %copy-done.5, bf16[2,256,256]{2,1,0:T(8,128)(2,1)S(1)} %copy-done.6, f32[17,4,128]{2,1,0:T(4,128)S(1)} %copy-done.7, ...), custom_call_target="tpu_custom_call" | custom-call | flops 3000000000 | bytes 2097152 | tf_op jit(solution)/shard_map/pallas_call | solution.py:302
  50.1 0.6 collective-permute-done.1
  50.7 1.3 %collective-permute-done.3 = bf16[16,16,128]{2,1,0:T(8,128)(2,1)S(1)} collective-permute-done((bf16[16,16,128]{2,1,0:T(8,128)(2,1)S(1)}, bf16[16,16,128]{2,1,0:T(8,128)(2,1)S(1)}, u32[]{:S(2)}, u32[]{:S(2)}) %collective-permute-start.3) | collective-permute-done | bytes 65568 | tf_op jit(solution)/shard_map/ppermute | solution.py:382
  52.1 0.1 pad_maximum_fusion
  52.1 0.0 copy-start
  52.1 0.0 copy-start.1
  52.1 0.0 copy-start.2
  52.2 0.0 copy-start.3
  52.2 18.1 %all_to_all.11.back = bf16[32,96,128]{2,1,0:T(8,128)(2,1)S(1)} all-to-all(bf16[32,96,128]{2,1,0:T(8,128)(2,1)S(1)} %pad_maximum_fusion), channel_id=1, replica_groups=mesh['dh'=2,'dm'=2,'pl'=2,'chan'=4,'seq'=16] {'pl','seq'}, dimensions={0} | all-to-all | bytes 1572864 | tf_op jit(solution)/shard_map/all_to_all | solution.py:377
  70.3 0.0 copy-done
  70.3 0.0 copy-done.3
  70.3 1.4 %shard_map.186 = (bf16[128,1024]{1,0:T(8,128)(2,1)}, bf16[128,1024]{1,0:T(8,128)(2,1)}, bf16[128,1024]{1,0:T(8,128)(2,1)}, bf16[128,1024]{1,0:T(8,128)(2,1)}, bf16[128,1024]{1,0:T(8,128)(2,1)}) custom-call(bf16[32,96,128]{2,1,0:T(8,128)(2,1)S(1)} %all_to_all.11.back, bf16[128,1024]{1,0:T(8,128)(2,1)S(1)} %bitcast.12, bf16[128,1024]{1,0:T(8,128)(2,1)S(1)} %bitcast.14, ...), custom_call_target="tpu_custom_call" | custom-call | bytes 2097152 | tf_op jit(solution)/shard_map/pallas_call | solution.py:302
  (7 shorter events, 0.1 us)
Async XLA Ops:
  2.3 20.5 %copy-start.5 = (bf16[2,256,256]{2,1,0:T(8,128)(2,1)S(1)}, bf16[2,256,256]{2,1,0:T(8,128)(2,1)}, u32[]{:S(2)}) copy-start(bf16[2,256,256]{2,1,0:T(8,128)(2,1)} %constant.8.clone.lane_ref) | copy-start | bytes 786436
  2.3 20.5 %copy-start.6 = (bf16[2,256,256]{2,1,0:T(8,128)(2,1)S(1)}, bf16[2,256,256]{2,1,0:T(8,128)(2,1)}, u32[]{:S(2)}) copy-start(bf16[2,256,256]{2,1,0:T(8,128)(2,1)} %constant.9.clone.back_lane_ref) | copy-start | bytes 786436
  2.3 20.5 %copy-start.8 = (f32[17,4,128]{2,1,0:T(4,128)S(1)}, f32[17,4,128]{2,1,0:T(4,128)}, u32[]{:S(2)}) copy-start(f32[17,4,128]{2,1,0:T(4,128)} %constant.10.clone.twist_ref) | copy-start | bytes 104452
  24.1 23.9 %copy-start.4 = (f32[1024]{0:T(1024)S(1)}, f32[1024]{0:T(1024)}, u32[]{:S(2)}) copy-start(f32[1024]{0:T(1024)} %param.19) | copy-start | bytes 12292
  24.1 23.9 %copy-start.7 = (f32[17,4,128]{2,1,0:T(4,128)S(1)}, f32[17,4,128]{2,1,0:T(4,128)}, u32[]{:S(2)}) copy-start(f32[17,4,128]{2,1,0:T(4,128)} %constant.11.clone.twist_ref) | copy-start | bytes 104452
  24.1 15.5 %collective-permute-start = (bf16[16,16,128]{2,1,0:T(8,128)(2,1)S(1)}, bf16[16,16,128]{2,1,0:T(8,128)(2,1)S(1)}, u32[]{:S(2)}, u32[]{:S(2)}) collective-permute-start(bf16[16,16,128]{2,1,0:T(8,128)(2,1)S(1)} %get-tuple-element.19), channel_id=1, source_target_pairs={{0,128},{128,0},{1,129},{129,1},{2,130},{130,2},{3,131},{131,3},{4... | collective-permute-start | bytes 196616 | tf_op jit(solution)/shard_map/ppermute | solution.py:382
  30.5 13.2 %collective-permute-start.2 = (bf16[16,16,128]{2,1,0:T(8,128)(2,1)S(1)}, bf16[16,16,128]{2,1,0:T(8,128)(2,1)S(1)}, u32[]{:S(2)}, u32[]{:S(2)}) collective-permute-start(bf16[16,16,128]{2,1,0:T(8,128)(2,1)S(1)} %get-tuple-element.20), channel_id=1, source_target_pairs={{0,256},{256,0},{1,257},{257,1},{2,258},{258,2},{3,259},{259,3},{4... | collective-permute-start | bytes 196616 | tf_op jit(solution)/shard_map/ppermute | solution.py:382
  39.6 11.1 %collective-permute-start.1 = (bf16[16,16,128]{2,1,0:T(8,128)(2,1)S(1)}, bf16[16,16,128]{2,1,0:T(8,128)(2,1)S(1)}, u32[]{:S(2)}, u32[]{:S(2)}) collective-permute-start(bf16[16,16,128]{2,1,0:T(8,128)(2,1)S(1)} %add_convert_fusion.3), channel_id=1, source_target_pairs={{0,256},{256,0},{1,257},{257,1},{2,258},{258,2},{3,259},{259,3},{4... | collective-permute-start | bytes 196616 | tf_op jit(solution)/shard_map/ppermute | solution.py:382
  43.8 8.2 %collective-permute-start.3 = (bf16[16,16,128]{2,1,0:T(8,128)(2,1)S(1)}, bf16[16,16,128]{2,1,0:T(8,128)(2,1)S(1)}, u32[]{:S(2)}, u32[]{:S(2)}) collective-permute-start(bf16[16,16,128]{2,1,0:T(8,128)(2,1)S(1)} %add_convert_fusion.2), channel_id=1, source_target_pairs={{0,128},{128,0},{1,129},{129,1},{2,130},{130,2},{3,131},{131,3},{4... | collective-permute-start | bytes 196616 | tf_op jit(solution)/shard_map/ppermute | solution.py:382
  52.1 18.1 %copy-start = (bf16[1,128,1024]{2,1,0:T(8,128)(2,1)S(1)}, bf16[1,128,1024]{2,1,0:T(8,128)(2,1)}, u32[]{:S(2)}) copy-start(bf16[1,128,1024]{2,1,0:T(8,128)(2,1)} %param.15) | copy-start | bytes 786436
  52.1 18.1 %copy-start.1 = (bf16[1,128,1024]{2,1,0:T(8,128)(2,1)S(1)}, bf16[1,128,1024]{2,1,0:T(8,128)(2,1)}, u32[]{:S(2)}) copy-start(bf16[1,128,1024]{2,1,0:T(8,128)(2,1)} %param.16) | copy-start | bytes 786436
  52.1 18.1 %copy-start.2 = (bf16[1,128,1024]{2,1,0:T(8,128)(2,1)S(1)}, bf16[1,128,1024]{2,1,0:T(8,128)(2,1)}, u32[]{:S(2)}) copy-start(bf16[1,128,1024]{2,1,0:T(8,128)(2,1)} %param.17) | copy-start | bytes 786436
  52.2 18.1 %copy-start.3 = (bf16[1,128,1024]{2,1,0:T(8,128)(2,1)S(1)}, bf16[1,128,1024]{2,1,0:T(8,128)(2,1)}, u32[]{:S(2)}) copy-start(bf16[1,128,1024]{2,1,0:T(8,128)(2,1)} %param.20) | copy-start | bytes 786436

commit v6 on v5

--- a/solution.py
+++ b/solution.py
@@ -223,12 +223,18 @@
     return real_inverse(freqs, FREQS, True)
 
 
-def taps_grad_kernel(first, signals, lane_ref, back_lane_ref, twist_ref, spec_ref, out):
+def half_start(kept):
+    mine = lax.axis_index("dm")
+    return pl.multiple_of((mine if kept else 1 - mine) * CHUNK, CHUNK)
+
+
+def taps_grad_kernel(kept, signals, lane_ref, back_lane_ref, twist_ref, spec_ref, out):
+    first = half_start(kept)
     batch = signals.shape[0] // ROWS
     chans = 2 * (signals.shape[1] // 5)
     rows = {}
     for which in range(2):
-        place = pl.ds(which * chans + first, CHUNK)
+        place = pl.ds(pl.multiple_of(which * chans + first, CHUNK), CHUNK)
         for b in range(batch):
             rows[which, b] = spectrum(
                 lambda r: signals[b * ROWS + r, place, :].astype(F32), twist_ref, lane_ref
@@ -251,18 +257,19 @@
     gains = jnp.broadcast_to(gain_ref[pl.ds(place // pieces, 1), :], (LANES, LANES))
     skip_ref[...] = gains.T
     begin = pl.multiple_of(place % pieces * chans, chans)
-    for first in range(0, chans, CHUNK):
-        source, place = divmod(first, share)
+    for kept, spec_ref in enumerate(specs):
+        first = half_start(kept)
+        source = first // share
         taps = spectrum(
-            lambda r: signals[source * ROWS + r, pl.ds(2 * chans + place, CHUNK), :].astype(F32),
+            lambda r: signals[source * ROWS + r, pl.ds(2 * chans, CHUNK), :].astype(F32),
             twist_ref,
             lane_ref,
         )
-        skip = skip_ref[pl.ds(begin + first, CHUNK), :]
+        skip = skip_ref[pl.ds(pl.multiple_of(begin + first, CHUNK), CHUNK), :]
         for which, product in enumerate((plain_product, conj_product)):
-            place = pl.ds(which * chans + first, CHUNK)
+            place = pl.ds(pl.multiple_of(which * chans + first, CHUNK), CHUNK)
             for b in range(batch):
-                spec = product(taps, specs[first // CHUNK][which * batch + b])
+                spec = product(taps, spec_ref[which * batch + b])
                 for r, row in enumerate(signal_rows(spec, twist_ref, back_lane_ref)):
                     own = signals[b * ROWS + r, place, :].astype(F32)
                     out[b * ROWS + r, place, :] = (row + skip * own).astype(BF16)
@@ -273,17 +280,18 @@
     own = back.shape[1] // 3
     pieces = LANES // own
     width = query.shape[1] // GROUPS
+    places = (half_start(1), half_start(0))
+    halves = [pl.ds(pl.multiple_of(2 * own + place, CHUNK), CHUNK) for place in places]
     sent = []
     for group in range(GROUPS):
         for tile in range(group * width // LANES, (group + 1) * width // LANES):
             cols = pl.ds(tile * LANES, LANES)
-            state, dmixed, term = (
-                jnp.concatenate(
-                    [back[tile * pieces + i, pl.ds(which * own, own), :] for i in range(pieces)],
-                    axis=0,
-                ).T
-                for which in range(3)
+            blocks = [tile * pieces + i for i in range(pieces)]
+            state, dmixed = (
+                jnp.concatenate([back[i, pl.ds(which * own, own), :] for i in blocks], axis=0).T
+                for which in range(2)
             )
+            term = jnp.concatenate([back[i, half, :] for i in blocks for half in halves], axis=0).T
             state, dmixed = state.astype(F32), dmixed.astype(F32)
             held[0][:, cols] = (query[:, cols].astype(F32) * state).astype(BF16)
             held[1][:, cols] = (grad[:, cols].astype(F32) * state).astype(BF16)
@@ -326,12 +334,12 @@
     )
 
 
-def taps_grad(signals, first, factor):
+def taps_grad(signals, kept, factor):
     batch = signals.shape[0] // ROWS
     forward_lane, inverse_lane = lane_tables()
     shape = jax.ShapeDtypeStruct
     return call(
-        functools.partial(taps_grad_kernel, first),
+        functools.partial(taps_grad_kernel, kept),
         (
             shape((2 * batch, HALF * CHUNK, 2 * LANES), F32),
             shape((ROWS, CHUNK, LANES), BF16),
@@ -384,15 +392,17 @@
     def plus(a, b):
         return (a.astype(F32) + b.astype(F32)).astype(BF16)
 
-    spectra, terms = zip(*(taps_grad(signals, first, factor) for first in range(0, own, CHUNK)))
-    orders = [("dm", "dh"), ("dh", "dm")]
-    terms = [plus(term, exchange(term, order[0])) for term, order in zip(terms, orders)]
-    others = [exchange(term, order[1]) for term, order in zip(terms, orders)]
-    spectra, _ = lax.optimization_barrier((spectra, terms[0]))
+    spectra, (given, term) = zip(*(taps_grad(signals, kept, factor) for kept in range(2)))
+    term = plus(term, exchange(given, "dm"))
+    other = exchange(term, "dh")
+    spectra, _ = lax.optimization_barrier((spectra, term))
     results = states(signals, spectra, skip_gain, own)
-    others, results = lax.optimization_barrier((others, results))
-    terms = [plus(term, other) for term, other in zip(terms, others)]
-    copies = [jnp.broadcast_to(t[None], (pair,) + t.shape).reshape((peers,) + t.shape[1:]) for t in terms]
+    other, results = lax.optimization_barrier((other, results))
+    term = plus(term, other)
+    copies = [
+        jnp.broadcast_to(t[None], (pair,) + t.shape).reshape((peers,) + t.shape[1:])
+        for t in (term, exchange(term, "dm"))
+    ]
     back = swap(jnp.concatenate([results, *copies], axis=1), ("pl", "seq"))
     outs = outputs(back, query, key, value, grad)
     return tuple(out[None] for out in outs[:4]) + (outs[4],)

time: 72 us -> 69.6 us (0.967)
  the two profiles are of different devices: /device:TPU:8 before, /device:TPU:64 now
where the time goes in v6:
time: 69.6 us; the launch traced here: 69.3 us
  blocking collectives  38.3 us (55%)
  starting transfers between devices  13.7 us (20%)
  waiting for transfers between devices  8.66 us (12%)
  Pallas kernels  7.56 us (11%)
  between operations  0.82 us (1%)
    all_to_all x2, blocking collectives, swap(): return lax.all_to_all(values, axes, split_axis=0, concat_axis=0, tiled=True)  38.3 us
    ppermute x3, starting transfers between devices, exchange(): return lax.ppermute(values, axis, [(0, 1), (1, 0)])  13.7 us
    ppermute x3, waiting for transfers between devices, exchange(): return lax.ppermute(values, axis, [(0, 1), (1, 0)])  8.66 us
    pallas_call x5, Pallas kernels, call(): pl.pallas_call(kernel, out_shape=shapes, in_specs=[place(in_hbm)] * len(a...  7.56 us
  transfers between devices with their start and end apart: 3, of which 3 were waited for; matrix products, arithmetic and copies ran while one was open for 0% of the time, Pallas kernels for 5%

profile of v6, /device:TPU:64, one launch (start us, length us, event | category | flops | bytes accessed | tf_op | source)
XLA Modules:
  0.0 69.3 jit_solution(16269078423038988238)
XLA Ops:
  0.6 1.6 %shard_map.182 = bf16[32,80,128]{2,1,0:T(8,128)(2,1)S(1)} custom-call(bf16[128,1024]{1,0:T(8,128)(2,1)} %bitcast.11, bf16[128,1024]{1,0:T(8,128)(2,1)} %bitcast.13, bf16[128,1024]{1,0:T(8,128)(2,1)} %bitcast.15, bf16[128,1024]{1,0:T(8,128)(2,1)} %bitcast.17, bf16[128,1024]{1,0:T(8,128)(2,1)} %taps.1), custom_call_target="tpu_custom_call" | custom-call | bytes 2097152 | tf_op jit(solution)/shard_map/pallas_call | solution.py:310
  2.3 0.0 copy-start.5
  2.3 0.0 copy-start.6
  2.3 0.0 copy-start.8
  2.3 21.4 %all_to_all.10.signals = bf16[32,80,128]{2,1,0:T(8,128)(2,1)S(1)} all-to-all(bf16[32,80,128]{2,1,0:T(8,128)(2,1)S(1)} %shard_map.182), channel_id=1, replica_groups=mesh['dh'=2,'dm'=2,'pl'=2,'chan'=4,'seq'=16] {'pl','seq'}, dimensions={0} | all-to-all | bytes 1310720 | tf_op jit(solution)/shard_map/all_to_all | solution.py:385
  23.7 0.0 copy-done.5
  23.8 0.0 copy-done.6
  23.8 0.0 copy-done.8
  23.8 1.2 %shard_map.184 = (f32[4,272,256]{2,1,0:T(8,128)S(1)}, bf16[16,16,128]{2,1,0:T(8,128)(2,1)S(1)}) custom-call(bf16[32,80,128]{2,1,0:T(8,128)(2,1)S(1)} %all_to_all.10.signals, bf16[2,256,256]{2,1,0:T(8,128)(2,1)S(1)} %copy-done.6, bf16[2,256,256]{2,1,0:T(8,128)(2,1)S(1)} %copy-done.5, f32[17,4,128]{2,1,0:T(4,128)S(1)} %copy-done.8), custom_call_target="tpu_custom_call" | custom-call | flops 2000000000 | bytes 2097152 | tf_op jit(solution)/shard_map/pallas_call | solution.py:310
  25.0 0.0 copy-start.4
  25.0 0.0 copy-start.7
  25.0 1.9 %collective-permute-start = (bf16[16,16,128]{2,1,0:T(8,128)(2,1)S(1)}, bf16[16,16,128]{2,1,0:T(8,128)(2,1)S(1)}, u32[]{:S(2)}, u32[]{:S(2)}) collective-permute-start(bf16[16,16,128]{2,1,0:T(8,128)(2,1)S(1)} %get-tuple-element.19), channel_id=1, source_target_pairs={{0,128},{128,0},{1,129},{129,1},{2,130},{130,2},{3,131},{131,3},{4... | collective-permute-start | bytes 196616 | tf_op jit(solution)/shard_map/ppermute | solution.py:390
  26.9 1.2 %shard_map.183 = (f32[4,272,256]{2,1,0:T(8,128)S(1)}, bf16[16,16,128]{2,1,0:T(8,128)(2,1)S(1)}) custom-call(bf16[32,80,128]{2,1,0:T(8,128)(2,1)S(1)} %all_to_all.10.signals, bf16[2,256,256]{2,1,0:T(8,128)(2,1)S(1)} %copy-done.6, bf16[2,256,256]{2,1,0:T(8,128)(2,1)S(1)} %copy-done.5, f32[17,4,128]{2,1,0:T(4,128)S(1)} %copy-done.8), custom_call_target="tpu_custom_call" | custom-call | flops 2000000000 | bytes 2097152 | tf_op jit(solution)/shard_map/pallas_call | solution.py:310
  28.1 4.0 %collective-permute-done = bf16[16,16,128]{2,1,0:T(8,128)(2,1)S(1)} collective-permute-done((bf16[16,16,128]{2,1,0:T(8,128)(2,1)S(1)}, bf16[16,16,128]{2,1,0:T(8,128)(2,1)S(1)}, u32[]{:S(2)}, u32[]{:S(2)}) %collective-permute-start) | collective-permute-done | bytes 65568 | tf_op jit(solution)/shard_map/ppermute | solution.py:390
  32.2 9.1 %collective-permute-start.1 = (bf16[16,16,128]{2,1,0:T(8,128)(2,1)S(1)}, bf16[16,16,128]{2,1,0:T(8,128)(2,1)S(1)}, u32[]{:S(2)}, u32[]{:S(2)}) collective-permute-start(bf16[16,16,128]{2,1,0:T(8,128)(2,1)S(1)} %add_convert_fusion.1), channel_id=1, source_target_pairs={{0,256},{256,0},{1,257},{257,1},{2,258},{258,2},{3,259},{259,3},{4... | collective-permute-start | bytes 196616 | tf_op jit(solution)/shard_map/ppermute | solution.py:390
  41.3 0.0 copy-done.4
  41.3 0.0 copy-done.7
  41.3 2.2 %shard_map.185 = bf16[32,64,128]{2,1,0:T(8,128)(2,1)S(1)} custom-call(bf16[32,80,128]{2,1,0:T(8,128)(2,1)S(1)} %all_to_all.10.signals, f32[8,128]{1,0:T(8,128)S(1)} %bitcast.19, bf16[2,256,256]{2,1,0:T(8,128)(2,1)S(1)} %copy-done.6, bf16[2,256,256]{2,1,0:T(8,128)(2,1)S(1)} %copy-done.5, f32[17,4,128]{2,1,0:T(4,128)S(1)} %copy-done.7, ...), custom_call_target="tpu_custom_call" | custom-call | flops 3000000000 | bytes 2097152 | tf_op jit(solution)/shard_map/pallas_call | solution.py:310
  43.5 0.3 collective-permute-done.1
  43.8 2.7 %collective-permute-start.2 = (bf16[16,16,128]{2,1,0:T(8,128)(2,1)S(1)}, bf16[16,16,128]{2,1,0:T(8,128)(2,1)S(1)}, u32[]{:S(2)}, u32[]{:S(2)}) collective-permute-start(bf16[16,16,128]{2,1,0:T(8,128)(2,1)S(1)} %add_convert_fusion), channel_id=1, source_target_pairs={{0,128},{128,0},{1,129},{129,1},{2,130},{130,2},{3,131},{131,3},{4... | collective-permute-start | bytes 196616 | tf_op jit(solution)/shard_map/ppermute | solution.py:390
  46.5 4.3 %collective-permute-done.2 = bf16[16,16,128]{2,1,0:T(8,128)(2,1)S(1)} collective-permute-done((bf16[16,16,128]{2,1,0:T(8,128)(2,1)S(1)}, bf16[16,16,128]{2,1,0:T(8,128)(2,1)S(1)}, u32[]{:S(2)}, u32[]{:S(2)}) %collective-permute-start.2) | collective-permute-done | bytes 65568 | tf_op jit(solution)/shard_map/ppermute | solution.py:390
  50.9 0.1 pad_maximum_fusion
  51.0 0.0 copy-start
  51.0 0.0 copy-start.1
  51.0 0.0 copy-start.2
  51.0 0.0 copy-start.3
  51.0 16.9 %all_to_all.11.back = bf16[32,96,128]{2,1,0:T(8,128)(2,1)S(1)} all-to-all(bf16[32,96,128]{2,1,0:T(8,128)(2,1)S(1)} %pad_maximum_fusion), channel_id=1, replica_groups=mesh['dh'=2,'dm'=2,'pl'=2,'chan'=4,'seq'=16] {'pl','seq'}, dimensions={0} | all-to-all | bytes 1572864 | tf_op jit(solution)/shard_map/all_to_all | solution.py:385
  67.9 0.0 copy-done
  67.9 0.0 copy-done.1
  67.9 0.0 copy-done.2
  67.9 0.0 copy-done.3
  67.9 1.3 %shard_map.186 = (bf16[128,1024]{1,0:T(8,128)(2,1)}, bf16[128,1024]{1,0:T(8,128)(2,1)}, bf16[128,1024]{1,0:T(8,128)(2,1)}, bf16[128,1024]{1,0:T(8,128)(2,1)}, bf16[128,1024]{1,0:T(8,128)(2,1)}) custom-call(bf16[32,96,128]{2,1,0:T(8,128)(2,1)S(1)} %all_to_all.11.back, bf16[128,1024]{1,0:T(8,128)(2,1)S(1)} %bitcast.12, bf16[128,1024]{1,0:T(8,128)(2,1)S(1)} %bitcast.14, ...), custom_call_target="tpu_custom_call" | custom-call | bytes 2097152 | tf_op jit(solution)/shard_map/pallas_call | solution.py:310
  (4 shorter events, 0.1 us)
Async XLA Ops:
  2.3 21.5 %copy-start.5 = (bf16[2,256,256]{2,1,0:T(8,128)(2,1)S(1)}, bf16[2,256,256]{2,1,0:T(8,128)(2,1)}, u32[]{:S(2)}) copy-start(bf16[2,256,256]{2,1,0:T(8,128)(2,1)} %constant.9.clone.back_lane_ref) | copy-start | bytes 786436
  2.3 21.5 %copy-start.6 = (bf16[2,256,256]{2,1,0:T(8,128)(2,1)S(1)}, bf16[2,256,256]{2,1,0:T(8,128)(2,1)}, u32[]{:S(2)}) copy-start(bf16[2,256,256]{2,1,0:T(8,128)(2,1)} %constant.8.clone.lane_ref) | copy-start | bytes 786436
  2.3 21.5 %copy-start.8 = (f32[17,4,128]{2,1,0:T(4,128)S(1)}, f32[17,4,128]{2,1,0:T(4,128)}, u32[]{:S(2)}) copy-start(f32[17,4,128]{2,1,0:T(4,128)} %constant.10.clone.twist_ref) | copy-start | bytes 104452
  25.0 16.3 %copy-start.4 = (f32[1024]{0:T(1024)S(1)}, f32[1024]{0:T(1024)}, u32[]{:S(2)}) copy-start(f32[1024]{0:T(1024)} %param.19) | copy-start | bytes 12292
  25.0 16.3 %copy-start.7 = (f32[17,4,128]{2,1,0:T(4,128)S(1)}, f32[17,4,128]{2,1,0:T(4,128)}, u32[]{:S(2)}) copy-start(f32[17,4,128]{2,1,0:T(4,128)} %constant.11.clone.twist_ref) | copy-start | bytes 104452
  25.0 7.2 %collective-permute-start = (bf16[16,16,128]{2,1,0:T(8,128)(2,1)S(1)}, bf16[16,16,128]{2,1,0:T(8,128)(2,1)S(1)}, u32[]{:S(2)}, u32[]{:S(2)}) collective-permute-start(bf16[16,16,128]{2,1,0:T(8,128)(2,1)S(1)} %get-tuple-element.19), channel_id=1, source_target_pairs={{0,128},{128,0},{1,129},{129,1},{2,130},{130,2},{3,131},{131,3},{4... | collective-permute-start | bytes 196616 | tf_op jit(solution)/shard_map/ppermute | solution.py:390
  32.2 11.6 %collective-permute-start.1 = (bf16[16,16,128]{2,1,0:T(8,128)(2,1)S(1)}, bf16[16,16,128]{2,1,0:T(8,128)(2,1)S(1)}, u32[]{:S(2)}, u32[]{:S(2)}) collective-permute-start(bf16[16,16,128]{2,1,0:T(8,128)(2,1)S(1)} %add_convert_fusion.1), channel_id=1, source_target_pairs={{0,256},{256,0},{1,257},{257,1},{2,258},{258,2},{3,259},{259,3},{4... | collective-permute-start | bytes 196616 | tf_op jit(solution)/shard_map/ppermute | solution.py:390
  43.8 7.1 %collective-permute-start.2 = (bf16[16,16,128]{2,1,0:T(8,128)(2,1)S(1)}, bf16[16,16,128]{2,1,0:T(8,128)(2,1)S(1)}, u32[]{:S(2)}, u32[]{:S(2)}) collective-permute-start(bf16[16,16,128]{2,1,0:T(8,128)(2,1)S(1)} %add_convert_fusion), channel_id=1, source_target_pairs={{0,128},{128,0},{1,129},{129,1},{2,130},{130,2},{3,131},{131,3},{4... | collective-permute-start | bytes 196616 | tf_op jit(solution)/shard_map/ppermute | solution.py:390
  51.0 16.9 %copy-start = (bf16[1,128,1024]{2,1,0:T(8,128)(2,1)S(1)}, bf16[1,128,1024]{2,1,0:T(8,128)(2,1)}, u32[]{:S(2)}) copy-start(bf16[1,128,1024]{2,1,0:T(8,128)(2,1)} %param.15) | copy-start | bytes 786436
  51.0 16.9 %copy-start.1 = (bf16[1,128,1024]{2,1,0:T(8,128)(2,1)S(1)}, bf16[1,128,1024]{2,1,0:T(8,128)(2,1)}, u32[]{:S(2)}) copy-start(bf16[1,128,1024]{2,1,0:T(8,128)(2,1)} %param.16) | copy-start | bytes 786436
  51.0 16.9 %copy-start.2 = (bf16[1,128,1024]{2,1,0:T(8,128)(2,1)S(1)}, bf16[1,128,1024]{2,1,0:T(8,128)(2,1)}, u32[]{:S(2)}) copy-start(bf16[1,128,1024]{2,1,0:T(8,128)(2,1)} %param.17) | copy-start | bytes 786436
  51.0 16.9 %copy-start.3 = (bf16[1,128,1024]{2,1,0:T(8,128)(2,1)S(1)}, bf16[1,128,1024]{2,1,0:T(8,128)(2,1)}, u32[]{:S(2)}) copy-start(bf16[1,128,1024]{2,1,0:T(8,128)(2,1)} %param.20) | copy-start | bytes 786436

commit v7 on v6

--- a/solution.py
+++ b/solution.py
@@ -14,6 +14,7 @@
 BF16 = jnp.bfloat16
 LANES = 128
 ROWS = 16
+SIDE = 4
 FREQS = 2 * ROWS
 HALF = ROWS + 1
 CHUNK = 16
@@ -223,6 +224,10 @@
     return real_inverse(freqs, FREQS, True)
 
 
+def slot(row):
+    return row % SIDE * SIDE + row // SIDE
+
+
 def half_start(kept):
     mine = lax.axis_index("dm")
     return pl.multiple_of((mine if kept else 1 - mine) * CHUNK, CHUNK)
@@ -237,14 +242,14 @@
         place = pl.ds(pl.multiple_of(which * chans + first, CHUNK), CHUNK)
         for b in range(batch):
             rows[which, b] = spectrum(
-                lambda r: signals[b * ROWS + r, place, :].astype(F32), twist_ref, lane_ref
+                lambda r: signals[b * ROWS + slot(r), place, :].astype(F32), twist_ref, lane_ref
             )
             spec_ref[which * batch + b] = rows[which, b]
     product = conj_product(rows[0, 0], rows[1, 0])
     for b in range(1, batch):
         product = product + conj_product(rows[0, b], rows[1, b])
     for r, row in enumerate(signal_rows(product, twist_ref, back_lane_ref)):
-        out[r] = row.astype(BF16)
+        out[slot(r)] = row.astype(BF16)
 
 
 def state_kernel(signals, gain_ref, lane_ref, back_lane_ref, twist_ref, *refs):
@@ -252,7 +257,7 @@
     batch = signals.shape[0] // ROWS
     chans = out.shape[1] // 2
     share = signals.shape[1] - 2 * chans
-    place = lax.axis_index("pl") * lax.axis_size("seq") + lax.axis_index("seq")
+    place = (lax.axis_index("pl") * SIDE + lax.axis_index("x")) * SIDE + lax.axis_index("y")
     pieces = LANES // chans
     gains = jnp.broadcast_to(gain_ref[pl.ds(place // pieces, 1), :], (LANES, LANES))
     skip_ref[...] = gains.T
@@ -261,7 +266,7 @@
         first = half_start(kept)
         source = first // share
         taps = spectrum(
-            lambda r: signals[source * ROWS + r, pl.ds(2 * chans, CHUNK), :].astype(F32),
+            lambda r: signals[source * ROWS + slot(r), pl.ds(2 * chans, CHUNK), :].astype(F32),
             twist_ref,
             lane_ref,
         )
@@ -271,8 +276,8 @@
             for b in range(batch):
                 spec = product(taps, spec_ref[which * batch + b])
                 for r, row in enumerate(signal_rows(spec, twist_ref, back_lane_ref)):
-                    own = signals[b * ROWS + r, place, :].astype(F32)
-                    out[b * ROWS + r, place, :] = (row + skip * own).astype(BF16)
+                    own = signals[b * ROWS + slot(r), place, :].astype(F32)
+                    out[b * ROWS + slot(r), place, :] = (row + skip * own).astype(BF16)
 
 
 def output_kernel(back, query, key, value, grad, *refs):
@@ -373,7 +378,7 @@
 
 
 def on_device(query_in, key_in, value_in, filter_taps, skip_gain, grad_out):
-    seq_count, pair = lax.axis_size("seq"), lax.axis_size("pl")
+    seq_count, pair = lax.axis_size("y") * lax.axis_size("x"), lax.axis_size("pl")
     peers = seq_count * pair
     rows_dev, chan_dev = query_in.shape[1:]
     own = chan_dev // peers
@@ -384,7 +389,7 @@
     def swap(values, axes):
         return lax.all_to_all(values, axes, split_axis=0, concat_axis=0, tiled=True)
 
-    signals = swap(gate(query, key, value, grad, filter_taps, peers), ("pl", "seq"))
+    signals = swap(gate(query, key, value, grad, filter_taps, peers), ("pl", "x", "y"))
 
     def exchange(values, axis):
         return lax.ppermute(values, axis, [(0, 1), (1, 0)])
@@ -403,7 +408,7 @@
         jnp.broadcast_to(t[None], (pair,) + t.shape).reshape((peers,) + t.shape[1:])
         for t in (term, exchange(term, "dm"))
     ]
-    back = swap(jnp.concatenate([results, *copies], axis=1), ("pl", "seq"))
+    back = swap(jnp.concatenate([results, *copies], axis=1), ("pl", "x", "y"))
     outs = outputs(back, query, key, value, grad)
     return tuple(out[None] for out in outs[:4]) + (outs[4],)
 
@@ -411,10 +416,11 @@
 def solution(mesh):
     dp, chan, seq = (mesh.shape[name] for name in ("dp", "chan", "seq"))
     split_mesh = Mesh(
-        mesh.devices.reshape(dp // 4, 2, 2, chan, seq), ("dh", "dm", "pl", "chan", "seq")
-    )
-    rows = P(("dh", "dm", "pl"), "seq", "chan")
-    taps = P("seq", "chan")
+        mesh.devices.reshape(dp // 4, 2, 2, chan, seq // SIDE, SIDE),
+        ("dh", "dm", "pl", "chan", "y", "x"),
+    )
+    rows = P(("dh", "dm", "pl"), ("y", "x"), "chan")
+    taps = P(("y", "x"), "chan")
     return jax.shard_map(
         on_device,
         mesh=split_mesh,

time: 69.6 us -> 69.7 us (level)
  waiting for transfers between devices: 8.66 us -> 9.48 us
  starting transfers between devices: 13.7 us -> 12.9 us
    ppermute x3, waiting for transfers between devices: 8.66 us -> 9.48 us  [exchange(): return lax.ppermute(values, axis, [(0, 1), (1, 0)])]
    ppermute x3, starting transfers between devices: 13.7 us -> 12.9 us  [exchange(): return lax.ppermute(values, axis, [(0, 1), (1, 0)])]
where the time goes in v7:
time: 69.7 us; the launch traced here: 69.4 us
  blocking collectives  38.4 us (55%)
  starting transfers between devices  12.9 us (19%)
  waiting for transfers between devices  9.48 us (14%)
  Pallas kernels  7.55 us (11%)
  between operations  0.82 us (1%)
    all_to_all x2, blocking collectives, swap(): return lax.all_to_all(values, axes, split_axis=0, concat_axis=0, tiled=True)  38.4 us
    ppermute x3, starting transfers between devices, exchange(): return lax.ppermute(values, axis, [(0, 1), (1, 0)])  12.9 us
    ppermute x3, waiting for transfers between devices, exchange(): return lax.ppermute(values, axis, [(0, 1), (1, 0)])  9.48 us
    pallas_call x5, Pallas kernels, call(): pl.pallas_call(kernel, out_shape=shapes, in_specs=[place(in_hbm)] * len(a...  7.55 us
  transfers between devices with their start and end apart: 3, of which 3 were waited for; matrix products, arithmetic and copies ran while one was open for 0% of the time, Pallas kernels for 5%

profile of v7, /device:TPU:64, one launch (start us, length us, event | category | flops | bytes accessed | tf_op | source)
XLA Modules:
  0.0 69.4 jit_solution(6589050444900089957)
XLA Ops:
  0.6 1.6 %shard_map.182 = bf16[32,80,128]{2,1,0:T(8,128)(2,1)S(1)} custom-call(bf16[128,1024]{1,0:T(8,128)(2,1)} %bitcast.11, bf16[128,1024]{1,0:T(8,128)(2,1)} %bitcast.13, bf16[128,1024]{1,0:T(8,128)(2,1)} %bitcast.15, bf16[128,1024]{1,0:T(8,128)(2,1)} %bitcast.17, bf16[128,1024]{1,0:T(8,128)(2,1)} %taps.1), custom_call_target="tpu_custom_call" | custom-call | bytes 2097152 | tf_op jit(solution)/shard_map/pallas_call | solution.py:315
  2.3 0.0 copy-start.5
  2.3 0.0 copy-start.6
  2.3 0.0 copy-start.8
  2.3 21.3 %all_to_all.10.signals = bf16[32,80,128]{2,1,0:T(8,128)(2,1)S(1)} all-to-all(bf16[32,80,128]{2,1,0:T(8,128)(2,1)S(1)} %shard_map.182), channel_id=1, replica_groups=mesh['dh'=2,'dm'=2,'pl'=2,'chan'=4,'y'=4,'x'=4] {'pl','x','y'}, dimensions={0} | all-to-all | bytes 1310720 | tf_op jit(solution)/shard_map/all_to_all | solution.py:390
  23.6 0.0 copy-done.5
  23.6 0.0 copy-done.6
  23.6 0.0 copy-done.8
  23.7 1.2 %shard_map.184 = (f32[4,272,256]{2,1,0:T(8,128)S(1)}, bf16[16,16,128]{2,1,0:T(8,128)(2,1)S(1)}) custom-call(bf16[32,80,128]{2,1,0:T(8,128)(2,1)S(1)} %all_to_all.10.signals, bf16[2,256,256]{2,1,0:T(8,128)(2,1)S(1)} %copy-done.6, bf16[2,256,256]{2,1,0:T(8,128)(2,1)S(1)} %copy-done.5, f32[17,4,128]{2,1,0:T(4,128)S(1)} %copy-done.8), custom_call_target="tpu_custom_call" | custom-call | flops 2000000000 | bytes 2097152 | tf_op jit(solution)/shard_map/pallas_call | solution.py:315
  24.9 0.0 copy-start.4
  24.9 0.0 copy-start.7
  24.9 1.9 %collective-permute-start = (bf16[16,16,128]{2,1,0:T(8,128)(2,1)S(1)}, bf16[16,16,128]{2,1,0:T(8,128)(2,1)S(1)}, u32[]{:S(2)}, u32[]{:S(2)}) collective-permute-start(bf16[16,16,128]{2,1,0:T(8,128)(2,1)S(1)} %get-tuple-element.19), channel_id=1, source_target_pairs={{0,128},{128,0},{1,129},{129,1},{2,130},{130,2},{3,131},{131,3},{4... | collective-permute-start | bytes 196616 | tf_op jit(solution)/shard_map/ppermute | solution.py:395
  26.8 1.2 %shard_map.183 = (f32[4,272,256]{2,1,0:T(8,128)S(1)}, bf16[16,16,128]{2,1,0:T(8,128)(2,1)S(1)}) custom-call(bf16[32,80,128]{2,1,0:T(8,128)(2,1)S(1)} %all_to_all.10.signals, bf16[2,256,256]{2,1,0:T(8,128)(2,1)S(1)} %copy-done.6, bf16[2,256,256]{2,1,0:T(8,128)(2,1)S(1)} %copy-done.5, f32[17,4,128]{2,1,0:T(4,128)S(1)} %copy-done.8), custom_call_target="tpu_custom_call" | custom-call | flops 2000000000 | bytes 2097152 | tf_op jit(solution)/shard_map/pallas_call | solution.py:315
  28.0 4.0 %collective-permute-done = bf16[16,16,128]{2,1,0:T(8,128)(2,1)S(1)} collective-permute-done((bf16[16,16,128]{2,1,0:T(8,128)(2,1)S(1)}, bf16[16,16,128]{2,1,0:T(8,128)(2,1)S(1)}, u32[]{:S(2)}, u32[]{:S(2)}) %collective-permute-start) | collective-permute-done | bytes 65568 | tf_op jit(solution)/shard_map/ppermute | solution.py:395
  32.1 9.1 %collective-permute-start.1 = (bf16[16,16,128]{2,1,0:T(8,128)(2,1)S(1)}, bf16[16,16,128]{2,1,0:T(8,128)(2,1)S(1)}, u32[]{:S(2)}, u32[]{:S(2)}) collective-permute-start(bf16[16,16,128]{2,1,0:T(8,128)(2,1)S(1)} %add_convert_fusion.1), channel_id=1, source_target_pairs={{0,256},{256,0},{1,257},{257,1},{2,258},{258,2},{3,259},{259,3},{4... | collective-permute-start | bytes 196616 | tf_op jit(solution)/shard_map/ppermute | solution.py:395
  41.2 0.0 copy-done.4
  41.2 0.0 copy-done.7
  41.2 2.2 %shard_map.185 = bf16[32,64,128]{2,1,0:T(8,128)(2,1)S(1)} custom-call(bf16[32,80,128]{2,1,0:T(8,128)(2,1)S(1)} %all_to_all.10.signals, f32[8,128]{1,0:T(8,128)S(1)} %bitcast.19, bf16[2,256,256]{2,1,0:T(8,128)(2,1)S(1)} %copy-done.6, bf16[2,256,256]{2,1,0:T(8,128)(2,1)S(1)} %copy-done.5, f32[17,4,128]{2,1,0:T(4,128)S(1)} %copy-done.7, ...), custom_call_target="tpu_custom_call" | custom-call | flops 3000000000 | bytes 2097152 | tf_op jit(solution)/shard_map/pallas_call | solution.py:315
  43.4 0.3 collective-permute-done.1
  43.7 1.9 %collective-permute-start.2 = (bf16[16,16,128]{2,1,0:T(8,128)(2,1)S(1)}, bf16[16,16,128]{2,1,0:T(8,128)(2,1)S(1)}, u32[]{:S(2)}, u32[]{:S(2)}) collective-permute-start(bf16[16,16,128]{2,1,0:T(8,128)(2,1)S(1)} %add_convert_fusion), channel_id=1, source_target_pairs={{0,128},{128,0},{1,129},{129,1},{2,130},{130,2},{3,131},{131,3},{4... | collective-permute-start | bytes 196616 | tf_op jit(solution)/shard_map/ppermute | solution.py:395
  45.6 5.1 %collective-permute-done.2 = bf16[16,16,128]{2,1,0:T(8,128)(2,1)S(1)} collective-permute-done((bf16[16,16,128]{2,1,0:T(8,128)(2,1)S(1)}, bf16[16,16,128]{2,1,0:T(8,128)(2,1)S(1)}, u32[]{:S(2)}, u32[]{:S(2)}) %collective-permute-start.2) | collective-permute-done | bytes 65568 | tf_op jit(solution)/shard_map/ppermute | solution.py:395
  50.8 0.1 pad_maximum_fusion
  50.9 0.0 copy-start
  50.9 0.0 copy-start.1
  50.9 0.0 copy-start.2
  50.9 0.0 copy-start.3
  50.9 17.1 %all_to_all.11.back = bf16[32,96,128]{2,1,0:T(8,128)(2,1)S(1)} all-to-all(bf16[32,96,128]{2,1,0:T(8,128)(2,1)S(1)} %pad_maximum_fusion), channel_id=1, replica_groups=mesh['dh'=2,'dm'=2,'pl'=2,'chan'=4,'y'=4,'x'=4] {'pl','x','y'}, dimensions={0} | all-to-all | bytes 1572864 | tf_op jit(solution)/shard_map/all_to_all | solution.py:390
  68.0 0.0 copy-done
  68.0 0.0 copy-done.1
  68.0 0.0 copy-done.2
  68.0 0.0 copy-done.3
  68.0 1.3 %shard_map.186 = (bf16[128,1024]{1,0:T(8,128)(2,1)}, bf16[128,1024]{1,0:T(8,128)(2,1)}, bf16[128,1024]{1,0:T(8,128)(2,1)}, bf16[128,1024]{1,0:T(8,128)(2,1)}, bf16[128,1024]{1,0:T(8,128)(2,1)}) custom-call(bf16[32,96,128]{2,1,0:T(8,128)(2,1)S(1)} %all_to_all.11.back, bf16[128,1024]{1,0:T(8,128)(2,1)S(1)} %bitcast.12, bf16[128,1024]{1,0:T(8,128)(2,1)S(1)} %bitcast.14, ...), custom_call_target="tpu_custom_call" | custom-call | bytes 2097152 | tf_op jit(solution)/shard_map/pallas_call | solution.py:315
  (4 shorter events, 0.1 us)
Async XLA Ops:
  2.3 21.4 %copy-start.5 = (bf16[2,256,256]{2,1,0:T(8,128)(2,1)S(1)}, bf16[2,256,256]{2,1,0:T(8,128)(2,1)}, u32[]{:S(2)}) copy-start(bf16[2,256,256]{2,1,0:T(8,128)(2,1)} %constant.9.clone.back_lane_ref) | copy-start | bytes 786436
  2.3 21.4 %copy-start.6 = (bf16[2,256,256]{2,1,0:T(8,128)(2,1)S(1)}, bf16[2,256,256]{2,1,0:T(8,128)(2,1)}, u32[]{:S(2)}) copy-start(bf16[2,256,256]{2,1,0:T(8,128)(2,1)} %constant.8.clone.lane_ref) | copy-start | bytes 786436
  2.3 21.4 %copy-start.8 = (f32[17,4,128]{2,1,0:T(4,128)S(1)}, f32[17,4,128]{2,1,0:T(4,128)}, u32[]{:S(2)}) copy-start(f32[17,4,128]{2,1,0:T(4,128)} %constant.10.clone.twist_ref) | copy-start | bytes 104452
  24.9 16.3 %copy-start.4 = (f32[1024]{0:T(1024)S(1)}, f32[1024]{0:T(1024)}, u32[]{:S(2)}) copy-start(f32[1024]{0:T(1024)} %param.19) | copy-start | bytes 12292
  24.9 16.3 %copy-start.7 = (f32[17,4,128]{2,1,0:T(4,128)S(1)}, f32[17,4,128]{2,1,0:T(4,128)}, u32[]{:S(2)}) copy-start(f32[17,4,128]{2,1,0:T(4,128)} %constant.11.clone.twist_ref) | copy-start | bytes 104452
  24.9 7.2 %collective-permute-start = (bf16[16,16,128]{2,1,0:T(8,128)(2,1)S(1)}, bf16[16,16,128]{2,1,0:T(8,128)(2,1)S(1)}, u32[]{:S(2)}, u32[]{:S(2)}) collective-permute-start(bf16[16,16,128]{2,1,0:T(8,128)(2,1)S(1)} %get-tuple-element.19), channel_id=1, source_target_pairs={{0,128},{128,0},{1,129},{129,1},{2,130},{130,2},{3,131},{131,3},{4... | collective-permute-start | bytes 196616 | tf_op jit(solution)/shard_map/ppermute | solution.py:395
  32.1 11.6 %collective-permute-start.1 = (bf16[16,16,128]{2,1,0:T(8,128)(2,1)S(1)}, bf16[16,16,128]{2,1,0:T(8,128)(2,1)S(1)}, u32[]{:S(2)}, u32[]{:S(2)}) collective-permute-start(bf16[16,16,128]{2,1,0:T(8,128)(2,1)S(1)} %add_convert_fusion.1), channel_id=1, source_target_pairs={{0,256},{256,0},{1,257},{257,1},{2,258},{258,2},{3,259},{259,3},{4... | collective-permute-start | bytes 196616 | tf_op jit(solution)/shard_map/ppermute | solution.py:395
  43.7 7.1 %collective-permute-start.2 = (bf16[16,16,128]{2,1,0:T(8,128)(2,1)S(1)}, bf16[16,16,128]{2,1,0:T(8,128)(2,1)S(1)}, u32[]{:S(2)}, u32[]{:S(2)}) collective-permute-start(bf16[16,16,128]{2,1,0:T(8,128)(2,1)S(1)} %add_convert_fusion), channel_id=1, source_target_pairs={{0,128},{128,0},{1,129},{129,1},{2,130},{130,2},{3,131},{131,3},{4... | collective-permute-start | bytes 196616 | tf_op jit(solution)/shard_map/ppermute | solution.py:395
  50.9 17.1 %copy-start = (bf16[1,128,1024]{2,1,0:T(8,128)(2,1)S(1)}, bf16[1,128,1024]{2,1,0:T(8,128)(2,1)}, u32[]{:S(2)}) copy-start(bf16[1,128,1024]{2,1,0:T(8,128)(2,1)} %param.15) | copy-start | bytes 786436
  50.9 17.1 %copy-start.1 = (bf16[1,128,1024]{2,1,0:T(8,128)(2,1)S(1)}, bf16[1,128,1024]{2,1,0:T(8,128)(2,1)}, u32[]{:S(2)}) copy-start(bf16[1,128,1024]{2,1,0:T(8,128)(2,1)} %param.16) | copy-start | bytes 786436
  50.9 17.1 %copy-start.2 = (bf16[1,128,1024]{2,1,0:T(8,128)(2,1)S(1)}, bf16[1,128,1024]{2,1,0:T(8,128)(2,1)}, u32[]{:S(2)}) copy-start(bf16[1,128,1024]{2,1,0:T(8,128)(2,1)} %param.17) | copy-start | bytes 786436
  50.9 17.1 %copy-start.3 = (bf16[1,128,1024]{2,1,0:T(8,128)(2,1)S(1)}, bf16[1,128,1024]{2,1,0:T(8,128)(2,1)}, u32[]{:S(2)}) copy-start(bf16[1,128,1024]{2,1,0:T(8,128)(2,1)} %param.20) | copy-start | bytes 786436

commit v8 on v7

--- a/solution.py
+++ b/solution.py
@@ -285,18 +285,15 @@
     own = back.shape[1] // 3
     pieces = LANES // own
     width = query.shape[1] // GROUPS
-    places = (half_start(1), half_start(0))
-    halves = [pl.ds(pl.multiple_of(2 * own + place, CHUNK), CHUNK) for place in places]
     sent = []
     for group in range(GROUPS):
         for tile in range(group * width // LANES, (group + 1) * width // LANES):
             cols = pl.ds(tile * LANES, LANES)
             blocks = [tile * pieces + i for i in range(pieces)]
-            state, dmixed = (
+            state, dmixed, term = (
                 jnp.concatenate([back[i, pl.ds(which * own, own), :] for i in blocks], axis=0).T
-                for which in range(2)
+                for which in range(3)
             )
-            term = jnp.concatenate([back[i, half, :] for i in blocks for half in halves], axis=0).T
             state, dmixed = state.astype(F32), dmixed.astype(F32)
             held[0][:, cols] = (query[:, cols].astype(F32) * state).astype(BF16)
             held[1][:, cols] = (grad[:, cols].astype(F32) * state).astype(BF16)
@@ -404,10 +401,8 @@
     results = states(signals, spectra, skip_gain, own)
     other, results = lax.optimization_barrier((other, results))
     term = plus(term, other)
-    copies = [
-        jnp.broadcast_to(t[None], (pair,) + t.shape).reshape((peers,) + t.shape[1:])
-        for t in (term, exchange(term, "dm"))
-    ]
+    halves = lax.all_gather(term, "dm")
+    copies = [jnp.broadcast_to(t[None], (pair,) + t.shape).reshape((peers,) + t.shape[1:]) for t in halves]
     back = swap(jnp.concatenate([results, *copies], axis=1), ("pl", "x", "y"))
     outs = outputs(back, query, key, value, grad)
     return tuple(out[None] for out in outs[:4]) + (outs[4],)

time: 69.7 us -> 68.5 us (0.983)
  blocking collectives: 38.4 us -> 44.2 us
  waiting for transfers between devices: 9.48 us -> 4.4 us
  starting transfers between devices: 12.9 us -> 11 us
    all_gather x0 -> x1, blocking collectives: none -> 5.84 us  [on_device(): halves = lax.all_gather(term, 'dm')]
    ppermute x3 -> x2, waiting for transfers between devices: 9.48 us -> 4.4 us  [exchange(): return lax.ppermute(values, axis, [(0, 1), (1, 0)])]
    ppermute x3 -> x2, starting transfers between devices: 12.9 us -> 11 us  [exchange(): return lax.ppermute(values, axis, [(0, 1), (1, 0)])]
  transfers between devices with their start and end apart: 3 -> 2, of which waited for: 3 -> 2; matrix products, arithmetic and copies ran while one was open for 0% -> 0% of each run, Pallas kernels for 5% -> 5%
where the time goes in v8:
time: 68.5 us; the launch traced here: 68.2 us
  blocking collectives  44.2 us (65%)
  starting transfers between devices  11 us (16%)
  Pallas kernels  7.55 us (11%)
  waiting for transfers between devices  4.4 us (6%)
  between operations  0.82 us (1%)
    all_to_all x2, blocking collectives, swap(): return lax.all_to_all(values, axes, split_axis=0, concat_axis=0, tiled=True)  38.4 us
    ppermute x2, starting transfers between devices, exchange(): return lax.ppermute(values, axis, [(0, 1), (1, 0)])  11 us
    pallas_call x5, Pallas kernels, call(): pl.pallas_call(kernel, out_shape=shapes, in_specs=[place(in_hbm)] * len(a...  7.55 us
    all_gather x1, blocking collectives, on_device(): halves = lax.all_gather(term, 'dm')  5.84 us
    ppermute x2, waiting for transfers between devices, exchange(): return lax.ppermute(values, axis, [(0, 1), (1, 0)])  4.4 us
  transfers between devices with their start and end apart: 2, of which 2 were waited for; matrix products, arithmetic and copies ran while one was open for 0% of the time, Pallas kernels for 5%

profile of v8, /device:TPU:64, one launch (start us, length us, event | category | flops | bytes accessed | tf_op | source)
XLA Modules:
  0.0 68.2 jit_solution(2182987561064731277)
XLA Ops:
  0.6 1.6 %shard_map.182 = bf16[32,80,128]{2,1,0:T(8,128)(2,1)S(1)} custom-call(bf16[128,1024]{1,0:T(8,128)(2,1)} %bitcast.11, bf16[128,1024]{1,0:T(8,128)(2,1)} %bitcast.13, bf16[128,1024]{1,0:T(8,128)(2,1)} %bitcast.15, bf16[128,1024]{1,0:T(8,128)(2,1)} %bitcast.17, bf16[128,1024]{1,0:T(8,128)(2,1)} %taps.1), custom_call_target="tpu_custom_call" | custom-call | bytes 2097152 | tf_op jit(solution)/shard_map/pallas_call | solution.py:312
  2.3 0.0 copy-start.5
  2.3 0.0 copy-start.6
  2.3 0.0 copy-start.8
  2.3 21.3 %all_to_all.10.signals = bf16[32,80,128]{2,1,0:T(8,128)(2,1)S(1)} all-to-all(bf16[32,80,128]{2,1,0:T(8,128)(2,1)S(1)} %shard_map.182), channel_id=1, replica_groups=mesh['dh'=2,'dm'=2,'pl'=2,'chan'=4,'y'=4,'x'=4] {'pl','x','y'}, dimensions={0} | all-to-all | bytes 1310720 | tf_op jit(solution)/shard_map/all_to_all | solution.py:387
  23.6 0.0 copy-done.5
  23.6 0.0 copy-done.6
  23.6 0.0 copy-done.8
  23.7 1.2 %shard_map.184 = (f32[4,272,256]{2,1,0:T(8,128)S(1)}, bf16[16,16,128]{2,1,0:T(8,128)(2,1)S(1)}) custom-call(bf16[32,80,128]{2,1,0:T(8,128)(2,1)S(1)} %all_to_all.10.signals, bf16[2,256,256]{2,1,0:T(8,128)(2,1)S(1)} %copy-done.6, bf16[2,256,256]{2,1,0:T(8,128)(2,1)S(1)} %copy-done.5, f32[17,4,128]{2,1,0:T(4,128)S(1)} %copy-done.8), custom_call_target="tpu_custom_call" | custom-call | flops 2000000000 | bytes 2097152 | tf_op jit(solution)/shard_map/pallas_call | solution.py:312
  24.9 0.0 copy-start.4
  24.9 0.0 copy-start.7
  24.9 1.9 %collective-permute-start = (bf16[16,16,128]{2,1,0:T(8,128)(2,1)S(1)}, bf16[16,16,128]{2,1,0:T(8,128)(2,1)S(1)}, u32[]{:S(2)}, u32[]{:S(2)}) collective-permute-start(bf16[16,16,128]{2,1,0:T(8,128)(2,1)S(1)} %get-tuple-element.19), channel_id=1, source_target_pairs={{0,128},{128,0},{1,129},{129,1},{2,130},{130,2},{3,131},{131,3},{4... | collective-permute-start | bytes 196616 | tf_op jit(solution)/shard_map/ppermute | solution.py:392
  26.8 1.2 %shard_map.183 = (f32[4,272,256]{2,1,0:T(8,128)S(1)}, bf16[16,16,128]{2,1,0:T(8,128)(2,1)S(1)}) custom-call(bf16[32,80,128]{2,1,0:T(8,128)(2,1)S(1)} %all_to_all.10.signals, bf16[2,256,256]{2,1,0:T(8,128)(2,1)S(1)} %copy-done.6, bf16[2,256,256]{2,1,0:T(8,128)(2,1)S(1)} %copy-done.5, f32[17,4,128]{2,1,0:T(4,128)S(1)} %copy-done.8), custom_call_target="tpu_custom_call" | custom-call | flops 2000000000 | bytes 2097152 | tf_op jit(solution)/shard_map/pallas_call | solution.py:312
  28.0 4.0 %collective-permute-done = bf16[16,16,128]{2,1,0:T(8,128)(2,1)S(1)} collective-permute-done((bf16[16,16,128]{2,1,0:T(8,128)(2,1)S(1)}, bf16[16,16,128]{2,1,0:T(8,128)(2,1)S(1)}, u32[]{:S(2)}, u32[]{:S(2)}) %collective-permute-start) | collective-permute-done | bytes 65568 | tf_op jit(solution)/shard_map/ppermute | solution.py:392
  32.1 9.1 %collective-permute-start.1 = (bf16[16,16,128]{2,1,0:T(8,128)(2,1)S(1)}, bf16[16,16,128]{2,1,0:T(8,128)(2,1)S(1)}, u32[]{:S(2)}, u32[]{:S(2)}) collective-permute-start(bf16[16,16,128]{2,1,0:T(8,128)(2,1)S(1)} %add_convert_fusion.1), channel_id=1, source_target_pairs={{0,256},{256,0},{1,257},{257,1},{2,258},{258,2},{3,259},{259,3},{4... | collective-permute-start | bytes 196616 | tf_op jit(solution)/shard_map/ppermute | solution.py:392
  41.2 0.0 copy-done.4
  41.2 0.0 copy-done.7
  41.2 2.2 %shard_map.185 = bf16[32,64,128]{2,1,0:T(8,128)(2,1)S(1)} custom-call(bf16[32,80,128]{2,1,0:T(8,128)(2,1)S(1)} %all_to_all.10.signals, f32[8,128]{1,0:T(8,128)S(1)} %bitcast.19, bf16[2,256,256]{2,1,0:T(8,128)(2,1)S(1)} %copy-done.6, bf16[2,256,256]{2,1,0:T(8,128)(2,1)S(1)} %copy-done.5, f32[17,4,128]{2,1,0:T(4,128)S(1)} %copy-done.7, ...), custom_call_target="tpu_custom_call" | custom-call | flops 3000000000 | bytes 2097152 | tf_op jit(solution)/shard_map/pallas_call | solution.py:312
  43.4 0.4 collective-permute-done.1
  43.8 5.8 %all-gather = bf16[32,16,128]{2,1,0:T(8,128)(2,1)S(1)} all-gather(bf16[16,16,128]{2,1,0:T(8,128)(2,1)S(1)} %add_convert_fusion), channel_id=2, replica_groups=mesh['dh'=2,'dm'=2,'pl'=2,'chan'=4,'y'=4,'x'=4] {'dm'}, dimensions={0}, use_global_device_ids=true | all-gather | bytes 196608 | tf_op jit(solution)/shard_map/all_gather | solution.py:404
  49.7 0.1 pad_maximum_fusion
  49.7 0.0 copy-start
  49.8 0.0 copy-start.1
  49.8 0.0 copy-start.2
  49.8 0.0 copy-start.3
  49.8 17.0 %all_to_all.11.back = bf16[32,96,128]{2,1,0:T(8,128)(2,1)S(1)} all-to-all(bf16[32,96,128]{2,1,0:T(8,128)(2,1)S(1)} %pad_maximum_fusion), channel_id=1, replica_groups=mesh['dh'=2,'dm'=2,'pl'=2,'chan'=4,'y'=4,'x'=4] {'pl','x','y'}, dimensions={0} | all-to-all | bytes 1572864 | tf_op jit(solution)/shard_map/all_to_all | solution.py:387
  66.8 0.0 copy-done
  66.8 0.0 copy-done.1
  66.8 0.0 copy-done.2
  66.8 0.0 copy-done.3
  66.8 1.4 %shard_map.186 = (bf16[128,1024]{1,0:T(8,128)(2,1)}, bf16[128,1024]{1,0:T(8,128)(2,1)}, bf16[128,1024]{1,0:T(8,128)(2,1)}, bf16[128,1024]{1,0:T(8,128)(2,1)}, bf16[128,1024]{1,0:T(8,128)(2,1)}) custom-call(bf16[32,96,128]{2,1,0:T(8,128)(2,1)S(1)} %all_to_all.11.back, bf16[128,1024]{1,0:T(8,128)(2,1)S(1)} %bitcast.12, bf16[128,1024]{1,0:T(8,128)(2,1)S(1)} %bitcast.14, ...), custom_call_target="tpu_custom_call" | custom-call | bytes 2097152 | tf_op jit(solution)/shard_map/pallas_call | solution.py:312
  (5 shorter events, 0.1 us)
Async XLA Ops:
  2.3 21.4 %copy-start.5 = (bf16[2,256,256]{2,1,0:T(8,128)(2,1)S(1)}, bf16[2,256,256]{2,1,0:T(8,128)(2,1)}, u32[]{:S(2)}) copy-start(bf16[2,256,256]{2,1,0:T(8,128)(2,1)} %constant.9.clone.back_lane_ref) | copy-start | bytes 786436
  2.3 21.4 %copy-start.6 = (bf16[2,256,256]{2,1,0:T(8,128)(2,1)S(1)}, bf16[2,256,256]{2,1,0:T(8,128)(2,1)}, u32[]{:S(2)}) copy-start(bf16[2,256,256]{2,1,0:T(8,128)(2,1)} %constant.8.clone.lane_ref) | copy-start | bytes 786436
  2.3 21.4 %copy-start.8 = (f32[17,4,128]{2,1,0:T(4,128)S(1)}, f32[17,4,128]{2,1,0:T(4,128)}, u32[]{:S(2)}) copy-start(f32[17,4,128]{2,1,0:T(4,128)} %constant.10.clone.twist_ref) | copy-start | bytes 104452
  24.9 16.3 %copy-start.4 = (f32[1024]{0:T(1024)S(1)}, f32[1024]{0:T(1024)}, u32[]{:S(2)}) copy-start(f32[1024]{0:T(1024)} %param.19) | copy-start | bytes 12292
  24.9 16.3 %copy-start.7 = (f32[17,4,128]{2,1,0:T(4,128)S(1)}, f32[17,4,128]{2,1,0:T(4,128)}, u32[]{:S(2)}) copy-start(f32[17,4,128]{2,1,0:T(4,128)} %constant.11.clone.twist_ref) | copy-start | bytes 104452
  24.9 7.2 %collective-permute-start = (bf16[16,16,128]{2,1,0:T(8,128)(2,1)S(1)}, bf16[16,16,128]{2,1,0:T(8,128)(2,1)S(1)}, u32[]{:S(2)}, u32[]{:S(2)}) collective-permute-start(bf16[16,16,128]{2,1,0:T(8,128)(2,1)S(1)} %get-tuple-element.19), channel_id=1, source_target_pairs={{0,128},{128,0},{1,129},{129,1},{2,130},{130,2},{3,131},{131,3},{4... | collective-permute-start | bytes 196616 | tf_op jit(solution)/shard_map/ppermute | solution.py:392
  32.1 11.7 %collective-permute-start.1 = (bf16[16,16,128]{2,1,0:T(8,128)(2,1)S(1)}, bf16[16,16,128]{2,1,0:T(8,128)(2,1)S(1)}, u32[]{:S(2)}, u32[]{:S(2)}) collective-permute-start(bf16[16,16,128]{2,1,0:T(8,128)(2,1)S(1)} %add_convert_fusion.1), channel_id=1, source_target_pairs={{0,256},{256,0},{1,257},{257,1},{2,258},{258,2},{3,259},{259,3},{4... | collective-permute-start | bytes 196616 | tf_op jit(solution)/shard_map/ppermute | solution.py:392
  49.7 17.1 %copy-start = (bf16[1,128,1024]{2,1,0:T(8,128)(2,1)S(1)}, bf16[1,128,1024]{2,1,0:T(8,128)(2,1)}, u32[]{:S(2)}) copy-start(bf16[1,128,1024]{2,1,0:T(8,128)(2,1)} %param.15) | copy-start | bytes 786436
  49.8 17.1 %copy-start.1 = (bf16[1,128,1024]{2,1,0:T(8,128)(2,1)S(1)}, bf16[1,128,1024]{2,1,0:T(8,128)(2,1)}, u32[]{:S(2)}) copy-start(bf16[1,128,1024]{2,1,0:T(8,128)(2,1)} %param.16) | copy-start | bytes 786436
  49.8 17.0 %copy-start.2 = (bf16[1,128,1024]{2,1,0:T(8,128)(2,1)S(1)}, bf16[1,128,1024]{2,1,0:T(8,128)(2,1)}, u32[]{:S(2)}) copy-start(bf16[1,128,1024]{2,1,0:T(8,128)(2,1)} %param.17) | copy-start | bytes 786436
  49.8 17.0 %copy-start.3 = (bf16[1,128,1024]{2,1,0:T(8,128)(2,1)S(1)}, bf16[1,128,1024]{2,1,0:T(8,128)(2,1)}, u32[]{:S(2)}) copy-start(bf16[1,128,1024]{2,1,0:T(8,128)(2,1)} %param.20) | copy-start | bytes 786436

commit v9 on v8

--- a/solution.py
+++ b/solution.py
@@ -388,19 +388,14 @@
 
     signals = swap(gate(query, key, value, grad, filter_taps, peers), ("pl", "x", "y"))
 
-    def exchange(values, axis):
-        return lax.ppermute(values, axis, [(0, 1), (1, 0)])
-
     def plus(a, b):
         return (a.astype(F32) + b.astype(F32)).astype(BF16)
 
     spectra, (given, term) = zip(*(taps_grad(signals, kept, factor) for kept in range(2)))
-    term = plus(term, exchange(given, "dm"))
-    other = exchange(term, "dh")
-    spectra, _ = lax.optimization_barrier((spectra, term))
+    taken = lax.ppermute(given, "dm", [(0, 1), (1, 0)])
     results = states(signals, spectra, skip_gain, own)
-    other, results = lax.optimization_barrier((other, results))
-    term = plus(term, other)
+    taken, results = lax.optimization_barrier((taken, results))
+    term = plus(*lax.all_gather(plus(term, taken), "dh"))
     halves = lax.all_gather(term, "dm")
     copies = [jnp.broadcast_to(t[None], (pair,) + t.shape).reshape((peers,) + t.shape[1:]) for t in halves]
     back = swap(jnp.concatenate([results, *copies], axis=1), ("pl", "x", "y"))

time: 68.5 us -> 69.6 us (1.016)
  the two profiles are of different devices: /device:TPU:64 before, /device:TPU:32 now
where the time goes in v9:
time: 69.6 us; the launch traced here: 69.3 us
  blocking collectives  55.5 us (80%)
  Pallas kernels  7.56 us (11%)
  starting transfers between devices  5.18 us (7%)
  between operations  0.82 us (1%)
    all_to_all x2, blocking collectives, swap(): return lax.all_to_all(values, axes, split_axis=0, concat_axis=0, tiled=True)  38.5 us
    all_gather x1, blocking collectives, on_device(): term = plus(*lax.all_gather(plus(term, taken), 'dh'))  11.1 us
    pallas_call x5, Pallas kernels, call(): pl.pallas_call(kernel, out_shape=shapes, in_specs=[place(in_hbm)] * len(a...  7.56 us
    all_gather x1, blocking collectives, on_device(): halves = lax.all_gather(term, 'dm')  5.84 us
    ppermute x1, starting transfers between devices, on_device(): taken = lax.ppermute(given, 'dm', [(0, 1), (1, 0)])  5.18 us
  transfers between devices with their start and end apart: 1, of which 0 were waited for; matrix products, arithmetic and copies ran while one was open for 0% of the time, Pallas kernels for 5%

profile of v9, /device:TPU:32, one launch (start us, length us, event | category | flops | bytes accessed | tf_op | source)
XLA Modules:
  0.0 69.3 jit_solution(8141976449458123066)
XLA Ops:
  0.6 1.6 %shard_map.182 = bf16[32,80,128]{2,1,0:T(8,128)(2,1)S(1)} custom-call(bf16[128,1024]{1,0:T(8,128)(2,1)} %bitcast.17, bf16[128,1024]{1,0:T(8,128)(2,1)} %bitcast.19, bf16[128,1024]{1,0:T(8,128)(2,1)} %bitcast.21, bf16[128,1024]{1,0:T(8,128)(2,1)} %bitcast.23, bf16[128,1024]{1,0:T(8,128)(2,1)} %taps.1), custom_call_target="tpu_custom_call" | custom-call | bytes 2097152 | tf_op jit(solution)/shard_map/pallas_call | solution.py:312
  2.3 0.0 copy-start.5
  2.3 0.0 copy-start.6
  2.3 0.0 copy-start.8
  2.3 20.7 %all_to_all.10.signals = bf16[32,80,128]{2,1,0:T(8,128)(2,1)S(1)} all-to-all(bf16[32,80,128]{2,1,0:T(8,128)(2,1)S(1)} %shard_map.182), channel_id=1, replica_groups=mesh['dh'=2,'dm'=2,'pl'=2,'chan'=4,'y'=4,'x'=4] {'pl','x','y'}, dimensions={0} | all-to-all | bytes 1310720 | tf_op jit(solution)/shard_map/all_to_all | solution.py:387
  23.0 0.0 copy-done.5
  23.0 0.0 copy-done.6
  23.0 0.0 copy-done.8
  23.0 1.2 %shard_map.183 = (f32[4,272,256]{2,1,0:T(8,128)S(1)}, bf16[16,16,128]{2,1,0:T(8,128)(2,1)S(1)}) custom-call(bf16[32,80,128]{2,1,0:T(8,128)(2,1)S(1)} %all_to_all.10.signals, bf16[2,256,256]{2,1,0:T(8,128)(2,1)S(1)} %copy-done.6, bf16[2,256,256]{2,1,0:T(8,128)(2,1)S(1)} %copy-done.5, f32[17,4,128]{2,1,0:T(4,128)S(1)} %copy-done.8), custom_call_target="tpu_custom_call" | custom-call | flops 2000000000 | bytes 2097152 | tf_op jit(solution)/shard_map/pallas_call | solution.py:312
  24.2 0.0 copy-start.4
  24.2 0.0 copy-start.7
  24.2 5.2 %collective-permute-start = (bf16[16,16,128]{2,1,0:T(8,128)(2,1)S(1)}, bf16[16,16,128]{2,1,0:T(8,128)(2,1)S(1)}, u32[]{:S(2)}, u32[]{:S(2)}) collective-permute-start(bf16[16,16,128]{2,1,0:T(8,128)(2,1)S(1)} %get-tuple-element.16), channel_id=1, source_target_pairs={{0,128},{128,0},{1,129},{129,1},{2,130},{130,2},{3,131},{131,3},{4... | collective-permute-start | bytes 196616 | tf_op jit(solution)/shard_map/ppermute | solution.py:395
  29.4 1.2 %shard_map.184 = (f32[4,272,256]{2,1,0:T(8,128)S(1)}, bf16[16,16,128]{2,1,0:T(8,128)(2,1)S(1)}) custom-call(bf16[32,80,128]{2,1,0:T(8,128)(2,1)S(1)} %all_to_all.10.signals, bf16[2,256,256]{2,1,0:T(8,128)(2,1)S(1)} %copy-done.6, bf16[2,256,256]{2,1,0:T(8,128)(2,1)S(1)} %copy-done.5, f32[17,4,128]{2,1,0:T(4,128)S(1)} %copy-done.8), custom_call_target="tpu_custom_call" | custom-call | flops 2000000000 | bytes 2097152 | tf_op jit(solution)/shard_map/pallas_call | solution.py:312
  30.6 0.0 copy-done.4
  30.6 0.0 copy-done.7
  30.7 2.2 %shard_map.185 = bf16[32,64,128]{2,1,0:T(8,128)(2,1)S(1)} custom-call(bf16[32,80,128]{2,1,0:T(8,128)(2,1)S(1)} %all_to_all.10.signals, f32[8,128]{1,0:T(8,128)S(1)} %bitcast.25, bf16[2,256,256]{2,1,0:T(8,128)(2,1)S(1)} %copy-done.6, bf16[2,256,256]{2,1,0:T(8,128)(2,1)S(1)} %copy-done.5, f32[17,4,128]{2,1,0:T(4,128)S(1)} %copy-done.7, ...), custom_call_target="tpu_custom_call" | custom-call | flops 3000000000 | bytes 2097152 | tf_op jit(solution)/shard_map/pallas_call | solution.py:312
  32.8 0.0 collective-permute-done
  32.9 11.1 %all-gather = bf16[32,16,128]{2,1,0:T(8,128)(2,1)S(1)} all-gather(bf16[16,16,128]{2,1,0:T(8,128)(2,1)S(1)} %add_convert_fusion.1), channel_id=2, replica_groups=mesh['dh'=2,'dm'=2,'pl'=2,'chan'=4,'y'=4,'x'=4] {'dh'}, dimensions={0}, use_global_device_ids=true | all-gather | bytes 196608 | tf_op jit(solution)/shard_map/all_gather | solution.py:398
  44.1 5.8 %all_gather.12 = bf16[2,16,16,128]{3,2,1,0:T(8,128)(2,1)S(1)} all-gather(bf16[1,16,16,128]{3,2,1,0:T(8,128)(2,1)S(1)} %fusion), channel_id=1, replica_groups=mesh['dh'=2,'dm'=2,'pl'=2,'chan'=4,'y'=4,'x'=4] {'dm'}, dimensions={0}, use_global_device_ids=true | all-gather | bytes 196608 | tf_op jit(solution)/shard_map/all_gather | solution.py:399
  50.0 0.1 pad_maximum_fusion
  50.0 0.0 copy-start
  50.0 0.0 copy-start.1
  50.0 0.0 copy-start.2
  50.1 0.0 copy-start.3
  50.1 17.8 %all_to_all.11.back = bf16[32,96,128]{2,1,0:T(8,128)(2,1)S(1)} all-to-all(bf16[32,96,128]{2,1,0:T(8,128)(2,1)S(1)} %pad_maximum_fusion), channel_id=1, replica_groups=mesh['dh'=2,'dm'=2,'pl'=2,'chan'=4,'y'=4,'x'=4] {'pl','x','y'}, dimensions={0} | all-to-all | bytes 1572864 | tf_op jit(solution)/shard_map/all_to_all | solution.py:387
  67.9 0.0 copy-done
  67.9 0.0 copy-done.1
  67.9 0.0 copy-done.2
  67.9 0.0 copy-done.3
  67.9 1.4 %shard_map.186 = (bf16[128,1024]{1,0:T(8,128)(2,1)}, bf16[128,1024]{1,0:T(8,128)(2,1)}, bf16[128,1024]{1,0:T(8,128)(2,1)}, bf16[128,1024]{1,0:T(8,128)(2,1)}, bf16[128,1024]{1,0:T(8,128)(2,1)}) custom-call(bf16[32,96,128]{2,1,0:T(8,128)(2,1)S(1)} %all_to_all.11.back, bf16[128,1024]{1,0:T(8,128)(2,1)S(1)} %bitcast.18, bf16[128,1024]{1,0:T(8,128)(2,1)S(1)} %bitcast.20, ...), custom_call_target="tpu_custom_call" | custom-call | bytes 2097152 | tf_op jit(solution)/shard_map/pallas_call | solution.py:312
  (5 shorter events, 0.1 us)
Async XLA Ops:
  2.3 20.7 %copy-start.5 = (bf16[2,256,256]{2,1,0:T(8,128)(2,1)S(1)}, bf16[2,256,256]{2,1,0:T(8,128)(2,1)}, u32[]{:S(2)}) copy-start(bf16[2,256,256]{2,1,0:T(8,128)(2,1)} %constant.9.clone.back_lane_ref) | copy-start | bytes 786436
  2.3 20.7 %copy-start.6 = (bf16[2,256,256]{2,1,0:T(8,128)(2,1)S(1)}, bf16[2,256,256]{2,1,0:T(8,128)(2,1)}, u32[]{:S(2)}) copy-start(bf16[2,256,256]{2,1,0:T(8,128)(2,1)} %constant.8.clone.lane_ref) | copy-start | bytes 786436
  2.3 20.7 %copy-start.8 = (f32[17,4,128]{2,1,0:T(4,128)S(1)}, f32[17,4,128]{2,1,0:T(4,128)}, u32[]{:S(2)}) copy-start(f32[17,4,128]{2,1,0:T(4,128)} %constant.10.clone.twist_ref) | copy-start | bytes 104452
  24.2 6.4 %copy-start.4 = (f32[1024]{0:T(1024)S(1)}, f32[1024]{0:T(1024)}, u32[]{:S(2)}) copy-start(f32[1024]{0:T(1024)} %param.19) | copy-start | bytes 12292
  24.2 6.4 %copy-start.7 = (f32[17,4,128]{2,1,0:T(4,128)S(1)}, f32[17,4,128]{2,1,0:T(4,128)}, u32[]{:S(2)}) copy-start(f32[17,4,128]{2,1,0:T(4,128)} %constant.11.clone.twist_ref) | copy-start | bytes 104452
  24.2 8.6 %collective-permute-start = (bf16[16,16,128]{2,1,0:T(8,128)(2,1)S(1)}, bf16[16,16,128]{2,1,0:T(8,128)(2,1)S(1)}, u32[]{:S(2)}, u32[]{:S(2)}) collective-permute-start(bf16[16,16,128]{2,1,0:T(8,128)(2,1)S(1)} %get-tuple-element.16), channel_id=1, source_target_pairs={{0,128},{128,0},{1,129},{129,1},{2,130},{130,2},{3,131},{131,3},{4... | collective-permute-start | bytes 196616 | tf_op jit(solution)/shard_map/ppermute | solution.py:395
  50.0 17.9 %copy-start = (bf16[1,128,1024]{2,1,0:T(8,128)(2,1)S(1)}, bf16[1,128,1024]{2,1,0:T(8,128)(2,1)}, u32[]{:S(2)}) copy-start(bf16[1,128,1024]{2,1,0:T(8,128)(2,1)} %param.15) | copy-start | bytes 786436
  50.0 17.9 %copy-start.1 = (bf16[1,128,1024]{2,1,0:T(8,128)(2,1)S(1)}, bf16[1,128,1024]{2,1,0:T(8,128)(2,1)}, u32[]{:S(2)}) copy-start(bf16[1,128,1024]{2,1,0:T(8,128)(2,1)} %param.16) | copy-start | bytes 786436
  50.0 17.9 %copy-start.2 = (bf16[1,128,1024]{2,1,0:T(8,128)(2,1)S(1)}, bf16[1,128,1024]{2,1,0:T(8,128)(2,1)}, u32[]{:S(2)}) copy-start(bf16[1,128,1024]{2,1,0:T(8,128)(2,1)} %param.17) | copy-start | bytes 786436
  50.1 17.9 %copy-start.3 = (bf16[1,128,1024]{2,1,0:T(8,128)(2,1)S(1)}, bf16[1,128,1024]{2,1,0:T(8,128)(2,1)}, u32[]{:S(2)}) copy-start(bf16[1,128,1024]{2,1,0:T(8,128)(2,1)} %param.20) | copy-start | bytes 786436

commit v10 on v9

--- a/solution.py
+++ b/solution.py
@@ -395,7 +395,8 @@
     taken = lax.ppermute(given, "dm", [(0, 1), (1, 0)])
     results = states(signals, spectra, skip_gain, own)
     taken, results = lax.optimization_barrier((taken, results))
-    term = plus(*lax.all_gather(plus(term, taken), "dh"))
+    term = plus(term, taken)
+    term = plus(term, lax.ppermute(term, "dh", [(0, 1), (1, 0)]))
     halves = lax.all_gather(term, "dm")
     copies = [jnp.broadcast_to(t[None], (pair,) + t.shape).reshape((peers,) + t.shape[1:]) for t in halves]
     back = swap(jnp.concatenate([results, *copies], axis=1), ("pl", "x", "y"))

time: 69.6 us -> 70.9 us (1.019)
  blocking collectives: 55.5 us -> 44.4 us
  starting transfers between devices: 5.18 us -> 14.3 us
  waiting for transfers between devices: 0.01 us -> 3.25 us
    all_gather x1 -> x0, blocking collectives: 11.1 us -> none  [on_device(): term = plus(*lax.all_gather(plus(term, taken), 'dh'))]
    ppermute x0 -> x1, starting transfers between devices: none -> 9.1 us  [on_device(): term = plus(term, lax.ppermute(term, 'dh', [(0, 1), (1, 0)]))]
    ppermute x0 -> x1, waiting for transfers between devices: none -> 3.24 us  [on_device(): term = plus(term, lax.ppermute(term, 'dh', [(0, 1), (1, 0)]))]
  transfers between devices with their start and end apart: 1 -> 2, of which waited for: 0 -> 1; matrix products, arithmetic and copies ran while one was open for 0% -> 0% of each run, Pallas kernels for 5% -> 5%
where the time goes in v10:
time: 70.9 us; the launch traced here: 70.5 us
  blocking collectives  44.4 us (63%)
  starting transfers between devices  14.3 us (20%)
  Pallas kernels  7.56 us (11%)
  waiting for transfers between devices  3.25 us (5%)
  between operations  0.83 us (1%)
    all_to_all x2, blocking collectives, swap(): return lax.all_to_all(values, axes, split_axis=0, concat_axis=0, tiled=True)  38.6 us
    ppermute x1, starting transfers between devices, on_device(): term = plus(term, lax.ppermute(term, 'dh', [(0, 1), (1, 0)]))  9.1 us
    pallas_call x5, Pallas kernels, call(): pl.pallas_call(kernel, out_shape=shapes, in_specs=[place(in_hbm)] * len(a...  7.56 us
    all_gather x1, blocking collectives, on_device(): halves = lax.all_gather(term, 'dm')  5.84 us
    ppermute x1, starting transfers between devices, on_device(): taken = lax.ppermute(given, 'dm', [(0, 1), (1, 0)])  5.18 us
    ppermute x1, waiting for transfers between devices, on_device(): term = plus(term, lax.ppermute(term, 'dh', [(0, 1), (1, 0)]))  3.24 us
  transfers between devices with their start and end apart: 2, of which 1 were waited for; matrix products, arithmetic and copies ran while one was open for 0% of the time, Pallas kernels for 5%

profile of v10, /device:TPU:32, one launch (start us, length us, event | category | flops | bytes accessed | tf_op | source)
XLA Modules:
  0.0 70.5 jit_solution(14121467026127095298)
XLA Ops:
  0.6 1.6 %shard_map.182 = bf16[32,80,128]{2,1,0:T(8,128)(2,1)S(1)} custom-call(bf16[128,1024]{1,0:T(8,128)(2,1)} %bitcast.11, bf16[128,1024]{1,0:T(8,128)(2,1)} %bitcast.13, bf16[128,1024]{1,0:T(8,128)(2,1)} %bitcast.15, bf16[128,1024]{1,0:T(8,128)(2,1)} %bitcast.17, bf16[128,1024]{1,0:T(8,128)(2,1)} %taps.1), custom_call_target="tpu_custom_call" | custom-call | bytes 2097152 | tf_op jit(solution)/shard_map/pallas_call | solution.py:312
  2.3 0.0 copy-start.5
  2.3 0.0 copy-start.6
  2.3 0.0 copy-start.8
  2.3 20.7 %all_to_all.10.signals = bf16[32,80,128]{2,1,0:T(8,128)(2,1)S(1)} all-to-all(bf16[32,80,128]{2,1,0:T(8,128)(2,1)S(1)} %shard_map.182), channel_id=1, replica_groups=mesh['dh'=2,'dm'=2,'pl'=2,'chan'=4,'y'=4,'x'=4] {'pl','x','y'}, dimensions={0} | all-to-all | bytes 1310720 | tf_op jit(solution)/shard_map/all_to_all | solution.py:387
  23.0 0.0 copy-done.5
  23.0 0.0 copy-done.6
  23.0 0.0 copy-done.8
  23.0 1.2 %shard_map.183 = (f32[4,272,256]{2,1,0:T(8,128)S(1)}, bf16[16,16,128]{2,1,0:T(8,128)(2,1)S(1)}) custom-call(bf16[32,80,128]{2,1,0:T(8,128)(2,1)S(1)} %all_to_all.10.signals, bf16[2,256,256]{2,1,0:T(8,128)(2,1)S(1)} %copy-done.6, bf16[2,256,256]{2,1,0:T(8,128)(2,1)S(1)} %copy-done.5, f32[17,4,128]{2,1,0:T(4,128)S(1)} %copy-done.8), custom_call_target="tpu_custom_call" | custom-call | flops 2000000000 | bytes 2097152 | tf_op jit(solution)/shard_map/pallas_call | solution.py:312
  24.2 0.0 copy-start.4
  24.2 0.0 copy-start.7
  24.2 5.2 %collective-permute-start = (bf16[16,16,128]{2,1,0:T(8,128)(2,1)S(1)}, bf16[16,16,128]{2,1,0:T(8,128)(2,1)S(1)}, u32[]{:S(2)}, u32[]{:S(2)}) collective-permute-start(bf16[16,16,128]{2,1,0:T(8,128)(2,1)S(1)} %get-tuple-element.16), channel_id=1, source_target_pairs={{0,128},{128,0},{1,129},{129,1},{2,130},{130,2},{3,131},{131,3},{4... | collective-permute-start | bytes 196616 | tf_op jit(solution)/shard_map/ppermute | solution.py:395
  29.4 1.2 %shard_map.184 = (f32[4,272,256]{2,1,0:T(8,128)S(1)}, bf16[16,16,128]{2,1,0:T(8,128)(2,1)S(1)}) custom-call(bf16[32,80,128]{2,1,0:T(8,128)(2,1)S(1)} %all_to_all.10.signals, bf16[2,256,256]{2,1,0:T(8,128)(2,1)S(1)} %copy-done.6, bf16[2,256,256]{2,1,0:T(8,128)(2,1)S(1)} %copy-done.5, f32[17,4,128]{2,1,0:T(4,128)S(1)} %copy-done.8), custom_call_target="tpu_custom_call" | custom-call | flops 2000000000 | bytes 2097152 | tf_op jit(solution)/shard_map/pallas_call | solution.py:312
  30.6 0.0 copy-done.4
  30.6 0.0 copy-done.7
  30.7 2.2 %shard_map.185 = bf16[32,64,128]{2,1,0:T(8,128)(2,1)S(1)} custom-call(bf16[32,80,128]{2,1,0:T(8,128)(2,1)S(1)} %all_to_all.10.signals, f32[8,128]{1,0:T(8,128)S(1)} %bitcast.19, bf16[2,256,256]{2,1,0:T(8,128)(2,1)S(1)} %copy-done.6, bf16[2,256,256]{2,1,0:T(8,128)(2,1)S(1)} %copy-done.5, f32[17,4,128]{2,1,0:T(4,128)S(1)} %copy-done.7, ...), custom_call_target="tpu_custom_call" | custom-call | flops 3000000000 | bytes 2097152 | tf_op jit(solution)/shard_map/pallas_call | solution.py:312
  32.8 0.0 collective-permute-done
  32.9 9.1 %collective-permute-start.1 = (bf16[16,16,128]{2,1,0:T(8,128)(2,1)S(1)}, bf16[16,16,128]{2,1,0:T(8,128)(2,1)S(1)}, u32[]{:S(2)}, u32[]{:S(2)}) collective-permute-start(bf16[16,16,128]{2,1,0:T(8,128)(2,1)S(1)} %add_convert_fusion.1), channel_id=1, source_target_pairs={{0,256},{256,0},{1,257},{257,1},{2,258},{258,2},{3,259},{259,3},{4... | collective-permute-start | bytes 196616 | tf_op jit(solution)/shard_map/ppermute | solution.py:399
  42.0 3.2 %collective-permute-done.1 = bf16[16,16,128]{2,1,0:T(8,128)(2,1)S(1)} collective-permute-done((bf16[16,16,128]{2,1,0:T(8,128)(2,1)S(1)}, bf16[16,16,128]{2,1,0:T(8,128)(2,1)S(1)}, u32[]{:S(2)}, u32[]{:S(2)}) %collective-permute-start.1) | collective-permute-done | bytes 65568 | tf_op jit(solution)/shard_map/ppermute | solution.py:399
  45.3 5.8 %all-gather = bf16[32,16,128]{2,1,0:T(8,128)(2,1)S(1)} all-gather(bf16[16,16,128]{2,1,0:T(8,128)(2,1)S(1)} %add_convert_fusion), channel_id=2, replica_groups=mesh['dh'=2,'dm'=2,'pl'=2,'chan'=4,'y'=4,'x'=4] {'dm'}, dimensions={0}, use_global_device_ids=true | all-gather | bytes 196608 | tf_op jit(solution)/shard_map/all_gather | solution.py:400
  51.2 0.1 pad_maximum_fusion
  51.2 0.0 copy-start
  51.2 0.0 copy-start.1
  51.3 0.0 copy-start.2
  51.3 0.0 copy-start.3
  51.3 17.9 %all_to_all.11.back = bf16[32,96,128]{2,1,0:T(8,128)(2,1)S(1)} all-to-all(bf16[32,96,128]{2,1,0:T(8,128)(2,1)S(1)} %pad_maximum_fusion), channel_id=1, replica_groups=mesh['dh'=2,'dm'=2,'pl'=2,'chan'=4,'y'=4,'x'=4] {'pl','x','y'}, dimensions={0} | all-to-all | bytes 1572864 | tf_op jit(solution)/shard_map/all_to_all | solution.py:387
  69.2 0.0 copy-done
  69.2 0.0 copy-done.1
  69.2 0.0 copy-done.2
  69.2 0.0 copy-done.3
  69.2 1.4 %shard_map.186 = (bf16[128,1024]{1,0:T(8,128)(2,1)}, bf16[128,1024]{1,0:T(8,128)(2,1)}, bf16[128,1024]{1,0:T(8,128)(2,1)}, bf16[128,1024]{1,0:T(8,128)(2,1)}, bf16[128,1024]{1,0:T(8,128)(2,1)}) custom-call(bf16[32,96,128]{2,1,0:T(8,128)(2,1)S(1)} %all_to_all.11.back, bf16[128,1024]{1,0:T(8,128)(2,1)S(1)} %bitcast.12, bf16[128,1024]{1,0:T(8,128)(2,1)S(1)} %bitcast.14, ...), custom_call_target="tpu_custom_call" | custom-call | bytes 2097152 | tf_op jit(solution)/shard_map/pallas_call | solution.py:312
  (5 shorter events, 0.1 us)
Async XLA Ops:
  2.3 20.7 %copy-start.5 = (bf16[2,256,256]{2,1,0:T(8,128)(2,1)S(1)}, bf16[2,256,256]{2,1,0:T(8,128)(2,1)}, u32[]{:S(2)}) copy-start(bf16[2,256,256]{2,1,0:T(8,128)(2,1)} %constant.9.clone.back_lane_ref) | copy-start | bytes 786436
  2.3 20.7 %copy-start.6 = (bf16[2,256,256]{2,1,0:T(8,128)(2,1)S(1)}, bf16[2,256,256]{2,1,0:T(8,128)(2,1)}, u32[]{:S(2)}) copy-start(bf16[2,256,256]{2,1,0:T(8,128)(2,1)} %constant.8.clone.lane_ref) | copy-start | bytes 786436
  2.3 20.7 %copy-start.8 = (f32[17,4,128]{2,1,0:T(4,128)S(1)}, f32[17,4,128]{2,1,0:T(4,128)}, u32[]{:S(2)}) copy-start(f32[17,4,128]{2,1,0:T(4,128)} %constant.10.clone.twist_ref) | copy-start | bytes 104452
  24.2 6.4 %copy-start.4 = (f32[1024]{0:T(1024)S(1)}, f32[1024]{0:T(1024)}, u32[]{:S(2)}) copy-start(f32[1024]{0:T(1024)} %param.19) | copy-start | bytes 12292
  24.2 6.4 %copy-start.7 = (f32[17,4,128]{2,1,0:T(4,128)S(1)}, f32[17,4,128]{2,1,0:T(4,128)}, u32[]{:S(2)}) copy-start(f32[17,4,128]{2,1,0:T(4,128)} %constant.11.clone.twist_ref) | copy-start | bytes 104452
  24.2 8.6 %collective-permute-start = (bf16[16,16,128]{2,1,0:T(8,128)(2,1)S(1)}, bf16[16,16,128]{2,1,0:T(8,128)(2,1)S(1)}, u32[]{:S(2)}, u32[]{:S(2)}) collective-permute-start(bf16[16,16,128]{2,1,0:T(8,128)(2,1)S(1)} %get-tuple-element.16), channel_id=1, source_target_pairs={{0,128},{128,0},{1,129},{129,1},{2,130},{130,2},{3,131},{131,3},{4... | collective-permute-start | bytes 196616 | tf_op jit(solution)/shard_map/ppermute | solution.py:395
  32.9 12.4 %collective-permute-start.1 = (bf16[16,16,128]{2,1,0:T(8,128)(2,1)S(1)}, bf16[16,16,128]{2,1,0:T(8,128)(2,1)S(1)}, u32[]{:S(2)}, u32[]{:S(2)}) collective-permute-start(bf16[16,16,128]{2,1,0:T(8,128)(2,1)S(1)} %add_convert_fusion.1), channel_id=1, source_target_pairs={{0,256},{256,0},{1,257},{257,1},{2,258},{258,2},{3,259},{259,3},{4... | collective-permute-start | bytes 196616 | tf_op jit(solution)/shard_map/ppermute | solution.py:399
  51.2 17.9 %copy-start = (bf16[1,128,1024]{2,1,0:T(8,128)(2,1)S(1)}, bf16[1,128,1024]{2,1,0:T(8,128)(2,1)}, u32[]{:S(2)}) copy-start(bf16[1,128,1024]{2,1,0:T(8,128)(2,1)} %param.15) | copy-start | bytes 786436
  51.2 17.9 %copy-start.1 = (bf16[1,128,1024]{2,1,0:T(8,128)(2,1)S(1)}, bf16[1,128,1024]{2,1,0:T(8,128)(2,1)}, u32[]{:S(2)}) copy-start(bf16[1,128,1024]{2,1,0:T(8,128)(2,1)} %param.16) | copy-start | bytes 786436
  51.3 17.9 %copy-start.2 = (bf16[1,128,1024]{2,1,0:T(8,128)(2,1)S(1)}, bf16[1,128,1024]{2,1,0:T(8,128)(2,1)}, u32[]{:S(2)}) copy-start(bf16[1,128,1024]{2,1,0:T(8,128)(2,1)} %param.17) | copy-start | bytes 786436
  51.3 17.9 %copy-start.3 = (bf16[1,128,1024]{2,1,0:T(8,128)(2,1)S(1)}, bf16[1,128,1024]{2,1,0:T(8,128)(2,1)}, u32[]{:S(2)}) copy-start(bf16[1,128,1024]{2,1,0:T(8,128)(2,1)} %param.20) | copy-start | bytes 786436

commit v11 on v7

--- a/solution.py
+++ b/solution.py
@@ -399,15 +399,12 @@
 
     spectra, (given, term) = zip(*(taps_grad(signals, kept, factor) for kept in range(2)))
     term = plus(term, exchange(given, "dm"))
-    other = exchange(term, "dh")
+    term = plus(*lax.all_gather(term, "dh"))
+    other = exchange(term, "dm")
     spectra, _ = lax.optimization_barrier((spectra, term))
     results = states(signals, spectra, skip_gain, own)
     other, results = lax.optimization_barrier((other, results))
-    term = plus(term, other)
-    copies = [
-        jnp.broadcast_to(t[None], (pair,) + t.shape).reshape((peers,) + t.shape[1:])
-        for t in (term, exchange(term, "dm"))
-    ]
+    copies = [jnp.broadcast_to(t[None], (pair,) + t.shape).reshape((peers,) + t.shape[1:]) for t in (term, other)]
     back = swap(jnp.concatenate([results, *copies], axis=1), ("pl", "x", "y"))
     outs = outputs(back, query, key, value, grad)
     return tuple(out[None] for out in outs[:4]) + (outs[4],)

time: 69.7 us -> 68.5 us (0.983)
  blocking collectives: 38.4 us -> 48.8 us
  starting transfers between devices: 12.9 us -> 3.84 us
  waiting for transfers between devices: 9.48 us -> 6.96 us
    all_gather x0 -> x1, blocking collectives: none -> 10.5 us  [on_device(): term = plus(*lax.all_gather(term, 'dh'))]
    ppermute x3 -> x2, starting transfers between devices: 12.9 us -> 3.84 us  [exchange(): return lax.ppermute(values, axis, [(0, 1), (1, 0)])]
    ppermute x3 -> x2, waiting for transfers between devices: 9.48 us -> 6.96 us  [exchange(): return lax.ppermute(values, axis, [(0, 1), (1, 0)])]
  transfers between devices with their start and end apart: 3 -> 2, of which waited for: 3 -> 2; matrix products, arithmetic and copies ran while one was open for 0% -> 0% of each run, Pallas kernels for 5% -> 5%
where the time goes in v11:
time: 68.5 us; the launch traced here: 68.2 us
  blocking collectives  48.8 us (71%)
  Pallas kernels  7.55 us (11%)
  waiting for transfers between devices  6.96 us (10%)
  starting transfers between devices  3.84 us (6%)
  between operations  0.81 us (1%)
    all_to_all x2, blocking collectives, swap(): return lax.all_to_all(values, axes, split_axis=0, concat_axis=0, tiled=True)  38.3 us
    all_gather x1, blocking collectives, on_device(): term = plus(*lax.all_gather(term, 'dh'))  10.5 us
    pallas_call x5, Pallas kernels, call(): pl.pallas_call(kernel, out_shape=shapes, in_specs=[place(in_hbm)] * len(a...  7.55 us
    ppermute x2, waiting for transfers between devices, exchange(): return lax.ppermute(values, axis, [(0, 1), (1, 0)])  6.96 us
    ppermute x2, starting transfers between devices, exchange(): return lax.ppermute(values, axis, [(0, 1), (1, 0)])  3.84 us
  transfers between devices with their start and end apart: 2, of which 2 were waited for; matrix products, arithmetic and copies ran while one was open for 0% of the time, Pallas kernels for 5%

profile of v11, /device:TPU:64, one launch (start us, length us, event | category | flops | bytes accessed | tf_op | source)
XLA Modules:
  0.0 68.2 jit_solution(17852991912847270079)
XLA Ops:
  0.6 1.6 %shard_map.182 = bf16[32,80,128]{2,1,0:T(8,128)(2,1)S(1)} custom-call(bf16[128,1024]{1,0:T(8,128)(2,1)} %bitcast.11, bf16[128,1024]{1,0:T(8,128)(2,1)} %bitcast.13, bf16[128,1024]{1,0:T(8,128)(2,1)} %bitcast.15, bf16[128,1024]{1,0:T(8,128)(2,1)} %bitcast.17, bf16[128,1024]{1,0:T(8,128)(2,1)} %taps.1), custom_call_target="tpu_custom_call" | custom-call | bytes 2097152 | tf_op jit(solution)/shard_map/pallas_call | solution.py:315
  2.3 0.0 copy-start.5
  2.3 0.0 copy-start.6
  2.3 0.0 copy-start.8
  2.3 21.3 %all_to_all.10.signals = bf16[32,80,128]{2,1,0:T(8,128)(2,1)S(1)} all-to-all(bf16[32,80,128]{2,1,0:T(8,128)(2,1)S(1)} %shard_map.182), channel_id=1, replica_groups=mesh['dh'=2,'dm'=2,'pl'=2,'chan'=4,'y'=4,'x'=4] {'pl','x','y'}, dimensions={0} | all-to-all | bytes 1310720 | tf_op jit(solution)/shard_map/all_to_all | solution.py:390
  23.6 0.0 copy-done.5
  23.6 0.0 copy-done.6
  23.6 0.0 copy-done.8
  23.7 1.2 %shard_map.184 = (f32[4,272,256]{2,1,0:T(8,128)S(1)}, bf16[16,16,128]{2,1,0:T(8,128)(2,1)S(1)}) custom-call(bf16[32,80,128]{2,1,0:T(8,128)(2,1)S(1)} %all_to_all.10.signals, bf16[2,256,256]{2,1,0:T(8,128)(2,1)S(1)} %copy-done.6, bf16[2,256,256]{2,1,0:T(8,128)(2,1)S(1)} %copy-done.5, f32[17,4,128]{2,1,0:T(4,128)S(1)} %copy-done.8), custom_call_target="tpu_custom_call" | custom-call | flops 2000000000 | bytes 2097152 | tf_op jit(solution)/shard_map/pallas_call | solution.py:315
  24.9 0.0 copy-start.4
  24.9 0.0 copy-start.7
  24.9 1.9 %collective-permute-start = (bf16[16,16,128]{2,1,0:T(8,128)(2,1)S(1)}, bf16[16,16,128]{2,1,0:T(8,128)(2,1)S(1)}, u32[]{:S(2)}, u32[]{:S(2)}) collective-permute-start(bf16[16,16,128]{2,1,0:T(8,128)(2,1)S(1)} %get-tuple-element.19), channel_id=1, source_target_pairs={{0,128},{128,0},{1,129},{129,1},{2,130},{130,2},{3,131},{131,3},{4... | collective-permute-start | bytes 196616 | tf_op jit(solution)/shard_map/ppermute | solution.py:395
  26.8 1.2 %shard_map.183 = (f32[4,272,256]{2,1,0:T(8,128)S(1)}, bf16[16,16,128]{2,1,0:T(8,128)(2,1)S(1)}) custom-call(bf16[32,80,128]{2,1,0:T(8,128)(2,1)S(1)} %all_to_all.10.signals, bf16[2,256,256]{2,1,0:T(8,128)(2,1)S(1)} %copy-done.6, bf16[2,256,256]{2,1,0:T(8,128)(2,1)S(1)} %copy-done.5, f32[17,4,128]{2,1,0:T(4,128)S(1)} %copy-done.8), custom_call_target="tpu_custom_call" | custom-call | flops 2000000000 | bytes 2097152 | tf_op jit(solution)/shard_map/pallas_call | solution.py:315
  28.0 4.0 %collective-permute-done = bf16[16,16,128]{2,1,0:T(8,128)(2,1)S(1)} collective-permute-done((bf16[16,16,128]{2,1,0:T(8,128)(2,1)S(1)}, bf16[16,16,128]{2,1,0:T(8,128)(2,1)S(1)}, u32[]{:S(2)}, u32[]{:S(2)}) %collective-permute-start) | collective-permute-done | bytes 65568 | tf_op jit(solution)/shard_map/ppermute | solution.py:395
  32.1 10.5 %all-gather = bf16[32,16,128]{2,1,0:T(8,128)(2,1)S(1)} all-gather(bf16[16,16,128]{2,1,0:T(8,128)(2,1)S(1)} %add_convert_fusion.1), channel_id=2, replica_groups=mesh['dh'=2,'dm'=2,'pl'=2,'chan'=4,'y'=4,'x'=4] {'dh'}, dimensions={0}, use_global_device_ids=true | all-gather | bytes 196608 | tf_op jit(solution)/shard_map/all_gather | solution.py:402
  42.6 1.9 %collective-permute-start.1 = (bf16[16,16,128]{2,1,0:T(8,128)(2,1)S(1)}, bf16[16,16,128]{2,1,0:T(8,128)(2,1)S(1)}, u32[]{:S(2)}, u32[]{:S(2)}) collective-permute-start(bf16[16,16,128]{2,1,0:T(8,128)(2,1)S(1)} %add_convert_fusion), channel_id=1, source_target_pairs={{0,128},{128,0},{1,129},{129,1},{2,130},{130,2},{3,131},{131,3},{4... | collective-permute-start | bytes 196616 | tf_op jit(solution)/shard_map/ppermute | solution.py:395
  44.5 0.0 copy-done.4
  44.5 0.0 copy-done.7
  44.5 2.2 %shard_map.185 = bf16[32,64,128]{2,1,0:T(8,128)(2,1)S(1)} custom-call(bf16[32,80,128]{2,1,0:T(8,128)(2,1)S(1)} %all_to_all.10.signals, f32[8,128]{1,0:T(8,128)S(1)} %bitcast.19, bf16[2,256,256]{2,1,0:T(8,128)(2,1)S(1)} %copy-done.6, bf16[2,256,256]{2,1,0:T(8,128)(2,1)S(1)} %copy-done.5, f32[17,4,128]{2,1,0:T(4,128)S(1)} %copy-done.7, ...), custom_call_target="tpu_custom_call" | custom-call | flops 3000000000 | bytes 2097152 | tf_op jit(solution)/shard_map/pallas_call | solution.py:315
  46.7 2.9 %collective-permute-done.1 = bf16[16,16,128]{2,1,0:T(8,128)(2,1)S(1)} collective-permute-done((bf16[16,16,128]{2,1,0:T(8,128)(2,1)S(1)}, bf16[16,16,128]{2,1,0:T(8,128)(2,1)S(1)}, u32[]{:S(2)}, u32[]{:S(2)}) %collective-permute-start.1) | collective-permute-done | bytes 65568 | tf_op jit(solution)/shard_map/ppermute | solution.py:395
  49.7 0.1 pad_maximum_fusion
  49.7 0.0 copy-start
  49.7 0.0 copy-start.1
  49.8 0.0 copy-start.2
  49.8 0.0 copy-start.3
  49.8 17.0 %all_to_all.11.back = bf16[32,96,128]{2,1,0:T(8,128)(2,1)S(1)} all-to-all(bf16[32,96,128]{2,1,0:T(8,128)(2,1)S(1)} %pad_maximum_fusion), channel_id=1, replica_groups=mesh['dh'=2,'dm'=2,'pl'=2,'chan'=4,'y'=4,'x'=4] {'pl','x','y'}, dimensions={0} | all-to-all | bytes 1572864 | tf_op jit(solution)/shard_map/all_to_all | solution.py:390
  66.8 0.0 copy-done
  66.8 0.0 copy-done.1
  66.8 0.0 copy-done.2
  66.8 0.0 copy-done.3
  66.8 1.3 %shard_map.186 = (bf16[128,1024]{1,0:T(8,128)(2,1)}, bf16[128,1024]{1,0:T(8,128)(2,1)}, bf16[128,1024]{1,0:T(8,128)(2,1)}, bf16[128,1024]{1,0:T(8,128)(2,1)}, bf16[128,1024]{1,0:T(8,128)(2,1)}) custom-call(bf16[32,96,128]{2,1,0:T(8,128)(2,1)S(1)} %all_to_all.11.back, bf16[128,1024]{1,0:T(8,128)(2,1)S(1)} %bitcast.12, bf16[128,1024]{1,0:T(8,128)(2,1)S(1)} %bitcast.14, ...), custom_call_target="tpu_custom_call" | custom-call | bytes 2097152 | tf_op jit(solution)/shard_map/pallas_call | solution.py:315
  (4 shorter events, 0.1 us)
Async XLA Ops:
  2.3 21.4 %copy-start.5 = (bf16[2,256,256]{2,1,0:T(8,128)(2,1)S(1)}, bf16[2,256,256]{2,1,0:T(8,128)(2,1)}, u32[]{:S(2)}) copy-start(bf16[2,256,256]{2,1,0:T(8,128)(2,1)} %constant.9.clone.back_lane_ref) | copy-start | bytes 786436
  2.3 21.4 %copy-start.6 = (bf16[2,256,256]{2,1,0:T(8,128)(2,1)S(1)}, bf16[2,256,256]{2,1,0:T(8,128)(2,1)}, u32[]{:S(2)}) copy-start(bf16[2,256,256]{2,1,0:T(8,128)(2,1)} %constant.8.clone.lane_ref) | copy-start | bytes 786436
  2.3 21.4 %copy-start.8 = (f32[17,4,128]{2,1,0:T(4,128)S(1)}, f32[17,4,128]{2,1,0:T(4,128)}, u32[]{:S(2)}) copy-start(f32[17,4,128]{2,1,0:T(4,128)} %constant.10.clone.twist_ref) | copy-start | bytes 104452
  24.9 19.6 %copy-start.4 = (f32[1024]{0:T(1024)S(1)}, f32[1024]{0:T(1024)}, u32[]{:S(2)}) copy-start(f32[1024]{0:T(1024)} %param.19) | copy-start | bytes 12292
  24.9 19.6 %copy-start.7 = (f32[17,4,128]{2,1,0:T(4,128)S(1)}, f32[17,4,128]{2,1,0:T(4,128)}, u32[]{:S(2)}) copy-start(f32[17,4,128]{2,1,0:T(4,128)} %constant.11.clone.twist_ref) | copy-start | bytes 104452
  24.9 7.2 %collective-permute-start = (bf16[16,16,128]{2,1,0:T(8,128)(2,1)S(1)}, bf16[16,16,128]{2,1,0:T(8,128)(2,1)S(1)}, u32[]{:S(2)}, u32[]{:S(2)}) collective-permute-start(bf16[16,16,128]{2,1,0:T(8,128)(2,1)S(1)} %get-tuple-element.19), channel_id=1, source_target_pairs={{0,128},{128,0},{1,129},{129,1},{2,130},{130,2},{3,131},{131,3},{4... | collective-permute-start | bytes 196616 | tf_op jit(solution)/shard_map/ppermute | solution.py:395
  42.6 7.1 %collective-permute-start.1 = (bf16[16,16,128]{2,1,0:T(8,128)(2,1)S(1)}, bf16[16,16,128]{2,1,0:T(8,128)(2,1)S(1)}, u32[]{:S(2)}, u32[]{:S(2)}) collective-permute-start(bf16[16,16,128]{2,1,0:T(8,128)(2,1)S(1)} %add_convert_fusion), channel_id=1, source_target_pairs={{0,128},{128,0},{1,129},{129,1},{2,130},{130,2},{3,131},{131,3},{4... | collective-permute-start | bytes 196616 | tf_op jit(solution)/shard_map/ppermute | solution.py:395
  49.7 17.1 %copy-start = (bf16[1,128,1024]{2,1,0:T(8,128)(2,1)S(1)}, bf16[1,128,1024]{2,1,0:T(8,128)(2,1)}, u32[]{:S(2)}) copy-start(bf16[1,128,1024]{2,1,0:T(8,128)(2,1)} %param.15) | copy-start | bytes 786436
  49.7 17.0 %copy-start.1 = (bf16[1,128,1024]{2,1,0:T(8,128)(2,1)S(1)}, bf16[1,128,1024]{2,1,0:T(8,128)(2,1)}, u32[]{:S(2)}) copy-start(bf16[1,128,1024]{2,1,0:T(8,128)(2,1)} %param.16) | copy-start | bytes 786436
  49.8 17.0 %copy-start.2 = (bf16[1,128,1024]{2,1,0:T(8,128)(2,1)S(1)}, bf16[1,128,1024]{2,1,0:T(8,128)(2,1)}, u32[]{:S(2)}) copy-start(bf16[1,128,1024]{2,1,0:T(8,128)(2,1)} %param.17) | copy-start | bytes 786436
  49.8 17.0 %copy-start.3 = (bf16[1,128,1024]{2,1,0:T(8,128)(2,1)S(1)}, bf16[1,128,1024]{2,1,0:T(8,128)(2,1)}, u32[]{:S(2)}) copy-start(bf16[1,128,1024]{2,1,0:T(8,128)(2,1)} %param.20) | copy-start | bytes 786436

commit v12 on v11

--- a/solution.py
+++ b/solution.py
@@ -252,32 +252,31 @@
         out[slot(r)] = row.astype(BF16)
 
 
-def state_kernel(signals, gain_ref, lane_ref, back_lane_ref, twist_ref, *refs):
-    *specs, out, skip_ref = refs
+def state_kernel(kept, signals, gain_ref, lane_ref, back_lane_ref, twist_ref, spec_ref, out, skip_ref):
     batch = signals.shape[0] // ROWS
-    chans = out.shape[1] // 2
+    chans = 2 * (signals.shape[1] // 5)
     share = signals.shape[1] - 2 * chans
     place = (lax.axis_index("pl") * SIDE + lax.axis_index("x")) * SIDE + lax.axis_index("y")
     pieces = LANES // chans
     gains = jnp.broadcast_to(gain_ref[pl.ds(place // pieces, 1), :], (LANES, LANES))
     skip_ref[...] = gains.T
-    begin = pl.multiple_of(place % pieces * chans, chans)
-    for kept, spec_ref in enumerate(specs):
-        first = half_start(kept)
-        source = first // share
-        taps = spectrum(
-            lambda r: signals[source * ROWS + slot(r), pl.ds(2 * chans, CHUNK), :].astype(F32),
-            twist_ref,
-            lane_ref,
-        )
-        skip = skip_ref[pl.ds(pl.multiple_of(begin + first, CHUNK), CHUNK), :]
-        for which, product in enumerate((plain_product, conj_product)):
-            place = pl.ds(pl.multiple_of(which * chans + first, CHUNK), CHUNK)
-            for b in range(batch):
-                spec = product(taps, spec_ref[which * batch + b])
-                for r, row in enumerate(signal_rows(spec, twist_ref, back_lane_ref)):
-                    own = signals[b * ROWS + slot(r), place, :].astype(F32)
-                    out[b * ROWS + slot(r), place, :] = (row + skip * own).astype(BF16)
+    first = half_start(kept)
+    begin = place % pieces * chans + first
+    skip = skip_ref[pl.ds(pl.multiple_of(begin, CHUNK), CHUNK), :]
+    source = first // share
+    taps = spectrum(
+        lambda r: signals[source * ROWS + slot(r), pl.ds(2 * chans, CHUNK), :].astype(F32),
+        twist_ref,
+        lane_ref,
+    )
+    for which, product in enumerate((plain_product, conj_product)):
+        rows = pl.ds(pl.multiple_of(which * chans + first, CHUNK), CHUNK)
+        for b in range(batch):
+            spec = product(taps, spec_ref[which * batch + b])
+            for r, row in enumerate(signal_rows(spec, twist_ref, back_lane_ref)):
+                own = signals[b * ROWS + slot(r), rows, :].astype(F32)
+                result = (row + skip * own).astype(BF16)
+                out[b * ROWS + slot(r), pl.ds(which * CHUNK, CHUNK), :] = result
 
 
 def output_kernel(back, query, key, value, grad, *refs):
@@ -285,15 +284,19 @@
     own = back.shape[1] // 3
     pieces = LANES // own
     width = query.shape[1] // GROUPS
-    places = (half_start(1), half_start(0))
-    halves = [pl.ds(pl.multiple_of(2 * own + place, CHUNK), CHUNK) for place in places]
+    places = (half_start(0), half_start(1))
+    parts = [
+        [pl.ds(pl.multiple_of(2 * place + which * CHUNK, CHUNK), CHUNK) for place in places]
+        for which in range(2)
+    ]
+    halves = [pl.ds(pl.multiple_of(2 * own + place, CHUNK), CHUNK) for place in places[::-1]]
     sent = []
     for group in range(GROUPS):
         for tile in range(group * width // LANES, (group + 1) * width // LANES):
             cols = pl.ds(tile * LANES, LANES)
             blocks = [tile * pieces + i for i in range(pieces)]
             state, dmixed = (
-                jnp.concatenate([back[i, pl.ds(which * own, own), :] for i in blocks], axis=0).T
+                jnp.concatenate([back[i, part, :] for i in blocks for part in parts[which]], axis=0).T
                 for which in range(2)
             )
             term = jnp.concatenate([back[i, half, :] for i in blocks for half in halves], axis=0).T
@@ -354,15 +357,14 @@
     )
 
 
-def states(signals, spectra, skip_gain, own):
-    batch = signals.shape[0] // ROWS
+def states(signals, kept, spectra, skip_gain):
     forward_lane, inverse_lane = lane_tables()
     return call(
-        state_kernel,
-        jax.ShapeDtypeStruct((batch * ROWS, 2 * own, LANES), BF16),
-        (signals, skip_gain.reshape(-1, LANES), forward_lane, inverse_lane, twist_tables(1.0), *spectra),
+        functools.partial(state_kernel, kept),
+        jax.ShapeDtypeStruct((signals.shape[0], 2 * CHUNK, LANES), BF16),
+        (signals, skip_gain.reshape(-1, LANES), forward_lane, inverse_lane, twist_tables(1.0), spectra),
         (pltpu.VMEM((LANES, LANES), F32),),
-        flops=3 * 10**9,
+        flops=2 * 10**9,
     )
 
 
@@ -397,15 +399,18 @@
     def plus(a, b):
         return (a.astype(F32) + b.astype(F32)).astype(BF16)
 
-    spectra, (given, term) = zip(*(taps_grad(signals, kept, factor) for kept in range(2)))
-    term = plus(term, exchange(given, "dm"))
+    (spec_given, spec_kept), (given, term) = zip(*(taps_grad(signals, kept, factor) for kept in range(2)))
+    taken = exchange(given, "dm")
+    state_given = states(signals, 0, spec_given, skip_gain)
+    taken, state_given = lax.optimization_barrier((taken, state_given))
+    term = plus(term, taken)
     term = plus(*lax.all_gather(term, "dh"))
     other = exchange(term, "dm")
-    spectra, _ = lax.optimization_barrier((spectra, term))
-    results = states(signals, spectra, skip_gain, own)
-    other, results = lax.optimization_barrier((other, results))
+    spec_kept, _ = lax.optimization_barrier((spec_kept, term))
+    state_kept = states(signals, 1, spec_kept, skip_gain)
+    other, state_kept = lax.optimization_barrier((other, state_kept))
     copies = [jnp.broadcast_to(t[None], (pair,) + t.shape).reshape((peers,) + t.shape[1:]) for t in (term, other)]
-    back = swap(jnp.concatenate([results, *copies], axis=1), ("pl", "x", "y"))
+    back = swap(jnp.concatenate([state_given, state_kept, *copies], axis=1), ("pl", "x", "y"))
     outs = outputs(back, query, key, value, grad)
     return tuple(out[None] for out in outs[:4]) + (outs[4],)
 

time: 68.5 us -> 68.6 us (level)
    pallas_call x5 -> x6, Pallas kernels: 7.55 us -> 7.67 us  [call(): pl.pallas_call(kernel, out_shape=shapes, in_specs=[place(in_hbm)] * len(a...]
where the time goes in v12:
time: 68.6 us; the launch traced here: 68.3 us
  blocking collectives  48.9 us (71%)
  Pallas kernels  7.67 us (11%)
  waiting for transfers between devices  6.87 us (10%)
  starting transfers between devices  3.84 us (6%)
  between operations  0.82 us (1%)
    all_to_all x2, blocking collectives, swap(): return lax.all_to_all(values, axes, split_axis=0, concat_axis=0, tiled=True)  38.3 us
    all_gather x1, blocking collectives, on_device(): term = plus(*lax.all_gather(term, 'dh'))  10.5 us
    pallas_call x6, Pallas kernels, call(): pl.pallas_call(kernel, out_shape=shapes, in_specs=[place(in_hbm)] * len(a...  7.67 us
    ppermute x2, waiting for transfers between devices, exchange(): return lax.ppermute(values, axis, [(0, 1), (1, 0)])  6.87 us
    ppermute x2, starting transfers between devices, exchange(): return lax.ppermute(values, axis, [(0, 1), (1, 0)])  3.84 us
  transfers between devices with their start and end apart: 2, of which 2 were waited for; matrix products, arithmetic and copies ran while one was open for 0% of the time, Pallas kernels for 5%

profile of v12, /device:TPU:64, one launch (start us, length us, event | category | flops | bytes accessed | tf_op | source)
XLA Modules:
  0.0 68.3 jit_solution(11142091000497197914)
XLA Ops:
  0.6 1.6 %shard_map.209 = bf16[32,80,128]{2,1,0:T(8,128)(2,1)S(1)} custom-call(bf16[128,1024]{1,0:T(8,128)(2,1)} %bitcast.11, bf16[128,1024]{1,0:T(8,128)(2,1)} %bitcast.13, bf16[128,1024]{1,0:T(8,128)(2,1)} %bitcast.15, bf16[128,1024]{1,0:T(8,128)(2,1)} %bitcast.17, bf16[128,1024]{1,0:T(8,128)(2,1)} %taps.1), custom_call_target="tpu_custom_call" | custom-call | bytes 2097152 | tf_op jit(solution)/shard_map/pallas_call | solution.py:318
  2.3 0.0 copy-start.5
  2.3 0.0 copy-start.6
  2.3 0.0 copy-start.8
  2.3 21.3 %all_to_all.10.signals = bf16[32,80,128]{2,1,0:T(8,128)(2,1)S(1)} all-to-all(bf16[32,80,128]{2,1,0:T(8,128)(2,1)S(1)} %shard_map.209), channel_id=1, replica_groups=mesh['dh'=2,'dm'=2,'pl'=2,'chan'=4,'y'=4,'x'=4] {'pl','x','y'}, dimensions={0} | all-to-all | bytes 1310720 | tf_op jit(solution)/shard_map/all_to_all | solution.py:392
  23.6 0.0 copy-done.5
  23.6 0.0 copy-done.6
  23.6 0.0 copy-done.8
  23.7 1.2 %shard_map.210 = (f32[4,272,256]{2,1,0:T(8,128)S(1)}, bf16[16,16,128]{2,1,0:T(8,128)(2,1)S(1)}) custom-call(bf16[32,80,128]{2,1,0:T(8,128)(2,1)S(1)} %all_to_all.10.signals, bf16[2,256,256]{2,1,0:T(8,128)(2,1)S(1)} %copy-done.5, bf16[2,256,256]{2,1,0:T(8,128)(2,1)S(1)} %copy-done.6, f32[17,4,128]{2,1,0:T(4,128)S(1)} %copy-done.8), custom_call_target="tpu_custom_call" | custom-call | flops 2000000000 | bytes 2097152 | tf_op jit(solution)/shard_map/pallas_call | solution.py:318
  24.9 0.0 copy-start.4
  24.9 0.0 copy-start.7
  24.9 1.9 %collective-permute-start = (bf16[16,16,128]{2,1,0:T(8,128)(2,1)S(1)}, bf16[16,16,128]{2,1,0:T(8,128)(2,1)S(1)}, u32[]{:S(2)}, u32[]{:S(2)}) collective-permute-start(bf16[16,16,128]{2,1,0:T(8,128)(2,1)S(1)} %get-tuple-element.19), channel_id=1, source_target_pairs={{0,128},{128,0},{1,129},{129,1},{2,130},{130,2},{3,131},{131,3},{4... | collective-permute-start | bytes 196616 | tf_op jit(solution)/shard_map/ppermute | solution.py:397
  26.9 1.2 %shard_map.212 = (f32[4,272,256]{2,1,0:T(8,128)S(1)}, bf16[16,16,128]{2,1,0:T(8,128)(2,1)S(1)}) custom-call(bf16[32,80,128]{2,1,0:T(8,128)(2,1)S(1)} %all_to_all.10.signals, bf16[2,256,256]{2,1,0:T(8,128)(2,1)S(1)} %copy-done.5, bf16[2,256,256]{2,1,0:T(8,128)(2,1)S(1)} %copy-done.6, f32[17,4,128]{2,1,0:T(4,128)S(1)} %copy-done.8), custom_call_target="tpu_custom_call" | custom-call | flops 2000000000 | bytes 2097152 | tf_op jit(solution)/shard_map/pallas_call | solution.py:318
  28.1 0.0 copy-done.4
  28.1 0.0 copy-done.7
  28.1 1.1 %shard_map.211 = bf16[32,32,128]{2,1,0:T(8,128)(2,1)S(1)} custom-call(bf16[32,80,128]{2,1,0:T(8,128)(2,1)S(1)} %all_to_all.10.signals, f32[8,128]{1,0:T(8,128)S(1)} %bitcast.19, bf16[2,256,256]{2,1,0:T(8,128)(2,1)S(1)} %copy-done.5, bf16[2,256,256]{2,1,0:T(8,128)(2,1)S(1)} %copy-done.6, f32[17,4,128]{2,1,0:T(4,128)S(1)} %copy-done.7, ...), custom_call_target="tpu_custom_call" | custom-call | flops 2000000000 | bytes 2097152 | tf_op jit(solution)/shard_map/pallas_call | solution.py:318
  29.2 2.9 %collective-permute-done = bf16[16,16,128]{2,1,0:T(8,128)(2,1)S(1)} collective-permute-done((bf16[16,16,128]{2,1,0:T(8,128)(2,1)S(1)}, bf16[16,16,128]{2,1,0:T(8,128)(2,1)S(1)}, u32[]{:S(2)}, u32[]{:S(2)}) %collective-permute-start) | collective-permute-done | bytes 65568 | tf_op jit(solution)/shard_map/ppermute | solution.py:397
  32.1 10.5 %all-gather = bf16[32,16,128]{2,1,0:T(8,128)(2,1)S(1)} all-gather(bf16[16,16,128]{2,1,0:T(8,128)(2,1)S(1)} %add_convert_fusion.1), channel_id=2, replica_groups=mesh['dh'=2,'dm'=2,'pl'=2,'chan'=4,'y'=4,'x'=4] {'dh'}, dimensions={0}, use_global_device_ids=true | all-gather | bytes 196608 | tf_op jit(solution)/shard_map/all_gather | solution.py:407
  42.6 1.9 %collective-permute-start.1 = (bf16[16,16,128]{2,1,0:T(8,128)(2,1)S(1)}, bf16[16,16,128]{2,1,0:T(8,128)(2,1)S(1)}, u32[]{:S(2)}, u32[]{:S(2)}) collective-permute-start(bf16[16,16,128]{2,1,0:T(8,128)(2,1)S(1)} %add_convert_fusion), channel_id=1, source_target_pairs={{0,128},{128,0},{1,129},{129,1},{2,130},{130,2},{3,131},{131,3},{4... | collective-permute-start | bytes 196616 | tf_op jit(solution)/shard_map/ppermute | solution.py:397
  44.6 1.1 %shard_map.213 = bf16[32,32,128]{2,1,0:T(8,128)(2,1)S(1)} custom-call(bf16[32,80,128]{2,1,0:T(8,128)(2,1)S(1)} %all_to_all.10.signals, f32[8,128]{1,0:T(8,128)S(1)} %bitcast.20, bf16[2,256,256]{2,1,0:T(8,128)(2,1)S(1)} %copy-done.5, bf16[2,256,256]{2,1,0:T(8,128)(2,1)S(1)} %copy-done.6, f32[17,4,128]{2,1,0:T(4,128)S(1)} %copy-done.7, ...), custom_call_target="tpu_custom_call" | custom-call | flops 2000000000 | bytes 2097152 | tf_op jit(solution)/shard_map/pallas_call | solution.py:318
  45.7 4.0 %collective-permute-done.1 = bf16[16,16,128]{2,1,0:T(8,128)(2,1)S(1)} collective-permute-done((bf16[16,16,128]{2,1,0:T(8,128)(2,1)S(1)}, bf16[16,16,128]{2,1,0:T(8,128)(2,1)S(1)}, u32[]{:S(2)}, u32[]{:S(2)}) %collective-permute-start.1) | collective-permute-done | bytes 65568 | tf_op jit(solution)/shard_map/ppermute | solution.py:397
  49.8 0.1 pad_maximum_fusion
  49.8 0.0 copy-start
  49.8 0.0 copy-start.1
  49.8 0.0 copy-start.2
  49.9 0.0 copy-start.3
  49.9 17.0 %all_to_all.11.back = bf16[32,96,128]{2,1,0:T(8,128)(2,1)S(1)} all-to-all(bf16[32,96,128]{2,1,0:T(8,128)(2,1)S(1)} %pad_maximum_fusion), channel_id=1, replica_groups=mesh['dh'=2,'dm'=2,'pl'=2,'chan'=4,'y'=4,'x'=4] {'pl','x','y'}, dimensions={0} | all-to-all | bytes 1572864 | tf_op jit(solution)/shard_map/all_to_all | solution.py:392
  66.9 0.0 copy-done
  66.9 0.0 copy-done.1
  66.9 0.0 copy-done.2
  66.9 0.0 copy-done.3
  66.9 1.4 %shard_map.214 = (bf16[128,1024]{1,0:T(8,128)(2,1)}, bf16[128,1024]{1,0:T(8,128)(2,1)}, bf16[128,1024]{1,0:T(8,128)(2,1)}, bf16[128,1024]{1,0:T(8,128)(2,1)}, bf16[128,1024]{1,0:T(8,128)(2,1)}) custom-call(bf16[32,96,128]{2,1,0:T(8,128)(2,1)S(1)} %all_to_all.11.back, bf16[128,1024]{1,0:T(8,128)(2,1)S(1)} %bitcast.12, bf16[128,1024]{1,0:T(8,128)(2,1)S(1)} %bitcast.14, ...), custom_call_target="tpu_custom_call" | custom-call | bytes 2097152 | tf_op jit(solution)/shard_map/pallas_call | solution.py:318
  (4 shorter events, 0.1 us)
Async XLA Ops:
  2.3 21.4 %copy-start.5 = (bf16[2,256,256]{2,1,0:T(8,128)(2,1)S(1)}, bf16[2,256,256]{2,1,0:T(8,128)(2,1)}, u32[]{:S(2)}) copy-start(bf16[2,256,256]{2,1,0:T(8,128)(2,1)} %constant.8.clone.lane_ref) | copy-start | bytes 786436
  2.3 21.4 %copy-start.6 = (bf16[2,256,256]{2,1,0:T(8,128)(2,1)S(1)}, bf16[2,256,256]{2,1,0:T(8,128)(2,1)}, u32[]{:S(2)}) copy-start(bf16[2,256,256]{2,1,0:T(8,128)(2,1)} %constant.9.clone.back_lane_ref) | copy-start | bytes 786436
  2.3 21.4 %copy-start.8 = (f32[17,4,128]{2,1,0:T(4,128)S(1)}, f32[17,4,128]{2,1,0:T(4,128)}, u32[]{:S(2)}) copy-start(f32[17,4,128]{2,1,0:T(4,128)} %constant.10.clone.twist_ref) | copy-start | bytes 104452
  24.9 3.2 %copy-start.4 = (f32[1024]{0:T(1024)S(1)}, f32[1024]{0:T(1024)}, u32[]{:S(2)}) copy-start(f32[1024]{0:T(1024)} %param.22) | copy-start | bytes 12292
  24.9 3.2 %copy-start.7 = (f32[17,4,128]{2,1,0:T(4,128)S(1)}, f32[17,4,128]{2,1,0:T(4,128)}, u32[]{:S(2)}) copy-start(f32[17,4,128]{2,1,0:T(4,128)} %constant.11.clone.twist_ref) | copy-start | bytes 104452
  24.9 7.2 %collective-permute-start = (bf16[16,16,128]{2,1,0:T(8,128)(2,1)S(1)}, bf16[16,16,128]{2,1,0:T(8,128)(2,1)S(1)}, u32[]{:S(2)}, u32[]{:S(2)}) collective-permute-start(bf16[16,16,128]{2,1,0:T(8,128)(2,1)S(1)} %get-tuple-element.19), channel_id=1, source_target_pairs={{0,128},{128,0},{1,129},{129,1},{2,130},{130,2},{3,131},{131,3},{4... | collective-permute-start | bytes 196616 | tf_op jit(solution)/shard_map/ppermute | solution.py:397
  42.6 7.1 %collective-permute-start.1 = (bf16[16,16,128]{2,1,0:T(8,128)(2,1)S(1)}, bf16[16,16,128]{2,1,0:T(8,128)(2,1)S(1)}, u32[]{:S(2)}, u32[]{:S(2)}) collective-permute-start(bf16[16,16,128]{2,1,0:T(8,128)(2,1)S(1)} %add_convert_fusion), channel_id=1, source_target_pairs={{0,128},{128,0},{1,129},{129,1},{2,130},{130,2},{3,131},{131,3},{4... | collective-permute-start | bytes 196616 | tf_op jit(solution)/shard_map/ppermute | solution.py:397
  49.8 17.1 %copy-start = (bf16[1,128,1024]{2,1,0:T(8,128)(2,1)S(1)}, bf16[1,128,1024]{2,1,0:T(8,128)(2,1)}, u32[]{:S(2)}) copy-start(bf16[1,128,1024]{2,1,0:T(8,128)(2,1)} %param.18) | copy-start | bytes 786436
  49.8 17.1 %copy-start.1 = (bf16[1,128,1024]{2,1,0:T(8,128)(2,1)S(1)}, bf16[1,128,1024]{2,1,0:T(8,128)(2,1)}, u32[]{:S(2)}) copy-start(bf16[1,128,1024]{2,1,0:T(8,128)(2,1)} %param.19) | copy-start | bytes 786436
  49.8 17.0 %copy-start.2 = (bf16[1,128,1024]{2,1,0:T(8,128)(2,1)S(1)}, bf16[1,128,1024]{2,1,0:T(8,128)(2,1)}, u32[]{:S(2)}) copy-start(bf16[1,128,1024]{2,1,0:T(8,128)(2,1)} %param.20) | copy-start | bytes 786436
  49.9 17.0 %copy-start.3 = (bf16[1,128,1024]{2,1,0:T(8,128)(2,1)S(1)}, bf16[1,128,1024]{2,1,0:T(8,128)(2,1)}, u32[]{:S(2)}) copy-start(bf16[1,128,1024]{2,1,0:T(8,128)(2,1)} %param.23) | copy-start | bytes 786436

commit v13 on v11

--- a/solution.py
+++ b/solution.py
@@ -158,25 +158,25 @@
         cols = pl.ds(group * width, width)
         pairs = [(a.at[:, cols], b.at[:, cols]) for a, b in zip((key, value, grad, query, taps), held)]
         arrivals.append(start_copies(pairs, sems.at[group]))
+    tiles = width // LANES
     for group, copies in enumerate(arrivals):
-        for copy in copies:
-            copy.wait()
-        tiles = width // LANES
-        for tile in range(group * tiles, (group + 1) * tiles):
-            cols = pl.ds(tile * LANES, LANES)
-            mixed = (key_v[:, cols].astype(F32) * value_v[:, cols].astype(F32)).astype(BF16)
-            state = (grad_v[:, cols].astype(F32) * query_v[:, cols].astype(F32)).astype(BF16)
-            for place, block in enumerate((mixed, state)):
-                turned = block.T
+        span = range(group * tiles, (group + 1) * tiles)
+        for place, (one, other) in enumerate(((key_v, value_v), (grad_v, query_v))):
+            copies[2 * place].wait()
+            copies[2 * place + 1].wait()
+            for tile in span:
+                cols = pl.ds(tile * LANES, LANES)
+                turned = (one[:, cols].astype(F32) * other[:, cols].astype(F32)).astype(BF16).T
                 for i in range(pieces):
                     rows = pl.ds(place * own, own)
                     out[tile * pieces + i, rows, :] = turned[i * own : (i + 1) * own]
-            turned = taps_v[:, cols].T
+        copies[4].wait()
+        for tile in span:
+            turned = taps_v[:, pl.ds(tile * LANES, LANES)].T
             for i in range(pieces):
                 low = turned[i * own : i * own + share]
                 high = turned[i * own + share : (i + 1) * own]
-                rows = pl.ds(2 * own, share)
-                out[tile * pieces + i, rows, :] = jnp.where(begin == 0, low, high)
+                out[tile * pieces + i, pl.ds(2 * own, share), :] = jnp.where(begin == 0, low, high)
 
 
 def spectrum(get_row, twist_ref, lane_ref):

time: 68.5 us -> 68.5 us (level)
  no operation moved by 1% of the time
where the time goes in v13:
time: 68.5 us; the launch traced here: 68.2 us
  blocking collectives  48.8 us (71%)
  Pallas kernels  7.58 us (11%)
  waiting for transfers between devices  6.96 us (10%)
  starting transfers between devices  3.84 us (6%)
  between operations  0.81 us (1%)
    all_to_all x2, blocking collectives, swap(): return lax.all_to_all(values, axes, split_axis=0, concat_axis=0, tiled=True)  38.3 us
    all_gather x1, blocking collectives, on_device(): term = plus(*lax.all_gather(term, 'dh'))  10.5 us
    pallas_call x5, Pallas kernels, call(): pl.pallas_call(kernel, out_shape=shapes, in_specs=[place(in_hbm)] * len(a...  7.58 us
    ppermute x2, waiting for transfers between devices, exchange(): return lax.ppermute(values, axis, [(0, 1), (1, 0)])  6.96 us
    ppermute x2, starting transfers between devices, exchange(): return lax.ppermute(values, axis, [(0, 1), (1, 0)])  3.84 us
  transfers between devices with their start and end apart: 2, of which 2 were waited for; matrix products, arithmetic and copies ran while one was open for 0% of the time, Pallas kernels for 5%

profile of v13, /device:TPU:64, one launch (start us, length us, event | category | flops | bytes accessed | tf_op | source)
XLA Modules:
  0.0 68.2 jit_solution(14729663151769815229)
XLA Ops:
  0.6 1.7 %shard_map.182 = bf16[32,80,128]{2,1,0:T(8,128)(2,1)S(1)} custom-call(bf16[128,1024]{1,0:T(8,128)(2,1)} %bitcast.11, bf16[128,1024]{1,0:T(8,128)(2,1)} %bitcast.13, bf16[128,1024]{1,0:T(8,128)(2,1)} %bitcast.15, bf16[128,1024]{1,0:T(8,128)(2,1)} %bitcast.17, bf16[128,1024]{1,0:T(8,128)(2,1)} %taps.1), custom_call_target="tpu_custom_call" | custom-call | bytes 2097152 | tf_op jit(solution)/shard_map/pallas_call | solution.py:315
  2.3 0.0 copy-start.5
  2.3 0.0 copy-start.6
  2.3 0.0 copy-start.8
  2.3 21.3 %all_to_all.10.signals = bf16[32,80,128]{2,1,0:T(8,128)(2,1)S(1)} all-to-all(bf16[32,80,128]{2,1,0:T(8,128)(2,1)S(1)} %shard_map.182), channel_id=1, replica_groups=mesh['dh'=2,'dm'=2,'pl'=2,'chan'=4,'y'=4,'x'=4] {'pl','x','y'}, dimensions={0} | all-to-all | bytes 1310720 | tf_op jit(solution)/shard_map/all_to_all | solution.py:390
  23.7 0.0 copy-done.5
  23.7 0.0 copy-done.6
  23.7 0.0 copy-done.8
  23.7 1.2 %shard_map.184 = (f32[4,272,256]{2,1,0:T(8,128)S(1)}, bf16[16,16,128]{2,1,0:T(8,128)(2,1)S(1)}) custom-call(bf16[32,80,128]{2,1,0:T(8,128)(2,1)S(1)} %all_to_all.10.signals, bf16[2,256,256]{2,1,0:T(8,128)(2,1)S(1)} %copy-done.6, bf16[2,256,256]{2,1,0:T(8,128)(2,1)S(1)} %copy-done.5, f32[17,4,128]{2,1,0:T(4,128)S(1)} %copy-done.8), custom_call_target="tpu_custom_call" | custom-call | flops 2000000000 | bytes 2097152 | tf_op jit(solution)/shard_map/pallas_call | solution.py:315
  24.9 0.0 copy-start.4
  24.9 0.0 copy-start.7
  24.9 1.9 %collective-permute-start = (bf16[16,16,128]{2,1,0:T(8,128)(2,1)S(1)}, bf16[16,16,128]{2,1,0:T(8,128)(2,1)S(1)}, u32[]{:S(2)}, u32[]{:S(2)}) collective-permute-start(bf16[16,16,128]{2,1,0:T(8,128)(2,1)S(1)} %get-tuple-element.19), channel_id=1, source_target_pairs={{0,128},{128,0},{1,129},{129,1},{2,130},{130,2},{3,131},{131,3},{4... | collective-permute-start | bytes 196616 | tf_op jit(solution)/shard_map/ppermute | solution.py:395
  26.8 1.2 %shard_map.183 = (f32[4,272,256]{2,1,0:T(8,128)S(1)}, bf16[16,16,128]{2,1,0:T(8,128)(2,1)S(1)}) custom-call(bf16[32,80,128]{2,1,0:T(8,128)(2,1)S(1)} %all_to_all.10.signals, bf16[2,256,256]{2,1,0:T(8,128)(2,1)S(1)} %copy-done.6, bf16[2,256,256]{2,1,0:T(8,128)(2,1)S(1)} %copy-done.5, f32[17,4,128]{2,1,0:T(4,128)S(1)} %copy-done.8), custom_call_target="tpu_custom_call" | custom-call | flops 2000000000 | bytes 2097152 | tf_op jit(solution)/shard_map/pallas_call | solution.py:315
  28.0 4.0 %collective-permute-done = bf16[16,16,128]{2,1,0:T(8,128)(2,1)S(1)} collective-permute-done((bf16[16,16,128]{2,1,0:T(8,128)(2,1)S(1)}, bf16[16,16,128]{2,1,0:T(8,128)(2,1)S(1)}, u32[]{:S(2)}, u32[]{:S(2)}) %collective-permute-start) | collective-permute-done | bytes 65568 | tf_op jit(solution)/shard_map/ppermute | solution.py:395
  32.1 10.5 %all-gather = bf16[32,16,128]{2,1,0:T(8,128)(2,1)S(1)} all-gather(bf16[16,16,128]{2,1,0:T(8,128)(2,1)S(1)} %add_convert_fusion.1), channel_id=2, replica_groups=mesh['dh'=2,'dm'=2,'pl'=2,'chan'=4,'y'=4,'x'=4] {'dh'}, dimensions={0}, use_global_device_ids=true | all-gather | bytes 196608 | tf_op jit(solution)/shard_map/all_gather | solution.py:402
  42.6 1.9 %collective-permute-start.1 = (bf16[16,16,128]{2,1,0:T(8,128)(2,1)S(1)}, bf16[16,16,128]{2,1,0:T(8,128)(2,1)S(1)}, u32[]{:S(2)}, u32[]{:S(2)}) collective-permute-start(bf16[16,16,128]{2,1,0:T(8,128)(2,1)S(1)} %add_convert_fusion), channel_id=1, source_target_pairs={{0,128},{128,0},{1,129},{129,1},{2,130},{130,2},{3,131},{131,3},{4... | collective-permute-start | bytes 196616 | tf_op jit(solution)/shard_map/ppermute | solution.py:395
  44.5 0.0 copy-done.4
  44.5 0.0 copy-done.7
  44.5 2.2 %shard_map.185 = bf16[32,64,128]{2,1,0:T(8,128)(2,1)S(1)} custom-call(bf16[32,80,128]{2,1,0:T(8,128)(2,1)S(1)} %all_to_all.10.signals, f32[8,128]{1,0:T(8,128)S(1)} %bitcast.19, bf16[2,256,256]{2,1,0:T(8,128)(2,1)S(1)} %copy-done.6, bf16[2,256,256]{2,1,0:T(8,128)(2,1)S(1)} %copy-done.5, f32[17,4,128]{2,1,0:T(4,128)S(1)} %copy-done.7, ...), custom_call_target="tpu_custom_call" | custom-call | flops 3000000000 | bytes 2097152 | tf_op jit(solution)/shard_map/pallas_call | solution.py:315
  46.7 2.9 %collective-permute-done.1 = bf16[16,16,128]{2,1,0:T(8,128)(2,1)S(1)} collective-permute-done((bf16[16,16,128]{2,1,0:T(8,128)(2,1)S(1)}, bf16[16,16,128]{2,1,0:T(8,128)(2,1)S(1)}, u32[]{:S(2)}, u32[]{:S(2)}) %collective-permute-start.1) | collective-permute-done | bytes 65568 | tf_op jit(solution)/shard_map/ppermute | solution.py:395
  49.7 0.1 pad_maximum_fusion
  49.8 0.0 copy-start
  49.8 0.0 copy-start.1
  49.8 0.0 copy-start.2
  49.8 0.0 copy-start.3
  49.8 17.0 %all_to_all.11.back = bf16[32,96,128]{2,1,0:T(8,128)(2,1)S(1)} all-to-all(bf16[32,96,128]{2,1,0:T(8,128)(2,1)S(1)} %pad_maximum_fusion), channel_id=1, replica_groups=mesh['dh'=2,'dm'=2,'pl'=2,'chan'=4,'y'=4,'x'=4] {'pl','x','y'}, dimensions={0} | all-to-all | bytes 1572864 | tf_op jit(solution)/shard_map/all_to_all | solution.py:390
  66.8 0.0 copy-done
  66.8 0.0 copy-done.1
  66.8 0.0 copy-done.2
  66.8 0.0 copy-done.3
  66.8 1.3 %shard_map.186 = (bf16[128,1024]{1,0:T(8,128)(2,1)}, bf16[128,1024]{1,0:T(8,128)(2,1)}, bf16[128,1024]{1,0:T(8,128)(2,1)}, bf16[128,1024]{1,0:T(8,128)(2,1)}, bf16[128,1024]{1,0:T(8,128)(2,1)}) custom-call(bf16[32,96,128]{2,1,0:T(8,128)(2,1)S(1)} %all_to_all.11.back, bf16[128,1024]{1,0:T(8,128)(2,1)S(1)} %bitcast.12, bf16[128,1024]{1,0:T(8,128)(2,1)S(1)} %bitcast.14, ...), custom_call_target="tpu_custom_call" | custom-call | bytes 2097152 | tf_op jit(solution)/shard_map/pallas_call | solution.py:315
  (4 shorter events, 0.1 us)
Async XLA Ops:
  2.3 21.4 %copy-start.5 = (bf16[2,256,256]{2,1,0:T(8,128)(2,1)S(1)}, bf16[2,256,256]{2,1,0:T(8,128)(2,1)}, u32[]{:S(2)}) copy-start(bf16[2,256,256]{2,1,0:T(8,128)(2,1)} %constant.9.clone.back_lane_ref) | copy-start | bytes 786436
  2.3 21.4 %copy-start.6 = (bf16[2,256,256]{2,1,0:T(8,128)(2,1)S(1)}, bf16[2,256,256]{2,1,0:T(8,128)(2,1)}, u32[]{:S(2)}) copy-start(bf16[2,256,256]{2,1,0:T(8,128)(2,1)} %constant.8.clone.lane_ref) | copy-start | bytes 786436
  2.3 21.4 %copy-start.8 = (f32[17,4,128]{2,1,0:T(4,128)S(1)}, f32[17,4,128]{2,1,0:T(4,128)}, u32[]{:S(2)}) copy-start(f32[17,4,128]{2,1,0:T(4,128)} %constant.10.clone.twist_ref) | copy-start | bytes 104452
  24.9 19.6 %copy-start.4 = (f32[1024]{0:T(1024)S(1)}, f32[1024]{0:T(1024)}, u32[]{:S(2)}) copy-start(f32[1024]{0:T(1024)} %param.19) | copy-start | bytes 12292
  24.9 19.6 %copy-start.7 = (f32[17,4,128]{2,1,0:T(4,128)S(1)}, f32[17,4,128]{2,1,0:T(4,128)}, u32[]{:S(2)}) copy-start(f32[17,4,128]{2,1,0:T(4,128)} %constant.11.clone.twist_ref) | copy-start | bytes 104452
  24.9 7.2 %collective-permute-start = (bf16[16,16,128]{2,1,0:T(8,128)(2,1)S(1)}, bf16[16,16,128]{2,1,0:T(8,128)(2,1)S(1)}, u32[]{:S(2)}, u32[]{:S(2)}) collective-permute-start(bf16[16,16,128]{2,1,0:T(8,128)(2,1)S(1)} %get-tuple-element.19), channel_id=1, source_target_pairs={{0,128},{128,0},{1,129},{129,1},{2,130},{130,2},{3,131},{131,3},{4... | collective-permute-start | bytes 196616 | tf_op jit(solution)/shard_map/ppermute | solution.py:395
  42.6 7.1 %collective-permute-start.1 = (bf16[16,16,128]{2,1,0:T(8,128)(2,1)S(1)}, bf16[16,16,128]{2,1,0:T(8,128)(2,1)S(1)}, u32[]{:S(2)}, u32[]{:S(2)}) collective-permute-start(bf16[16,16,128]{2,1,0:T(8,128)(2,1)S(1)} %add_convert_fusion), channel_id=1, source_target_pairs={{0,128},{128,0},{1,129},{129,1},{2,130},{130,2},{3,131},{131,3},{4... | collective-permute-start | bytes 196616 | tf_op jit(solution)/shard_map/ppermute | solution.py:395
  49.8 17.1 %copy-start = (bf16[1,128,1024]{2,1,0:T(8,128)(2,1)S(1)}, bf16[1,128,1024]{2,1,0:T(8,128)(2,1)}, u32[]{:S(2)}) copy-start(bf16[1,128,1024]{2,1,0:T(8,128)(2,1)} %param.15) | copy-start | bytes 786436
  49.8 17.0 %copy-start.1 = (bf16[1,128,1024]{2,1,0:T(8,128)(2,1)S(1)}, bf16[1,128,1024]{2,1,0:T(8,128)(2,1)}, u32[]{:S(2)}) copy-start(bf16[1,128,1024]{2,1,0:T(8,128)(2,1)} %param.16) | copy-start | bytes 786436
  49.8 17.0 %copy-start.2 = (bf16[1,128,1024]{2,1,0:T(8,128)(2,1)S(1)}, bf16[1,128,1024]{2,1,0:T(8,128)(2,1)}, u32[]{:S(2)}) copy-start(bf16[1,128,1024]{2,1,0:T(8,128)(2,1)} %param.17) | copy-start | bytes 786436
  49.8 17.0 %copy-start.3 = (bf16[1,128,1024]{2,1,0:T(8,128)(2,1)S(1)}, bf16[1,128,1024]{2,1,0:T(8,128)(2,1)}, u32[]{:S(2)}) copy-start(bf16[1,128,1024]{2,1,0:T(8,128)(2,1)} %param.20) | copy-start | bytes 786436
